TPU v7x, 512 devices: a whole 4x8x8 slice. The times are simulated.
512 devices in a mesh: expert: 64 (over x, y, core), seq: 8 (over z).
Axes of the slice: x: 4, y: 8, z: 8, core: 2. Of those that a mesh axis runs over, the one named last changes fastest.
Arguments:
- hidden_rows: bfloat16 [32768, 8, 1024], P(('expert', 'seq')), may hold values from -16 to 16
- routes: int32 [32768, 8], P(('expert', 'seq')), may hold values from 0 to 63, all different within a row; in each aligned block of 64 rows (0 to 63, 64 to 127, ...) at most 16 rows name the same one
- down_weight: bfloat16 [64, 7168, 1024], P('expert', 'seq'), may hold values from -0.1875 to 0.1875
- probe: bfloat16 [7168, 256], P('seq'), may hold values from -0.0625 to 0.0625
Outputs:
- basis: float32 [7168, 256], P(('seq', 'expert'))
- coefficients: float32 [64, 256, 1024], P('expert', None, 'seq')
Inputs may be any that keep to these rules, and one draw needn't show every extreme that they name: `routes`: in each aligned block of 64 tokens no expert is named in more than 16 places, and some expert in exactly 16; the 8 experts of a token differ.
All inputs are finite; a program needn't handle non-finite values.
Results may differ from a plain program's by a relative error of at most 0.0054.
Values may be sent and summed in bfloat16 or wider, within the bound.
No kernel may reach another device: no remote copies, remote signals or barrier semaphores. Data moves between devices by JAX's collectives and lax.ppermute only.
A program may use at most 64 MiB of HBM per device.

v0:
```python
import jax
import jax.numpy as jnp
from jax import lax
from jax.sharding import PartitionSpec as P


def body(hidden_rows, routes, down_weight, probe):
    weight = down_weight[0]
    tok_count, top_count = routes.shape
    feature_width = hidden_rows.shape[2]
    experts = lax.axis_size("expert")
    capacity = 2 * tok_count * top_count // experts
    row_mean = tok_count * top_count * lax.axis_size("seq")
    partial_value = lax.dot_general(
        weight, probe, (((0,), (0,)), ((), ())), preferred_element_type=jnp.float32
    )
    probe_proj = lax.psum(partial_value, "seq").astype(jnp.bfloat16)
    expert_ids = routes.reshape(-1)
    onehot = (expert_ids[:, None] == jnp.arange(experts, dtype=jnp.int32)[None, :]).astype(
        jnp.int32
    )
    position = jnp.sum(onehot * (jnp.cumsum(onehot, axis=0) - 1), axis=1)
    destination = expert_ids * capacity + position
    outgoing = jnp.zeros((experts * capacity, feature_width), jnp.bfloat16)
    outgoing = outgoing.at[destination].set(hidden_rows.reshape(-1, feature_width))
    outgoing = outgoing.reshape(experts, capacity, feature_width)
    arrived = lax.all_to_all(outgoing, "expert", split_axis=0, concat_axis=0, tiled=True)
    arrived_rows = arrived.reshape(-1, feature_width)
    mixed = jnp.dot(arrived_rows, probe_proj, preferred_element_type=jnp.float32).astype(
        jnp.bfloat16
    )
    gram_part = lax.dot_general(
        arrived_rows, mixed, (((0,), (0,)), ((), ())), preferred_element_type=jnp.float32
    )
    gram_full = lax.psum(gram_part, "seq") / row_mean
    panel_image = jnp.dot(
        weight, gram_full.astype(jnp.bfloat16), preferred_element_type=jnp.float32
    )
    basis_rows = lax.psum_scatter(panel_image, "expert", scatter_dimension=0, tiled=True)
    coef_part = lax.dot_general(
        lax.all_gather(basis_rows.astype(jnp.bfloat16), "expert", axis=0, tiled=True),
        weight,
        (((0,), (0,)), ((), ())),
        preferred_element_type=jnp.float32,
    )
    coefficients = lax.psum_scatter(coef_part, "seq", scatter_dimension=1, tiled=True)
    return (basis_rows, coefficients[None])


def solution(mesh):
    in_specs = (
        P(("expert", "seq"), None, None),
        P(("expert", "seq"), None),
        P("expert", "seq", None),
        P("seq", None),
    )
    out_specs = (P(("seq", "expert"), None), P("expert", None, "seq"))
    return jax.shard_map(body, mesh=mesh, in_specs=in_specs, out_specs=out_specs, check_vma=False)
```

profile of v0, /device:TPU:1, one launch (start us, length us, event | category | flops | bytes accessed | tf_op | source)
XLA Modules:
  0.0 471.9 jit_solution(1125313786212875297)
XLA Ops:
  7.2 0.0 copy-start
  7.2 0.9 copy.14
  8.1 0.1 eq.29
  8.2 0.1 eq.25
  8.3 0.7 broadcast_multiply_fusion
  9.0 1.2 reduce-window.6
  10.2 0.2 slice_reduce_fusion
  10.5 0.1 copy.13
  10.5 0.1 mul.21
  10.6 0.1 fusion.17
  10.8 4.8 %scatter_custom_fusion = bf16[1024,1024]{1,0:T(8,128)(2,1)} fusion(s32[512]{0:T(512)S(1)} %bitcast.46, bf16[64,8,1024]{2,1,0:T(8,128)(2,1)} %param.4, bf16[]{:T(256)} %constant.6.clone.1), kind=kCustom, calls=%fused_computation.10 | custom fusion | bytes 3145730 | tf_op jit(solution)/shard_map/scatter | solution.py:25
  15.5 0.0 copy-start.1
  15.5 11.9 %all-to-all-start = ((bf16[64,16,1024]{2,1,0:T(8,128)(2,1)}), bf16[64,16,1024]{2,1,0:T(8,128)(2,1)}, u32[]{:S(2)}, u32[]{:S(2)}) async-start(bf16[64,16,1024]{2,1,0:T(8,128)(2,1)} %bitcast.44), calls=%async_computation | async-start | bytes 4194304 | tf_op jit(solution)/shard_map/all_to_all | solution.py:27
  27.5 0.0 all-reduce.5.cloned.1.call-start
  27.5 0.0 copy-done
  27.5 0.0 copy-done.1
  27.6 0.7 fusion.4
  28.3 59.2 %all-reduce.8 = bf16[1024,256]{1,0:T(8,128)(2,1)S(1)} all-reduce(f32[1024,256]{1,0:T(8,128)S(1)} %fusion.4), channel_id=1, replica_groups=mesh['expert'=64,'seq'=8] {'seq'}, use_global_device_ids=true, to_apply=%region_4.5 | all-reduce | flops 262144 | bytes 1572864 | tf_op jit(solution)/shard_map/psum | solution.py:17
  87.5 0.0 all-to-all-done
  87.5 5.4 %fusion.9 = f32[1024,256]{1,0:T(8,128)} fusion(bf16[1024,1024]{1,0:T(8,128)(2,1)} %bitcast.5, bf16[1024,256]{1,0:T(8,128)(2,1)S(1)} %all-reduce.8), kind=kOutput, calls=%fused_computation.9 | convolution fusion | flops 1074003968 | bytes 3670016 | tf_op jit(solution)/shard_map/dot_general | solution.py:32
  92.9 0.0 all-reduce.5.cloned.1.call-update
  93.0 0.0 all-reduce.7.cloned.1.call-start
  93.0 83.4 %all-reduce.5.cloned.1.call-done = f32[1024,256]{1,0:T(8,128)} async-done(((f32[1024,256]{1,0:T(8,128)}), f32[1024,256]{1,0:T(8,128)}) %all-reduce.5.cloned.1.call-update) | async-done | bytes 1048592 | tf_op jit(solution)/shard_map/psum | solution.py:35
  176.4 2.9 fusion.6
  179.4 0.0 all-reduce.7.cloned.1.call-update
  179.4 0.0 reduce-scatter.3.cloned.1.call-start
  179.4 1.3 dynamic-slice
  181.4 195.3 %all-reduce.7.cloned.1.call-done = f32[896,256]{0,1:T(8,128)} async-done(((f32[896,256]{0,1:T(8,128)}), f32[896,256]{0,1:T(8,128)}) %all-reduce.7.cloned.1.call-update) | async-done | bytes 917520
  376.6 1.0 convert_bitcast_fusion
  377.7 0.1 copy.17
  377.7 50.5 %all-gather = bf16[64,14,256]{2,1,0:T(8,128)(2,1)S(1)} all-gather(bf16[1,14,256]{2,1,0:T(8,128)(2,1)S(1)} %copy.17), channel_id=1, replica_groups=mesh['expert'=64,'seq'=8] {'expert'}, dimensions={0}, use_global_device_ids=true | all-gather | bytes 465920 | tf_op jit(solution)/shard_map/all_gather | solution.py:41
  428.2 0.1 reshape.74
  428.4 1.7 fusion
  430.1 0.0 reduce-scatter.3.cloned.1.call-update
  430.1 0.7 copy.18
  430.8 34.6 %reduce-scatter.3.cloned.1.call-done = f32[256,128]{1,0:T(8,128)} async-done(((f32[256,1024]{1,0:T(8,128)}), f32[256,128]{1,0:T(8,128)}) %reduce-scatter.3.cloned.1.call-update) | async-done | bytes 131088 | tf_op jit(solution)/shard_map/reduce_scatter | solution.py:46
  (4 shorter events, 0.1 us)
Async XLA Ops:
  7.2 20.4 %copy-start = (bf16[1,896,1024]{2,1,0:T(8,128)(2,1)S(1)}, bf16[1,896,1024]{2,1,0:T(8,128)(2,1)}, u32[]{:S(2)}) copy-start(bf16[1,896,1024]{2,1,0:T(8,128)(2,1)} %param.6) | copy-start | bytes 5505028
  15.5 12.0 %copy-start.1 = (bf16[896,256]{1,0:T(8,128)(2,1)S(1)}, bf16[896,256]{1,0:T(8,128)(2,1)}, u32[]{:S(2)}) copy-start(bf16[896,256]{1,0:T(8,128)(2,1)} %param.7) | copy-start | bytes 1376260
  15.5 72.0 %all-to-all-start = ((bf16[64,16,1024]{2,1,0:T(8,128)(2,1)}), bf16[64,16,1024]{2,1,0:T(8,128)(2,1)}, u32[]{:S(2)}, u32[]{:S(2)}) async-start(bf16[64,16,1024]{2,1,0:T(8,128)(2,1)} %bitcast.44), calls=%async_computation | async-start | bytes 4194304 | tf_op jit(solution)/shard_map/all_to_all | solution.py:27
  27.5 148.9 %all-reduce.5.cloned.1.call-start = ((), (), s32[]{:S(2)}) async-start(), calls=%async_computation.2 | async-start | bytes 2097152 | tf_op jit(solution)/shard_map/psum | solution.py:35
  93.0 283.6 %all-reduce.7.cloned.1.call-start = ((), (), s32[]{:S(2)}) async-start(), calls=%async_computation.4 | async-start | bytes 1835008
  179.4 286.0 %reduce-scatter.3.cloned.1.call-start = ((), (), s32[]{:S(2)}) async-start(), calls=%async_computation.3 | async-start | bytes 1179648 | tf_op jit(solution)/shard_map/reduce_scatter | solution.py:46
Sparse Core Ops, SparseCore 0:
  93.1 83.2 all-reduce.4
  179.8 196.7 all-reduce.6
  430.2 35.1 reduce-scatter.2
where the time goes:
time: 477 us; the launch traced here: 472 us
  waiting for transfers between devices  313 us (66%)
  blocking collectives  110 us (23%)
  between operations  14.5 us (3%)
  starting transfers between devices  12.1 us (3%)
  matrix products  10.8 us (2%)
  local copies, waits for them, and re-layouts  8.45 us (2%)
    unnamed x4, waiting for transfers between devices  195 us
    psum x1, waiting for transfers between devices, body(): gram_full = lax.psum(gram_part, 'seq') / row_mean  83.4 us
    psum x1, blocking collectives, body(): probe_proj = lax.psum(partial_value, 'seq').astype(jnp.bfloat16)  59.2 us
    all_gather x1, blocking collectives, body(): lax.all_gather(basis_rows.astype(jnp.bfloat16), 'expert', axis=0, tiled=T...  50.5 us
    reduce_scatter x1, waiting for transfers between devices, body(): lax.psum_scatter(coef_part, 'seq', scatter_dimension=1, tiled=True)  34.6 us
    all_to_all x1, starting transfers between devices, body(): lax.all_to_all(outgoing, 'expert', split_axis=0, concat_axis=0, tiled=True)  11.9 us
  transfers between devices with their start and end apart: 4, of which 3 were waited for; matrix products, arithmetic and copies ran while one was open for 1% of the time, Pallas kernels for 0%

commit v1 on v0

v1 whole, which is shorter than its diff:
```python
import jax
import jax.numpy as jnp
from jax import lax
from jax.sharding import Mesh, PartitionSpec as P

F32 = jnp.float32
BF16 = jnp.bfloat16


def contract(a, b, ca, cb):
    return lax.dot_general(a, b, (((ca,), (cb,)), ((), ())), preferred_element_type=F32)


def swap(value, axes):
    return lax.all_to_all(value, axes, split_axis=0, concat_axis=0, tiled=False)


def body(hidden_rows, routes, down_weight, probe):
    weight = down_weight[0]
    tokens, top, width = hidden_rows.shape
    nx, ny, nc, nz = (lax.axis_size(a) for a in ("x", "y", "c", "z"))
    experts = nx * ny * nc
    chips = nx * ny
    capacity = 2 * tokens * top // experts
    row_mean = tokens * top * nz
    panel = probe.shape[1]

    expert_ids = routes.reshape(-1)
    named = (expert_ids[:, None] == jnp.arange(experts, dtype=jnp.int32)[None, :])
    onehot = named.astype(BF16)
    count = tokens * top
    earlier = jnp.tril(jnp.ones((count, count), BF16), -1)
    before = contract(earlier, onehot, 1, 0)
    position = jnp.sum(jnp.where(named, before, 0.0), axis=1).astype(jnp.int32)
    slot = expert_ids * capacity + position
    pick = (jnp.arange(experts * capacity, dtype=jnp.int32)[:, None] == slot[None, :]).astype(BF16)
    outgoing = contract(pick, hidden_rows.reshape(-1, width), 1, 0).astype(BF16)
    arrived = swap(outgoing.reshape(experts, capacity, width), ("x", "y", "c"))
    rows = arrived.reshape(-1, width)

    proj_part = contract(weight, probe, 0, 0)
    proj_own = jnp.sum(swap(proj_part.reshape(nz, width // nz, panel), "z"), axis=0).astype(BF16)
    probe_proj = lax.all_gather(proj_own, "z", axis=0, tiled=True)

    mixed = jnp.dot(rows, probe_proj, preferred_element_type=F32).astype(BF16)
    gram_part = contract(rows, mixed, 0, 0).astype(BF16)
    gram_own = jnp.sum(swap(gram_part.reshape(nz, width // nz, panel), "z").astype(F32), axis=0)
    gram = lax.all_gather((gram_own / row_mean).astype(BF16), "z", axis=0, tiled=True)

    image = jnp.dot(weight, gram, preferred_element_type=F32).astype(BF16)
    half = panel // nc
    depth = image.shape[0]
    core = lax.axis_index("c")
    kept = lax.dynamic_slice_in_dim(image, core * half, half, 1)
    given = lax.dynamic_slice_in_dim(image, (1 - core) * half, half, 1)
    flip = [(i, 1 - i) for i in range(nc)]
    chip_sum = kept.astype(F32) + lax.ppermute(given, "c", flip).astype(F32)
    pieces = swap(chip_sum.astype(BF16).reshape(chips, depth // chips, half), ("x", "y"))
    own = jnp.sum(pieces.astype(F32), axis=0)

    rows_own = depth // chips // nc
    mine = lax.dynamic_slice_in_dim(own, core * rows_own, rows_own, 0)
    other = lax.ppermute(lax.dynamic_slice_in_dim(own, (1 - core) * rows_own, rows_own, 0), "c", flip)
    basis_rows = jnp.where(core == 0, jnp.concatenate([mine, other], 1), jnp.concatenate([other, mine], 1))

    spread = swap(jnp.broadcast_to(own.astype(BF16)[None], (chips,) + own.shape), ("x", "y"))
    basis_half = spread.reshape(depth, half)
    basis = lax.all_gather(basis_half, "c", axis=1, tiled=True)
    coef_part = contract(basis, weight, 0, 0).astype(BF16)
    coef_split = coef_part.reshape(panel, nz, width // nz).transpose(1, 0, 2)
    coefficients = jnp.sum(swap(coef_split, "z").astype(F32), axis=0)
    return basis_rows, coefficients[None]


def solution(mesh):
    grid = Mesh(mesh.devices.reshape(4, 8, 2, 8), ("x", "y", "c", "z"))
    expert = ("x", "y", "c")
    in_specs = (
        P(expert + ("z",), None, None),
        P(expert + ("z",), None),
        P(expert, "z", None),
        P("z", None),
    )
    out_specs = (P(("z",) + expert, None), P(expert, None, "z"))
    return jax.shard_map(body, mesh=grid, in_specs=in_specs, out_specs=out_specs, check_vma=False)
```

time: 477 us -> 226 us (0.47)
  waiting for transfers between devices: 313 us -> 89.7 us
  blocking collectives: 110 us -> 76.3 us
  starting transfers between devices: 12.1 us -> 39.5 us
  between operations: 14.5 us -> 0.84 us
    unnamed x4 -> x0, waiting for transfers between devices: 195 us -> none
    all_to_all x1 -> x4, waiting for transfers between devices: 0.01 us -> 87.9 us  [swap(): return lax.all_to_all(value, axes, split_axis=0, concat_axis=0, tiled=False)]
    psum x1 -> x0, waiting for transfers between devices: 83.4 us -> none  [body(): gram_full = lax.psum(gram_part, 'seq') / row_mean]
    psum x1 -> x0, blocking collectives: 59.2 us -> none  [body(): probe_proj = lax.psum(partial_value, 'seq').astype(jnp.bfloat16)]
    reduce_scatter x1 -> x0, waiting for transfers between devices: 34.6 us -> none  [body(): lax.psum_scatter(coef_part, 'seq', scatter_dimension=1, tiled=True)]
    all_to_all x0 -> x2, blocking collectives: none -> 30.3 us  [swap(): return lax.all_to_all(value, axes, split_axis=0, concat_axis=0, tiled=False)]
    all_to_all x1 -> x4, starting transfers between devices: 11.9 us -> 28.8 us  [swap(): return lax.all_to_all(value, axes, split_axis=0, concat_axis=0, tiled=False)]
    ppermute x0 -> x2, starting transfers between devices: none -> 10.8 us  [the longest x1 8.48 us: body(): chip_sum = kept.astype(F32) + lax.ppermute(given, 'c', flip).astype(F32)]
  transfers between devices with their start and end apart: 4 -> 6, of which waited for: 3 -> 6; matrix products, arithmetic and copies ran while one was open for 1% -> 2% of each run, Pallas kernels for 0% -> 0%
where the time goes in v1:
time: 226 us
  waiting for transfers between devices  89.7 us (40%)
  blocking collectives  76.3 us (34%)
  starting transfers between devices  39.5 us (17%)
  matrix products  11.4 us (5%)
  local copies, waits for them, and re-layouts  5.34 us (2%)
  other arithmetic  2.55 us (1%)
    all_to_all x4, waiting for transfers between devices, swap(): return lax.all_to_all(value, axes, split_axis=0, concat_axis=0, tiled=False)  87.9 us
    all_to_all x2, blocking collectives, swap(): return lax.all_to_all(value, axes, split_axis=0, concat_axis=0, tiled=False)  30.3 us
    all_to_all x4, starting transfers between devices, swap(): return lax.all_to_all(value, axes, split_axis=0, concat_axis=0, tiled=False)  28.8 us
    all_gather x1, blocking collectives, body(): probe_proj = lax.all_gather(proj_own, 'z', axis=0, tiled=True)  21.3 us
    all_gather x1, blocking collectives, body(): lax.all_gather((gram_own / row_mean).astype(BF16), 'z', axis=0, tiled=True)  19.4 us
    dot_general x5, matrix products, contract(): lax.dot_general(a, b, (((ca,), (cb,)), ((), ())), preferred_element_type=...  10.6 us
    ppermute x1, starting transfers between devices, body(): chip_sum = kept.astype(F32) + lax.ppermute(given, 'c', flip).astype(F32)  8.48 us
    all_gather x1, blocking collectives, body(): basis = lax.all_gather(basis_half, 'c', axis=1, tiled=True)  5.35 us
  transfers between devices with their start and end apart: 6, of which 6 were waited for; matrix products, arithmetic and copies ran while one was open for 2% of the time, Pallas kernels for 0%

profile of v1, /device:TPU:1, one launch (start us, length us, event | category | flops | bytes accessed | tf_op | source)
XLA Modules:
  0.0 225.7 jit_solution(15201904150336880675)
XLA Ops:
  0.6 0.0 copy-start
  0.6 0.0 copy-start.2
  0.7 3.2 %copy.12 = bf16[1024,896]{1,0:T(8,128)(2,1)S(1)} copy(bf16[1024,896]{0,1:T(8,128)(2,1)} %bitcast.45) | data formatting | bytes 3670016 | tf_op jit(solution)/shard_map/dot_general | solution.py:11
  3.8 0.0 copy-done.2
  3.8 0.0 copy-start.4
  3.9 1.7 fusion.22
  5.5 10.9 %all-to-all-start.1 = ((f32[8,128,256]{2,1,0:T(8,128)}), f32[8,128,256]{2,1,0:T(8,128)S(1)}, u32[]{:S(2)}, u32[]{:S(2)}) async-start(f32[8,128,256]{2,1,0:T(8,128)} %fusion.22), calls=%async_computation.1 | async-start | bytes 2097152 | tf_op jit(solution)/shard_map/all_to_all | solution.py:15
  16.4 0.0 copy-done.4
  16.4 0.1 copy.8
  16.5 0.1 reshape.43
  16.6 0.4 fusion.15
  17.0 0.0 copy-done
  17.0 2.6 %fusion.1 = bf16[1024,1024]{1,0:T(8,128)(2,1)} fusion(bf16[64,8,1024]{2,1,0:T(8,128)(2,1)S(1)} %copy-done, s32[512]{0:T(512)S(1)} %convert_add_fusion), kind=kOutput, calls=%fused_computation.2 | convolution fusion | flops 1075314688 | bytes 3147776 | tf_op jit(solution)/shard_map/dot_general | solution.py:11
  19.6 26.0 %all-to-all-done.1 = f32[8,128,256]{2,1,0:T(8,128)S(1)} async-done(((f32[8,128,256]{2,1,0:T(8,128)}), f32[8,128,256]{2,1,0:T(8,128)S(1)}, u32[]{:S(2)}, u32[]{:S(2)}) %all-to-all-start.1) | async-done | bytes 1048608 | tf_op jit(solution)/shard_map/all_to_all | solution.py:15
  45.6 10.8 %all-to-all-start = ((bf16[64,16,1024]{2,1,0:T(8,128)(2,1)}), bf16[64,16,1024]{2,1,0:T(8,128)(2,1)}, u32[]{:S(2)}, u32[]{:S(2)}) async-start(bf16[64,16,1024]{2,1,0:T(8,128)(2,1)} %bitcast.46), calls=%async_computation | async-start | bytes 4194304 | tf_op jit(solution)/shard_map/all_to_all | solution.py:15
  56.4 0.1 reduce_sum.46
  56.5 21.3 %all_gather.9 = bf16[1024,256]{1,0:T(8,128)(2,1)S(1)} all-gather(bf16[128,256]{1,0:T(8,128)(2,1)S(1)} %reduce_sum.46), channel_id=1, replica_groups=mesh['x'=4,'y'=8,'c'=2,'z'=8] {'z'}, dimensions={0}, use_global_device_ids=true | all-gather | bytes 589824 | tf_op jit(solution)/shard_map/all_gather | solution.py:43
  77.8 29.8 %all-to-all-done = bf16[64,16,1024]{2,1,0:T(8,128)(2,1)} async-done(((bf16[64,16,1024]{2,1,0:T(8,128)(2,1)}), bf16[64,16,1024]{2,1,0:T(8,128)(2,1)}, u32[]{:S(2)}, u32[]{:S(2)}) %all-to-all-start) | async-done | bytes 2097184 | tf_op jit(solution)/shard_map/all_to_all | solution.py:15
  107.6 5.2 %convolution_convert_fusion = bf16[1024,256]{1,0:T(8,128)(2,1)} fusion(bf16[1024,1024]{1,0:T(8,128)(2,1)} %bitcast.2, bf16[1024,256]{1,0:T(8,128)(2,1)S(1)} %all_gather.9), kind=kOutput, calls=%fused_computation.8 | convolution fusion | flops 1074266112 | bytes 3145728 | tf_op jit(solution)/shard_map/dot_general | solution.py:11
  112.8 0.0 copy-start.1
  112.8 3.6 %all-to-all-start.2 = ((bf16[8,128,256]{2,1,0:T(8,128)(2,1)}), bf16[8,128,256]{2,1,0:T(8,128)(2,1)S(1)}, u32[]{:S(2)}, u32[]{:S(2)}) async-start(bf16[8,128,256]{2,1,0:T(8,128)(2,1)} %bitcast.47), calls=%async_computation.2 | async-start | bytes 1048576 | tf_op jit(solution)/shard_map/all_to_all | solution.py:15
  116.5 17.9 %all-to-all-done.2 = bf16[8,128,256]{2,1,0:T(8,128)(2,1)S(1)} async-done(((bf16[8,128,256]{2,1,0:T(8,128)(2,1)}), bf16[8,128,256]{2,1,0:T(8,128)(2,1)S(1)}, u32[]{:S(2)}, u32[]{:S(2)}) %all-to-all-start.2) | async-done | bytes 524320 | tf_op jit(solution)/shard_map/all_to_all | solution.py:15
  134.3 0.1 convert_reduce_fusion.1
  134.4 19.4 %all_gather.10 = bf16[1024,256]{1,0:T(8,128)(2,1)S(1)} all-gather(bf16[128,256]{1,0:T(8,128)(2,1)S(1)} %multiply_convert_fusion), channel_id=1, replica_groups=mesh['x'=4,'y'=8,'c'=2,'z'=8] {'z'}, dimensions={0}, use_global_device_ids=true | all-gather | bytes 589824 | tf_op jit(solution)/shard_map/all_gather | solution.py:48
  153.8 0.0 copy-done.1
  153.8 0.8 fusion.9
  154.6 0.0 copy-start.3
  154.6 0.8 copy-done.3
  155.4 8.5 %collective-permute-start = (bf16[896,128]{0,1:T(8,128)(2,1)S(1)}, bf16[896,128]{0,1:T(8,128)(2,1)S(1)}, u32[]{:S(2)}, u32[]{:S(2)}) collective-permute-start(bf16[896,128]{0,1:T(8,128)(2,1)S(1)} %dynamic-slice_bitcast_fusion), channel_id=1, source_target_pairs={{0,8},{8,0},{1,9},{9,1},{2,10},{10,2},{3,11},{11,3},{4,12},{12,4},... | collective-permute-start | bytes 688136 | tf_op jit(solution)/shard_map/ppermute | solution.py:57
  163.8 1.1 collective-permute-done
  164.9 1.0 fusion.21
  165.9 0.2 copy.10
  166.2 14.1 %all_to_all.30 = bf16[32,28,128]{2,1,0:T(8,128)(2,1)S(1)} all-to-all(bf16[32,28,128]{2,1,0:T(8,128)(2,1)S(1)} %reshape.48), channel_id=1, replica_groups=mesh['x'=4,'y'=8,'c'=2,'z'=8] {'x','y'}, dimensions={0} | all-to-all | bytes 458752 | tf_op jit(solution)/shard_map/all_to_all | solution.py:15
  180.3 0.1 convert_reduce_fusion.2
  180.4 16.2 %all_to_all.31 = bf16[32,28,128]{2,1,0:T(8,128)(2,1)S(1)} all-to-all(bf16[32,28,128]{2,1,0:T(8,128)(2,1)S(1)} %broadcast_in_dim.26), channel_id=1, replica_groups=mesh['x'=4,'y'=8,'c'=2,'z'=8] {'x','y'}, dimensions={0} | all-to-all | bytes 458752 | tf_op jit(solution)/shard_map/all_to_all | solution.py:15
  196.6 5.4 %all_gather.11 = bf16[896,256]{1,0:T(8,128)(2,1)S(1)} all-gather(bf16[896,128]{1,0:T(8,128)(2,1)S(1)} %reshape.49), channel_id=1, replica_groups=mesh['x'=4,'y'=8,'c'=2,'z'=8] {'c'}, dimensions={1}, use_global_device_ids=true | all-gather | bytes 688128 | tf_op jit(solution)/shard_map/all_gather | solution.py:68
  201.9 0.7 fusion.12
  202.7 0.9 copy.15
  203.6 3.5 %all-to-all-start.5 = ((bf16[8,256,128]{2,1,0:T(8,128)(2,1)}), bf16[8,256,128]{2,1,0:T(8,128)(2,1)S(1)}, u32[]{:S(2)}, u32[]{:S(2)}) async-start(bf16[8,256,128]{2,1,0:T(8,128)(2,1)} %bitcast.43), calls=%async_computation.5 | async-start | bytes 1048576 | tf_op jit(solution)/shard_map/all_to_all | solution.py:15
  207.1 2.3 %collective-permute-start.1 = (f32[14,128]{1,0:T(8,128)S(1)}, f32[14,128]{1,0:T(8,128)S(1)}, u32[]{:S(2)}, u32[]{:S(2)}) collective-permute-start(f32[14,128]{1,0:T(8,128)S(1)} %get-tuple-element.3), channel_id=1, source_target_pairs={{0,8},{8,0},{1,9},{9,1},{2,10},{10,2},{3,11},{11,3},{4,12},{12,4},... | collective-permute-start | bytes 21512 | tf_op jit(solution)/shard_map/ppermute | solution.py:63
  209.4 0.8 collective-permute-done.1
  210.2 0.6 maximum_select_fusion
  210.8 14.2 %all-to-all-done.5 = bf16[8,256,128]{2,1,0:T(8,128)(2,1)S(1)} async-done(((bf16[8,256,128]{2,1,0:T(8,128)(2,1)}), bf16[8,256,128]{2,1,0:T(8,128)(2,1)S(1)}, u32[]{:S(2)}, u32[]{:S(2)}) %all-to-all-start.5) | async-done | bytes 524320 | tf_op jit(solution)/shard_map/all_to_all | solution.py:15
  225.0 0.7 convert_reduce_fusion
  (9 shorter events, 0.2 us)
Async XLA Ops:
  0.6 16.4 %copy-start = (bf16[64,8,1024]{2,1,0:T(8,128)(2,1)S(1)}, bf16[64,8,1024]{2,1,0:T(8,128)(2,1)}, u32[]{:S(2)}) copy-start(bf16[64,8,1024]{2,1,0:T(8,128)(2,1)} %param.4) | copy-start | bytes 3145732
  0.6 3.2 %copy-start.2 = (bf16[896,256]{1,0:T(8,128)(2,1)S(1)}, bf16[896,256]{1,0:T(8,128)(2,1)}, u32[]{:S(2)}) copy-start(bf16[896,256]{1,0:T(8,128)(2,1)} %param.7) | copy-start | bytes 1376260
  3.8 12.6 %copy-start.4 = (s32[64,8]{0,1:T(8,128)S(1)}, s32[64,8]{0,1:T(8,128)}, u32[]{:S(2)}) copy-start(s32[64,8]{0,1:T(8,128)} %param.5) | copy-start | bytes 6148
  5.5 40.1 %all-to-all-start.1 = ((f32[8,128,256]{2,1,0:T(8,128)}), f32[8,128,256]{2,1,0:T(8,128)S(1)}, u32[]{:S(2)}, u32[]{:S(2)}) async-start(f32[8,128,256]{2,1,0:T(8,128)} %fusion.22), calls=%async_computation.1 | async-start | bytes 2097152 | tf_op jit(solution)/shard_map/all_to_all | solution.py:15
  45.6 62.0 %all-to-all-start = ((bf16[64,16,1024]{2,1,0:T(8,128)(2,1)}), bf16[64,16,1024]{2,1,0:T(8,128)(2,1)}, u32[]{:S(2)}, u32[]{:S(2)}) async-start(bf16[64,16,1024]{2,1,0:T(8,128)(2,1)} %bitcast.46), calls=%async_computation | async-start | bytes 4194304 | tf_op jit(solution)/shard_map/all_to_all | solution.py:15
  112.8 41.0 %copy-start.1 = (bf16[1,896,1024]{2,1,0:T(8,128)(2,1)S(1)}, bf16[1,896,1024]{2,1,0:T(8,128)(2,1)}, u32[]{:S(2)}) copy-start(bf16[1,896,1024]{2,1,0:T(8,128)(2,1)} %param.6) | copy-start | bytes 5505028
  112.8 21.5 %all-to-all-start.2 = ((bf16[8,128,256]{2,1,0:T(8,128)(2,1)}), bf16[8,128,256]{2,1,0:T(8,128)(2,1)S(1)}, u32[]{:S(2)}, u32[]{:S(2)}) async-start(bf16[8,128,256]{2,1,0:T(8,128)(2,1)} %bitcast.47), calls=%async_computation.2 | async-start | bytes 1048576 | tf_op jit(solution)/shard_map/all_to_all | solution.py:15
  154.6 0.8 copy-start.3
  155.4 9.6 %collective-permute-start = (bf16[896,128]{0,1:T(8,128)(2,1)S(1)}, bf16[896,128]{0,1:T(8,128)(2,1)S(1)}, u32[]{:S(2)}, u32[]{:S(2)}) collective-permute-start(bf16[896,128]{0,1:T(8,128)(2,1)S(1)} %dynamic-slice_bitcast_fusion), channel_id=1, source_target_pairs={{0,8},{8,0},{1,9},{9,1},{2,10},{10,2},{3,11},{11,3},{4,12},{12,4},... | collective-permute-start | bytes 688136 | tf_op jit(solution)/shard_map/ppermute | solution.py:57
  203.6 21.4 %all-to-all-start.5 = ((bf16[8,256,128]{2,1,0:T(8,128)(2,1)}), bf16[8,256,128]{2,1,0:T(8,128)(2,1)S(1)}, u32[]{:S(2)}, u32[]{:S(2)}) async-start(bf16[8,256,128]{2,1,0:T(8,128)(2,1)} %bitcast.43), calls=%async_computation.5 | async-start | bytes 1048576 | tf_op jit(solution)/shard_map/all_to_all | solution.py:15
  207.1 3.1 %collective-permute-start.1 = (f32[14,128]{1,0:T(8,128)S(1)}, f32[14,128]{1,0:T(8,128)S(1)}, u32[]{:S(2)}, u32[]{:S(2)}) collective-permute-start(f32[14,128]{1,0:T(8,128)S(1)} %get-tuple-element.3), channel_id=1, source_target_pairs={{0,8},{8,0},{1,9},{9,1},{2,10},{10,2},{3,11},{11,3},{4,12},{12,4},... | collective-permute-start | bytes 21512 | tf_op jit(solution)/shard_map/ppermute | solution.py:63

commit v2 on v1

v2 whole, which is shorter than its diff:
```python
import functools

import jax
import jax.numpy as jnp
from jax import lax
from jax.experimental import pallas as pl
from jax.experimental.pallas import tpu as pltpu
from jax.sharding import Mesh, PartitionSpec as P

F32 = jnp.float32
BF16 = jnp.bfloat16
VMEM_BYTES = 16 * 1024 * 1024
WIDE_BYTES = 125 * 512 * 1024


def contract(a, b, ca, cb):
    return lax.dot_general(a, b, (((ca,), (cb,)), ((), ())), preferred_element_type=F32)


def swap(value, axes):
    return lax.all_to_all(value, axes, split_axis=0, concat_axis=0, tiled=False)


def share(value, axes, count):
    copies = jnp.broadcast_to(value[None], (count,) + value.shape)
    return swap(copies, axes).reshape(-1, value.shape[1])


VMEM = pl.BlockSpec(memory_space=pltpu.VMEM)
SMEM = pl.BlockSpec(memory_space=pltpu.SMEM)
HBM = pl.BlockSpec(memory_space=pltpu.MemorySpace.HBM)


def call(kernel, outs, flops, operands, in_specs=None, out_specs=None, scratch=(), limit=VMEM_BYTES):
    sizes = [a.size * a.dtype.itemsize for a in tuple(operands) + tuple(outs)]
    out = pl.pallas_call(
        kernel,
        out_shape=outs,
        in_specs=in_specs or [VMEM] * len(operands),
        out_specs=out_specs or [VMEM] * len(outs),
        scratch_shapes=scratch,
        compiler_params=pltpu.CompilerParams(vmem_limit_bytes=limit),
        cost_estimate=pl.CostEstimate(flops=flops, bytes_accessed=sum(sizes), transcendentals=0),
    )(*operands)
    return out[0] if len(outs) == 1 else out


def dispatch_kernel(capacity, routes_ref, rows_hbm, out_hbm, rows_ref, out_ref, in_sem, out_sem):
    top, tokens = routes_ref.shape
    count = tokens * top
    experts = out_ref.shape[0] // capacity
    fetch = pltpu.make_async_copy(rows_hbm, rows_ref, in_sem)
    fetch.start()

    def iota(dims, axis):
        return lax.broadcasted_iota(jnp.int32, dims, axis)

    def flag(condition):
        return jnp.where(condition, 1.0, 0.0).astype(BF16)

    spread = flag(iota((top, count), 0) == iota((top, count), 1) % top)
    token = flag(iota((tokens, count), 0) == iota((tokens, count), 1) // top)
    names = contract(routes_ref[...].astype(F32).astype(BF16), spread, 0, 0)
    expert = jnp.sum(names * token.astype(F32), axis=0, keepdims=True).astype(jnp.int32)
    named = flag(iota((experts, count), 0) == expert)
    by_token = contract(named, token, 1, 1).astype(BF16)
    earlier = flag(iota((tokens, tokens), 0) < iota((tokens, tokens), 1))
    before = jnp.dot(by_token, earlier, preferred_element_type=F32).astype(BF16)
    position = jnp.sum(jnp.dot(before, token, preferred_element_type=F32) * named.astype(F32), axis=0, keepdims=True)
    slot = expert * capacity + position.astype(jnp.int32)

    block = 256
    fetch.wait()
    rows = rows_ref[...]
    sends = []
    for i in range(out_ref.shape[0] // block):
        part = pl.ds(i * block, block)
        pick = flag(iota((block, count), 0) + i * block == slot)
        out_ref[part, :] = jnp.dot(pick, rows, preferred_element_type=F32).astype(BF16)
        sends.append(pltpu.make_async_copy(out_ref.at[part, :], out_hbm.at[part, :], out_sem.at[i]))
        sends[-1].start()
    for send in sends:
        send.wait()


def probe_kernel(quarter_ref, weight_ref, probe_ref, kept_ref, given_ref):
    quarter = quarter_ref[0]
    size = kept_ref.shape[0]
    probe = probe_ref[...]
    for step in (3, 2, 1, 0):
        start = pl.multiple_of((quarter ^ step) * size, size)
        part = contract(weight_ref[:, pl.ds(start, size)], probe, 0, 0)
        if step == 0:
            kept_ref[...] = part
        else:
            given_ref[step - 1] = part.astype(BF16)


def gram_kernel(quarter_ref, rows_ref, proj0, proj1, proj2, proj3, out_ref, proj_ref):
    quarter = quarter_ref[0]
    block = 256
    count, width = rows_ref.shape
    size = out_ref.shape[2]
    depth = proj0.shape[0]
    for step, part in enumerate((proj0, proj1, proj2, proj3)):
        proj_ref[pl.ds(pl.multiple_of((quarter ^ step) * depth, depth), depth), :] = part[...]
    proj = proj_ref[...]
    turned = []
    for i in range(count // block):
        mixed = jnp.dot(rows_ref[i * block : (i + 1) * block, :], proj, preferred_element_type=F32)
        turned.append(mixed.astype(BF16).T)
    turned = jnp.concatenate(turned, axis=1)
    for i in range(0, width, block):
        part = jnp.dot(turned, rows_ref[:, i : i + block], preferred_element_type=F32).astype(BF16)
        for j in range(0, block, size):
            out_ref[(i + j) // size] = part[:, j : j + size]


def coef_kernel(basis_ref, weight_ref, out_ref):
    block = 256
    size = out_ref.shape[2]
    turned = basis_ref[...].T
    for i in range(0, weight_ref.shape[1], block):
        part = jnp.dot(turned, weight_ref[:, i : i + block], preferred_element_type=F32).astype(BF16)
        for j in range(0, block, size):
            out_ref[(i + j) // size] = part[:, j : j + size]


def body(hidden_rows, routes, down_weight, probe):
    weight = down_weight[0]
    tokens, top, width = hidden_rows.shape
    nx, ny, nc, nz = (lax.axis_size(a) for a in ("x", "y", "c", "z"))
    experts = nx * ny * nc
    chips = nx * ny
    capacity = 2 * tokens * top // experts
    row_mean = tokens * top * nz
    depth, panel = probe.shape
    half = panel // nc
    block = width // nz
    count = tokens * top
    core = lax.axis_index("c")
    me = lax.axis_index("z")

    def across(value, axis, size, step):
        return lax.ppermute(value, axis, [(i, i ^ step) for i in range(size)])

    def shape(dims, dtype):
        return jax.ShapeDtypeStruct(dims, dtype)

    slots = experts * capacity
    outgoing = call(
        functools.partial(dispatch_kernel, capacity),
        [shape((slots, width), BF16)],
        2 * slots * count * width,
        [routes.T, hidden_rows.reshape(count, width)],
        [VMEM, HBM],
        [HBM],
        [
            pltpu.VMEM((count, width), BF16),
            pltpu.VMEM((slots, width), BF16),
            pltpu.SemaphoreType.DMA,
            pltpu.SemaphoreType.DMA((slots // 256,)),
        ],
        WIDE_BYTES,
    )
    rows = swap(outgoing.reshape(experts, capacity, width), ("x", "y", "c")).reshape(slots, width)

    quarter = (me % 4)[None]
    four = width // 4
    kept, given = call(
        probe_kernel,
        [shape((four, panel), F32), shape((3, four, panel), BF16)],
        2 * depth * width * panel,
        [quarter, weight, probe],
        [SMEM, VMEM, VMEM],
    )
    proj = kept + sum(across(given[step - 1], "z", nz, step).astype(F32) for step in (3, 2, 1))
    proj = (proj + across(proj.astype(BF16), "z", nz, 4).astype(F32)).astype(BF16)
    quarters = [across(proj, "z", nz, step) for step in (3, 2, 1)]

    gram_part = call(
        gram_kernel,
        [shape((nz, panel, block), BF16)],
        4 * slots * width * panel,
        [quarter, rows, proj] + quarters[::-1],
        [SMEM] + [VMEM] * 5,
        None,
        [pltpu.VMEM((width, panel), BF16)],
    )
    gram_own = jnp.sum(swap(gram_part, "z").astype(F32), axis=0) / row_mean
    gram = swap(jnp.broadcast_to(gram_own.astype(BF16)[None], gram_part.shape), "z")
    gram = gram.transpose(1, 0, 2).reshape(panel, width)

    image = contract(weight, gram, 1, 1).astype(BF16)
    kept = lax.dynamic_slice_in_dim(image, core * half, half, 1)
    given = lax.dynamic_slice_in_dim(image, (1 - core) * half, half, 1)
    came = lax.dynamic_index_in_dim(lax.all_gather(given, "c"), 1 - core, 0, False)
    chip_sum = kept.astype(F32) + came.astype(F32)
    pieces = swap(chip_sum.astype(BF16).reshape(chips, depth // chips, half), ("x", "y"))
    own = jnp.sum(pieces.astype(F32), axis=0).astype(BF16)
    basis_half = share(own, ("x", "y"), chips)
    basis = lax.all_gather(basis_half, "c", axis=1, tiled=True)

    rows_own = depth // experts
    place = (lax.axis_index("x") * ny + lax.axis_index("y")) * nc + core
    basis_rows = lax.dynamic_slice_in_dim(basis, place * rows_own, rows_own, 0).astype(F32)
    coef_part = call(coef_kernel, [shape((nz, panel, block), BF16)], 2 * depth * width * panel, [basis, weight])
    coefficients = jnp.sum(swap(coef_part, "z").astype(F32), axis=0)
    return basis_rows, coefficients[None]


def solution(mesh):
    grid = Mesh(mesh.devices.reshape(4, 8, 2, 8), ("x", "y", "c", "z"))
    expert = ("x", "y", "c")
    in_specs = (
        P(expert + ("z",), None, None),
        P(expert + ("z",), None),
        P(expert, "z", None),
        P("z", None),
    )
    out_specs = (P(("z",) + expert, None), P(expert, None, "z"))
    return jax.shard_map(body, mesh=grid, in_specs=in_specs, out_specs=out_specs, check_vma=False)
```

time: 226 us -> 185 us (0.82)
  waiting for transfers between devices: 89.7 us -> 49.5 us
  starting transfers between devices: 39.5 us -> 52.7 us
  matrix products: 11.4 us -> 0.76 us
  Pallas kernels: 0 us -> 9.23 us
  blocking collectives: 76.3 us -> 67.7 us
  local copies, waits for them, and re-layouts: 5.34 us -> 1.9 us
    all_to_all x4 -> x3, waiting for transfers between devices: 87.9 us -> 35.9 us  [swap(): return lax.all_to_all(value, axes, split_axis=0, concat_axis=0, tiled=False)]
    all_gather x2 -> x1, blocking collectives: 40.7 us -> 4.31 us  [body(): lax.all_gather(given, 'c')]
    all_to_all x2 -> x3, blocking collectives: 30.3 us -> 58.1 us  [swap(): return lax.all_to_all(value, axes, split_axis=0, concat_axis=0, tiled=False)]
    ppermute x2 -> x7, starting transfers between devices: 10.8 us -> 33.8 us  [across(): return lax.ppermute(value, axis, [(i, i ^ step) for i in range(size)])]
    ppermute x2 -> x7, waiting for transfers between devices: 1.89 us -> 13.6 us  [across(): return lax.ppermute(value, axis, [(i, i ^ step) for i in range(size)])]
    all_to_all x4 -> x3, starting transfers between devices: 28.8 us -> 18.9 us  [swap(): return lax.all_to_all(value, axes, split_axis=0, concat_axis=0, tiled=False)]
    dot_general x5 -> x1, matrix products: 10.6 us -> 0.76 us  [contract(): lax.dot_general(a, b, (((ca,), (cb,)), ((), ())), preferred_element_type=...]
    pallas_call x0 -> x4, Pallas kernels: none -> 9.23 us  [call(): pl.pallas_call(kernel, out_shape=outs, in_specs=in_specs or [VMEM] * len(...]
  transfers between devices with their start and end apart: 6 -> 10, of which waited for: 6 -> 7; matrix products, arithmetic and copies ran while one was open for 2% -> 0% of each run, Pallas kernels for 0% -> 0%
where the time goes in v2:
time: 185 us; the launch traced here: 184 us
  blocking collectives  67.7 us (37%)
  starting transfers between devices  52.7 us (28%)
  waiting for transfers between devices  49.5 us (27%)
  Pallas kernels  9.23 us (5%)
  local copies, waits for them, and re-layouts  1.9 us (1%)
    all_to_all x3, blocking collectives, swap(): return lax.all_to_all(value, axes, split_axis=0, concat_axis=0, tiled=False)  58.1 us
    all_to_all x3, waiting for transfers between devices, swap(): return lax.all_to_all(value, axes, split_axis=0, concat_axis=0, tiled=False)  35.9 us
    ppermute x7, starting transfers between devices, across(): return lax.ppermute(value, axis, [(i, i ^ step) for i in range(size)])  33.8 us
    all_to_all x3, starting transfers between devices, swap(): return lax.all_to_all(value, axes, split_axis=0, concat_axis=0, tiled=False)  18.9 us
    ppermute x7, waiting for transfers between devices, across(): return lax.ppermute(value, axis, [(i, i ^ step) for i in range(size)])  13.6 us
    pallas_call x4, Pallas kernels, call(): pl.pallas_call(kernel, out_shape=outs, in_specs=in_specs or [VMEM] * len(...  9.23 us
    all_gather x1, blocking collectives, body(): basis = lax.all_gather(basis_half, 'c', axis=1, tiled=True)  5.35 us
    all_gather x1, blocking collectives, body(): lax.all_gather(given, 'c')  4.31 us
  transfers between devices with their start and end apart: 10, of which 7 were waited for; matrix products, arithmetic and copies ran while one was open for 0% of the time, Pallas kernels for 0%

profile of v2, /device:TPU:1, one launch (start us, length us, event | category | flops | bytes accessed | tf_op | source)
XLA Modules:
  0.0 184.4 jit_solution(7967644375328575358)
XLA Ops:
  0.6 4.0 %shard_map.59 = bf16[1024,1024]{1,0:T(8,128)(2,1)} custom-call(s32[8,64]{1,0:T(8,128)} %bitcast.36, bf16[512,1024]{1,0:T(8,128)(2,1)} %bitcast.35), custom_call_target="tpu_custom_call" | custom-call | flops 1073741824 | bytes 3147776 | tf_op jit(solution)/shard_map/pallas_call | solution.py:36
  4.6 0.0 copy-start
  4.7 0.0 copy-start.1
  4.7 12.0 %all-to-all-start = ((bf16[64,16,1024]{2,1,0:T(8,128)(2,1)}), bf16[64,16,1024]{2,1,0:T(8,128)(2,1)}, u32[]{:S(2)}, u32[]{:S(2)}) async-start(bf16[64,16,1024]{2,1,0:T(8,128)(2,1)} %bitcast.32), calls=%async_computation | async-start | bytes 4194304 | tf_op jit(solution)/shard_map/all_to_all | solution.py:21
  16.6 0.0 copy-done
  16.7 0.0 copy-done.1
  16.7 0.8 shard_map.60
  17.5 4.0 %collective-permute-start.2 = (bf16[256,256]{1,0:T(8,128)(2,1)S(1)}, bf16[256,256]{1,0:T(8,128)(2,1)S(1)}, u32[]{:S(2)}, u32[]{:S(2)}) collective-permute-start(bf16[256,256]{1,0:T(8,128)(2,1)S(1)} %get-tuple-element.7), channel_id=1, source_target_pairs={{0,1},{1,0},{2,3},{3,2},{4,5},{5,4},{6,7},{7,6},{8,9},{9,8},{10,11... | collective-permute-start | bytes 393224 | tf_op jit(solution)/shard_map/ppermute | solution.py:145
  21.5 5.8 %collective-permute-start.1 = (bf16[256,256]{1,0:T(8,128)(2,1)S(1)}, bf16[256,256]{1,0:T(8,128)(2,1)S(1)}, u32[]{:S(2)}, u32[]{:S(2)}) collective-permute-start(bf16[256,256]{1,0:T(8,128)(2,1)S(1)} %get-tuple-element.8), channel_id=1, source_target_pairs={{0,2},{1,3},{2,0},{3,1},{4,6},{5,7},{6,4},{7,5},{8,10},{9,11},{10,... | collective-permute-start | bytes 393224 | tf_op jit(solution)/shard_map/ppermute | solution.py:145
  27.3 1.9 %collective-permute-start = (bf16[256,256]{1,0:T(8,128)(2,1)S(1)}, bf16[256,256]{1,0:T(8,128)(2,1)S(1)}, u32[]{:S(2)}, u32[]{:S(2)}) collective-permute-start(bf16[256,256]{1,0:T(8,128)(2,1)S(1)} %get-tuple-element.6), channel_id=1, source_target_pairs={{0,3},{1,2},{2,1},{3,0},{4,7},{5,6},{6,5},{7,4},{8,11},{9,10},{10,... | collective-permute-start | bytes 393224 | tf_op jit(solution)/shard_map/ppermute | solution.py:145
  29.2 0.0 collective-permute-done.2
  29.2 4.5 %collective-permute-done.1 = bf16[256,256]{1,0:T(8,128)(2,1)S(1)} collective-permute-done((bf16[256,256]{1,0:T(8,128)(2,1)S(1)}, bf16[256,256]{1,0:T(8,128)(2,1)S(1)}, u32[]{:S(2)}, u32[]{:S(2)}) %collective-permute-start.1) | collective-permute-done | bytes 131104 | tf_op jit(solution)/shard_map/ppermute | solution.py:145
  33.7 1.4 collective-permute-done
  35.1 0.1 fusion.1
  35.2 8.1 %collective-permute-start.3 = (bf16[256,256]{1,0:T(8,128)(2,1)S(1)}, bf16[256,256]{1,0:T(8,128)(2,1)S(1)}, u32[]{:S(2)}, u32[]{:S(2)}) collective-permute-start(bf16[256,256]{1,0:T(8,128)(2,1)S(1)} %fusion.1), channel_id=1, source_target_pairs={{0,4},{1,5},{2,6},{3,7},{4,0},{5,1},{6,2},{7,3},{8,12},{9,13},{10,... | collective-permute-start | bytes 393224 | tf_op jit(solution)/shard_map/ppermute | solution.py:145
  43.3 2.4 %collective-permute-done.3 = bf16[256,256]{1,0:T(8,128)(2,1)S(1)} collective-permute-done((bf16[256,256]{1,0:T(8,128)(2,1)S(1)}, bf16[256,256]{1,0:T(8,128)(2,1)S(1)}, u32[]{:S(2)}, u32[]{:S(2)}) %collective-permute-start.3) | collective-permute-done | bytes 131104 | tf_op jit(solution)/shard_map/ppermute | solution.py:145
  45.7 0.1 add_convert_fusion.proj0
  45.8 8.1 %collective-permute-start.4 = (bf16[256,256]{1,0:T(8,128)(2,1)S(1)}, bf16[256,256]{1,0:T(8,128)(2,1)S(1)}, u32[]{:S(2)}, u32[]{:S(2)}) collective-permute-start(bf16[256,256]{1,0:T(8,128)(2,1)S(1)} %add_convert_fusion.proj0), channel_id=1, source_target_pairs={{0,1},{1,0},{2,3},{3,2},{4,5},{5,4},{6,7},{7,6},{8,9},{9,8},{10,11... | collective-permute-start | bytes 393224 | tf_op jit(solution)/shard_map/ppermute | solution.py:145
  53.9 2.4 %collective-permute-start.5 = (bf16[256,256]{1,0:T(8,128)(2,1)S(1)}, bf16[256,256]{1,0:T(8,128)(2,1)S(1)}, u32[]{:S(2)}, u32[]{:S(2)}) collective-permute-start(bf16[256,256]{1,0:T(8,128)(2,1)S(1)} %add_convert_fusion.proj0), channel_id=1, source_target_pairs={{0,2},{1,3},{2,0},{3,1},{4,6},{5,7},{6,4},{7,5},{8,10},{9,11},{10,... | collective-permute-start | bytes 393224 | tf_op jit(solution)/shard_map/ppermute | solution.py:145
  56.3 3.5 %collective-permute-start.6 = (bf16[256,256]{1,0:T(8,128)(2,1)S(1)}, bf16[256,256]{1,0:T(8,128)(2,1)S(1)}, u32[]{:S(2)}, u32[]{:S(2)}) collective-permute-start(bf16[256,256]{1,0:T(8,128)(2,1)S(1)} %add_convert_fusion.proj0), channel_id=1, source_target_pairs={{0,3},{1,2},{2,1},{3,0},{4,7},{5,6},{6,5},{7,4},{8,11},{9,10},{10,... | collective-permute-start | bytes 393224 | tf_op jit(solution)/shard_map/ppermute | solution.py:145
  59.8 0.0 collective-permute-done.4.proj1
  59.8 5.2 %collective-permute-done.5.proj2 = bf16[256,256]{1,0:T(8,128)(2,1)S(1)} collective-permute-done((bf16[256,256]{1,0:T(8,128)(2,1)S(1)}, bf16[256,256]{1,0:T(8,128)(2,1)S(1)}, u32[]{:S(2)}, u32[]{:S(2)}) %collective-permute-start.5) | collective-permute-done | bytes 131104 | tf_op jit(solution)/shard_map/ppermute | solution.py:145
  65.0 0.0 collective-permute-done.6.proj3
  65.1 2.8 %all-to-all-done = bf16[64,16,1024]{2,1,0:T(8,128)(2,1)} async-done(((bf16[64,16,1024]{2,1,0:T(8,128)(2,1)}), bf16[64,16,1024]{2,1,0:T(8,128)(2,1)}, u32[]{:S(2)}, u32[]{:S(2)}) %all-to-all-start) | async-done | bytes 2097184 | tf_op jit(solution)/shard_map/all_to_all | solution.py:21
  67.9 2.9 %shard_map.61 = bf16[8,256,128]{2,1,0:T(8,128)(2,1)S(1)} custom-call(s32[1]{0:T(128)} %bitcast.quarter_ref, bf16[1024,1024]{1,0:T(8,128)(2,1)} %bitcast.4.rows_ref, bf16[256,256]{1,0:T(8,128)(2,1)S(1)} %add_convert_fusion.proj0, bf16[256,256]{1,0:T(8,128)(2,1)S(1)} %collective-permute-done.4.proj1, bf16[256,256]{1,0:T(8,128)(2,1)S(1)} %collective-permute-done.5.proj2, ...), custom_call_target="tpu_custom_call" | custom-call | flops 1073741824 | bytes 3145732 | tf_op jit(solution)/shard_map/pallas_call | solution.py:36
  70.8 26.3 %all_to_all.30 = bf16[8,256,128]{2,1,0:T(8,128)(2,1)S(1)} all-to-all(bf16[8,256,128]{2,1,0:T(8,128)(2,1)S(1)} %shard_map.61), channel_id=1, replica_groups=mesh['x'=4,'y'=8,'c'=2,'z'=8] {'z'}, dimensions={0} | all-to-all | bytes 1048576 | tf_op jit(solution)/shard_map/all_to_all | solution.py:21
  97.1 0.1 convert_reduce_fusion.1
  97.2 0.1 copy.9
  97.3 0.8 broadcast_in_dim.9
  98.2 3.5 %all-to-all-start.2 = ((bf16[8,256,128]{1,2,0:T(8,128)(2,1)}), bf16[8,256,128]{1,2,0:T(8,128)(2,1)S(1)}, u32[]{:S(2)}, u32[]{:S(2)}) async-start(bf16[8,256,128]{1,2,0:T(8,128)(2,1)} %broadcast_in_dim.9), calls=%async_computation.2 | async-start | bytes 1048576 | tf_op jit(solution)/shard_map/all_to_all | solution.py:21
  101.7 15.8 %all-to-all-done.2 = bf16[8,256,128]{1,2,0:T(8,128)(2,1)S(1)} async-done(((bf16[8,256,128]{1,2,0:T(8,128)(2,1)}), bf16[8,256,128]{1,2,0:T(8,128)(2,1)S(1)}, u32[]{:S(2)}, u32[]{:S(2)}) %all-to-all-start.2) | async-done | bytes 524320 | tf_op jit(solution)/shard_map/all_to_all | solution.py:21
  117.5 0.8 convolution_convert_fusion
  118.3 4.3 %all-gather = bf16[1792,128]{0,1:T(8,128)(2,1)S(1)} all-gather(bf16[896,128]{0,1:T(8,128)(2,1)S(1)} %dynamic-slice_bitcast_fusion), channel_id=2, replica_groups=mesh['x'=4,'y'=8,'c'=2,'z'=8] {'c'}, dimensions={0}, use_global_device_ids=true | all-gather | bytes 688128 | tf_op jit(solution)/shard_map/all_gather | solution.py:197
  122.6 0.1 reshape.36
  122.7 0.5 constant_dynamic-slice_fusion
  123.2 0.1 fusion
  123.2 0.2 copy.11
  123.5 15.6 %all_to_all.31 = bf16[32,28,128]{2,1,0:T(8,128)(2,1)S(1)} all-to-all(bf16[32,28,128]{2,1,0:T(8,128)(2,1)S(1)} %reshape.33), channel_id=1, replica_groups=mesh['x'=4,'y'=8,'c'=2,'z'=8] {'x','y'}, dimensions={0} | all-to-all | bytes 458752 | tf_op jit(solution)/shard_map/all_to_all | solution.py:21
  139.1 0.1 reduce_sum.31
  139.2 16.2 %all_to_all.32 = bf16[32,28,128]{2,1,0:T(8,128)(2,1)S(1)} all-to-all(bf16[32,28,128]{2,1,0:T(8,128)(2,1)S(1)} %broadcast_in_dim.20), channel_id=1, replica_groups=mesh['x'=4,'y'=8,'c'=2,'z'=8] {'x','y'}, dimensions={0} | all-to-all | bytes 458752 | tf_op jit(solution)/shard_map/all_to_all | solution.py:21
  155.4 5.4 %all_gather.11.basis_ref = bf16[896,256]{1,0:T(8,128)(2,1)S(1)} all-gather(bf16[896,128]{1,0:T(8,128)(2,1)S(1)} %reshape.34), channel_id=1, replica_groups=mesh['x'=4,'y'=8,'c'=2,'z'=8] {'c'}, dimensions={1}, use_global_device_ids=true | all-gather | bytes 688128 | tf_op jit(solution)/shard_map/all_gather | solution.py:202
  160.7 1.5 shard_map.62
  162.3 3.5 %all-to-all-start.5 = ((bf16[8,256,128]{2,1,0:T(8,128)(2,1)}), bf16[8,256,128]{2,1,0:T(8,128)(2,1)S(1)}, u32[]{:S(2)}, u32[]{:S(2)}) async-start(bf16[8,256,128]{2,1,0:T(8,128)(2,1)} %shard_map.62), calls=%async_computation.5 | async-start | bytes 1048576 | tf_op jit(solution)/shard_map/all_to_all | solution.py:21
  165.8 0.6 dynamic-slice_convert_fusion
  166.4 17.3 %all-to-all-done.5 = bf16[8,256,128]{2,1,0:T(8,128)(2,1)S(1)} async-done(((bf16[8,256,128]{2,1,0:T(8,128)(2,1)}), bf16[8,256,128]{2,1,0:T(8,128)(2,1)S(1)}, u32[]{:S(2)}, u32[]{:S(2)}) %all-to-all-start.5) | async-done | bytes 524320 | tf_op jit(solution)/shard_map/all_to_all | solution.py:21
  183.7 0.7 convert_reduce_fusion
  (6 shorter events, 0.2 us)
Async XLA Ops:
  4.6 12.0 %copy-start = (bf16[1,896,1024]{2,1,0:T(8,128)(2,1)S(1)}, bf16[1,896,1024]{2,1,0:T(8,128)(2,1)}, u32[]{:S(2)}) copy-start(bf16[1,896,1024]{2,1,0:T(8,128)(2,1)} %param.6) | copy-start | bytes 5505028
  4.7 12.0 %copy-start.1 = (bf16[896,256]{1,0:T(8,128)(2,1)S(1)}, bf16[896,256]{1,0:T(8,128)(2,1)}, u32[]{:S(2)}) copy-start(bf16[896,256]{1,0:T(8,128)(2,1)} %probe_ref.1) | copy-start | bytes 1376260
  4.7 63.2 %all-to-all-start = ((bf16[64,16,1024]{2,1,0:T(8,128)(2,1)}), bf16[64,16,1024]{2,1,0:T(8,128)(2,1)}, u32[]{:S(2)}, u32[]{:S(2)}) async-start(bf16[64,16,1024]{2,1,0:T(8,128)(2,1)} %bitcast.32), calls=%async_computation | async-start | bytes 4194304 | tf_op jit(solution)/shard_map/all_to_all | solution.py:21
  17.5 11.7 %collective-permute-start.2 = (bf16[256,256]{1,0:T(8,128)(2,1)S(1)}, bf16[256,256]{1,0:T(8,128)(2,1)S(1)}, u32[]{:S(2)}, u32[]{:S(2)}) collective-permute-start(bf16[256,256]{1,0:T(8,128)(2,1)S(1)} %get-tuple-element.7), channel_id=1, source_target_pairs={{0,1},{1,0},{2,3},{3,2},{4,5},{5,4},{6,7},{7,6},{8,9},{9,8},{10,11... | collective-permute-start | bytes 393224 | tf_op jit(solution)/shard_map/ppermute | solution.py:145
  21.5 12.2 %collective-permute-start.1 = (bf16[256,256]{1,0:T(8,128)(2,1)S(1)}, bf16[256,256]{1,0:T(8,128)(2,1)S(1)}, u32[]{:S(2)}, u32[]{:S(2)}) collective-permute-start(bf16[256,256]{1,0:T(8,128)(2,1)S(1)} %get-tuple-element.8), channel_id=1, source_target_pairs={{0,2},{1,3},{2,0},{3,1},{4,6},{5,7},{6,4},{7,5},{8,10},{9,11},{10,... | collective-permute-start | bytes 393224 | tf_op jit(solution)/shard_map/ppermute | solution.py:145
  27.3 7.8 %collective-permute-start = (bf16[256,256]{1,0:T(8,128)(2,1)S(1)}, bf16[256,256]{1,0:T(8,128)(2,1)S(1)}, u32[]{:S(2)}, u32[]{:S(2)}) collective-permute-start(bf16[256,256]{1,0:T(8,128)(2,1)S(1)} %get-tuple-element.6), channel_id=1, source_target_pairs={{0,3},{1,2},{2,1},{3,0},{4,7},{5,6},{6,5},{7,4},{8,11},{9,10},{10,... | collective-permute-start | bytes 393224 | tf_op jit(solution)/shard_map/ppermute | solution.py:145
  35.2 10.5 %collective-permute-start.3 = (bf16[256,256]{1,0:T(8,128)(2,1)S(1)}, bf16[256,256]{1,0:T(8,128)(2,1)S(1)}, u32[]{:S(2)}, u32[]{:S(2)}) collective-permute-start(bf16[256,256]{1,0:T(8,128)(2,1)S(1)} %fusion.1), channel_id=1, source_target_pairs={{0,4},{1,5},{2,6},{3,7},{4,0},{5,1},{6,2},{7,3},{8,12},{9,13},{10,... | collective-permute-start | bytes 393224 | tf_op jit(solution)/shard_map/ppermute | solution.py:145
  45.8 14.0 %collective-permute-start.4 = (bf16[256,256]{1,0:T(8,128)(2,1)S(1)}, bf16[256,256]{1,0:T(8,128)(2,1)S(1)}, u32[]{:S(2)}, u32[]{:S(2)}) collective-permute-start(bf16[256,256]{1,0:T(8,128)(2,1)S(1)} %add_convert_fusion.proj0), channel_id=1, source_target_pairs={{0,1},{1,0},{2,3},{3,2},{4,5},{5,4},{6,7},{7,6},{8,9},{9,8},{10,11... | collective-permute-start | bytes 393224 | tf_op jit(solution)/shard_map/ppermute | solution.py:145
  53.9 11.1 %collective-permute-start.5 = (bf16[256,256]{1,0:T(8,128)(2,1)S(1)}, bf16[256,256]{1,0:T(8,128)(2,1)S(1)}, u32[]{:S(2)}, u32[]{:S(2)}) collective-permute-start(bf16[256,256]{1,0:T(8,128)(2,1)S(1)} %add_convert_fusion.proj0), channel_id=1, source_target_pairs={{0,2},{1,3},{2,0},{3,1},{4,6},{5,7},{6,4},{7,5},{8,10},{9,11},{10,... | collective-permute-start | bytes 393224 | tf_op jit(solution)/shard_map/ppermute | solution.py:145
  56.3 8.7 %collective-permute-start.6 = (bf16[256,256]{1,0:T(8,128)(2,1)S(1)}, bf16[256,256]{1,0:T(8,128)(2,1)S(1)}, u32[]{:S(2)}, u32[]{:S(2)}) collective-permute-start(bf16[256,256]{1,0:T(8,128)(2,1)S(1)} %add_convert_fusion.proj0), channel_id=1, source_target_pairs={{0,3},{1,2},{2,1},{3,0},{4,7},{5,6},{6,5},{7,4},{8,11},{9,10},{10,... | collective-permute-start | bytes 393224 | tf_op jit(solution)/shard_map/ppermute | solution.py:145
  98.2 19.3 %all-to-all-start.2 = ((bf16[8,256,128]{1,2,0:T(8,128)(2,1)}), bf16[8,256,128]{1,2,0:T(8,128)(2,1)S(1)}, u32[]{:S(2)}, u32[]{:S(2)}) async-start(bf16[8,256,128]{1,2,0:T(8,128)(2,1)} %broadcast_in_dim.9), calls=%async_computation.2 | async-start | bytes 1048576 | tf_op jit(solution)/shard_map/all_to_all | solution.py:21
  162.3 21.4 %all-to-all-start.5 = ((bf16[8,256,128]{2,1,0:T(8,128)(2,1)}), bf16[8,256,128]{2,1,0:T(8,128)(2,1)S(1)}, u32[]{:S(2)}, u32[]{:S(2)}) async-start(bf16[8,256,128]{2,1,0:T(8,128)(2,1)} %shard_map.62), calls=%async_computation.5 | async-start | bytes 1048576 | tf_op jit(solution)/shard_map/all_to_all | solution.py:21

commit v3 on v2

--- a/solution.py
+++ b/solution.py
@@ -45,11 +45,13 @@
     return out[0] if len(outs) == 1 else out
 
 
-def dispatch_kernel(capacity, routes_ref, rows_hbm, out_hbm, rows_ref, out_ref, in_sem, out_sem):
+def dispatch_kernel(capacity, routes_hbm, rows_hbm, out_hbm, routes_ref, rows_ref, out_ref, in_sem, out_sem):
     top, tokens = routes_ref.shape
     count = tokens * top
     experts = out_ref.shape[0] // capacity
-    fetch = pltpu.make_async_copy(rows_hbm, rows_ref, in_sem)
+    names = pltpu.make_async_copy(routes_hbm, routes_ref, in_sem.at[0])
+    names.start()
+    fetch = pltpu.make_async_copy(rows_hbm, rows_ref, in_sem.at[1])
     fetch.start()
 
     def iota(dims, axis):
@@ -60,11 +62,12 @@
 
     spread = flag(iota((top, count), 0) == iota((top, count), 1) % top)
     token = flag(iota((tokens, count), 0) == iota((tokens, count), 1) // top)
-    names = contract(routes_ref[...].astype(F32).astype(BF16), spread, 0, 0)
-    expert = jnp.sum(names * token.astype(F32), axis=0, keepdims=True).astype(jnp.int32)
+    earlier = flag(iota((tokens, tokens), 0) < iota((tokens, tokens), 1))
+    names.wait()
+    spelled = contract(routes_ref[...].astype(F32).astype(BF16), spread, 0, 0)
+    expert = jnp.sum(spelled * token.astype(F32), axis=0, keepdims=True).astype(jnp.int32)
     named = flag(iota((experts, count), 0) == expert)
     by_token = contract(named, token, 1, 1).astype(BF16)
-    earlier = flag(iota((tokens, tokens), 0) < iota((tokens, tokens), 1))
     before = jnp.dot(by_token, earlier, preferred_element_type=F32).astype(BF16)
     position = jnp.sum(jnp.dot(before, token, preferred_element_type=F32) * named.astype(F32), axis=0, keepdims=True)
     slot = expert * capacity + position.astype(jnp.int32)
@@ -116,14 +119,33 @@
             out_ref[(i + j) // size] = part[:, j : j + size]
 
 
-def coef_kernel(basis_ref, weight_ref, out_ref):
-    block = 256
-    size = out_ref.shape[2]
-    turned = basis_ref[...].T
-    for i in range(0, weight_ref.shape[1], block):
-        part = jnp.dot(turned, weight_ref[:, i : i + block], preferred_element_type=F32).astype(BF16)
-        for j in range(0, block, size):
-            out_ref[(i + j) // size] = part[:, j : j + size]
+def share_kernel(scale, parts_ref, out_ref):
+    total = jnp.sum(parts_ref[...].astype(F32), axis=0) * scale
+    value = total.astype(BF16).T
+    for i in range(out_ref.shape[0]):
+        out_ref[i] = value
+
+
+def image_kernel(core_ref, weight_ref, gram_ref, kept_ref, given_ref):
+    half = kept_ref.shape[1]
+    image = jnp.dot(weight_ref[...], gram_ref[...], preferred_element_type=F32)
+    left, right = image[:, :half], image[:, half:]
+    first = core_ref[0] == 0
+    kept_ref[...] = jnp.where(first, left, right)
+    given_ref[...] = jnp.where(first, right, left).astype(BF16)
+
+
+def coef_kernel(weight_ref, basis_ref, out_ref):
+    size = out_ref.shape[1]
+    basis = basis_ref[...]
+    for i in range(0, weight_ref.shape[1], 2 * size):
+        part = contract(weight_ref[:, i : i + 2 * size], basis, 0, 0).astype(BF16)
+        out_ref[i // size] = part[:size]
+        out_ref[i // size + 1] = part[size:]
+
+
+def total_kernel(parts_ref, out_ref):
+    out_ref[...] = jnp.sum(parts_ref[...].astype(F32), axis=0).T
 
 
 def body(hidden_rows, routes, down_weight, probe):
@@ -153,12 +175,13 @@
         [shape((slots, width), BF16)],
         2 * slots * count * width,
         [routes.T, hidden_rows.reshape(count, width)],
-        [VMEM, HBM],
+        [HBM, HBM],
         [HBM],
         [
+            pltpu.VMEM((top, tokens), jnp.int32),
             pltpu.VMEM((count, width), BF16),
             pltpu.VMEM((slots, width), BF16),
-            pltpu.SemaphoreType.DMA,
+            pltpu.SemaphoreType.DMA((2,)),
             pltpu.SemaphoreType.DMA((slots // 256,)),
         ],
         WIDE_BYTES,
@@ -187,15 +210,22 @@
         None,
         [pltpu.VMEM((width, panel), BF16)],
     )
-    gram_own = jnp.sum(swap(gram_part, "z").astype(F32), axis=0) / row_mean
-    gram = swap(jnp.broadcast_to(gram_own.astype(BF16)[None], gram_part.shape), "z")
-    gram = gram.transpose(1, 0, 2).reshape(panel, width)
-
-    image = contract(weight, gram, 1, 1).astype(BF16)
-    kept = lax.dynamic_slice_in_dim(image, core * half, half, 1)
-    given = lax.dynamic_slice_in_dim(image, (1 - core) * half, half, 1)
-    came = lax.dynamic_index_in_dim(lax.all_gather(given, "c"), 1 - core, 0, False)
-    chip_sum = kept.astype(F32) + came.astype(F32)
+    copies = call(
+        functools.partial(share_kernel, 1.0 / row_mean),
+        [shape((nz, block, panel), BF16)],
+        nz * block * panel,
+        [swap(gram_part, "z")],
+    )
+    gram = swap(copies, "z").reshape(width, panel)
+
+    kept, given = call(
+        image_kernel,
+        [shape((depth, half), F32), shape((depth, half), BF16)],
+        2 * depth * width * panel,
+        [core[None], weight, gram],
+        [SMEM, VMEM, VMEM],
+    )
+    chip_sum = kept + lax.dynamic_index_in_dim(lax.all_gather(given, "c"), 1 - core, 0, False).astype(F32)
     pieces = swap(chip_sum.astype(BF16).reshape(chips, depth // chips, half), ("x", "y"))
     own = jnp.sum(pieces.astype(F32), axis=0).astype(BF16)
     basis_half = share(own, ("x", "y"), chips)
@@ -204,8 +234,8 @@
     rows_own = depth // experts
     place = (lax.axis_index("x") * ny + lax.axis_index("y")) * nc + core
     basis_rows = lax.dynamic_slice_in_dim(basis, place * rows_own, rows_own, 0).astype(F32)
-    coef_part = call(coef_kernel, [shape((nz, panel, block), BF16)], 2 * depth * width * panel, [basis, weight])
-    coefficients = jnp.sum(swap(coef_part, "z").astype(F32), axis=0)
+    coef_part = call(coef_kernel, [shape((nz, block, panel), BF16)], 2 * depth * width * panel, [weight, basis])
+    coefficients = call(total_kernel, [shape((panel, block), F32)], nz * block * panel, [swap(coef_part, "z")])
     return basis_rows, coefficients[None]
 
 

time: 185 us -> 184 us (level)
    pallas_call x4 -> x7, Pallas kernels: 9.23 us -> 11 us  [call(): pl.pallas_call(kernel, out_shape=outs, in_specs=in_specs or [VMEM] * len(...]
where the time goes in v3:
time: 184 us; the launch traced here: 183 us
  blocking collectives  67.8 us (37%)
  starting transfers between devices  52.7 us (29%)
  waiting for transfers between devices  49.5 us (27%)
  Pallas kernels  11 us (6%)
    all_to_all x3, blocking collectives, swap(): return lax.all_to_all(value, axes, split_axis=0, concat_axis=0, tiled=False)  58.1 us
    all_to_all x3, waiting for transfers between devices, swap(): return lax.all_to_all(value, axes, split_axis=0, concat_axis=0, tiled=False)  36 us
    ppermute x7, starting transfers between devices, across(): return lax.ppermute(value, axis, [(i, i ^ step) for i in range(size)])  33.8 us
    all_to_all x3, starting transfers between devices, swap(): return lax.all_to_all(value, axes, split_axis=0, concat_axis=0, tiled=False)  18.9 us
    ppermute x7, waiting for transfers between devices, across(): return lax.ppermute(value, axis, [(i, i ^ step) for i in range(size)])  13.6 us
    pallas_call x7, Pallas kernels, call(): pl.pallas_call(kernel, out_shape=outs, in_specs=in_specs or [VMEM] * len(...  11 us
    all_gather x1, blocking collectives, body(): basis = lax.all_gather(basis_half, 'c', axis=1, tiled=True)  5.35 us
    all_gather x1, blocking collectives, body(): lax.all_gather(given, 'c')  4.31 us
  transfers between devices with their start and end apart: 10, of which 7 were waited for; matrix products, arithmetic and copies ran while one was open for 0% of the time, Pallas kernels for 0%

profile of v3, /device:TPU:1, one launch (start us, length us, event | category | flops | bytes accessed | tf_op | source)
XLA Modules:
  0.0 183.0 jit_solution(5717425955780572824)
XLA Ops:
  0.6 3.4 %shard_map.59 = bf16[1024,1024]{1,0:T(8,128)(2,1)} custom-call(s32[8,64]{1,0:T(8,128)} %bitcast.27, bf16[512,1024]{1,0:T(8,128)(2,1)} %bitcast.26), custom_call_target="tpu_custom_call" | custom-call | flops 1073741824 | bytes 3147776 | tf_op jit(solution)/shard_map/pallas_call | solution.py:36
  4.0 0.0 copy-start
  4.1 0.0 copy-start.1
  4.1 12.0 %all-to-all-start = ((bf16[64,16,1024]{2,1,0:T(8,128)(2,1)}), bf16[64,16,1024]{2,1,0:T(8,128)(2,1)}, u32[]{:S(2)}, u32[]{:S(2)}) async-start(bf16[64,16,1024]{2,1,0:T(8,128)(2,1)} %bitcast.23), calls=%async_computation | async-start | bytes 4194304 | tf_op jit(solution)/shard_map/all_to_all | solution.py:21
  16.0 0.0 copy-done
  16.1 0.0 copy-done.1
  16.1 0.8 shard_map.60
  16.9 4.0 %collective-permute-start.2 = (bf16[256,256]{1,0:T(8,128)(2,1)S(1)}, bf16[256,256]{1,0:T(8,128)(2,1)S(1)}, u32[]{:S(2)}, u32[]{:S(2)}) collective-permute-start(bf16[256,256]{1,0:T(8,128)(2,1)S(1)} %get-tuple-element.11), channel_id=1, source_target_pairs={{0,1},{1,0},{2,3},{3,2},{4,5},{5,4},{6,7},{7,6},{8,9},{9,8},{10,11... | collective-permute-start | bytes 393224 | tf_op jit(solution)/shard_map/ppermute | solution.py:167
  20.9 5.8 %collective-permute-start.1 = (bf16[256,256]{1,0:T(8,128)(2,1)S(1)}, bf16[256,256]{1,0:T(8,128)(2,1)S(1)}, u32[]{:S(2)}, u32[]{:S(2)}) collective-permute-start(bf16[256,256]{1,0:T(8,128)(2,1)S(1)} %get-tuple-element.12), channel_id=1, source_target_pairs={{0,2},{1,3},{2,0},{3,1},{4,6},{5,7},{6,4},{7,5},{8,10},{9,11},{10,... | collective-permute-start | bytes 393224 | tf_op jit(solution)/shard_map/ppermute | solution.py:167
  26.7 1.9 %collective-permute-start = (bf16[256,256]{1,0:T(8,128)(2,1)S(1)}, bf16[256,256]{1,0:T(8,128)(2,1)S(1)}, u32[]{:S(2)}, u32[]{:S(2)}) collective-permute-start(bf16[256,256]{1,0:T(8,128)(2,1)S(1)} %get-tuple-element.10), channel_id=1, source_target_pairs={{0,3},{1,2},{2,1},{3,0},{4,7},{5,6},{6,5},{7,4},{8,11},{9,10},{10,... | collective-permute-start | bytes 393224 | tf_op jit(solution)/shard_map/ppermute | solution.py:167
  28.6 0.0 collective-permute-done.2
  28.6 4.5 %collective-permute-done.1 = bf16[256,256]{1,0:T(8,128)(2,1)S(1)} collective-permute-done((bf16[256,256]{1,0:T(8,128)(2,1)S(1)}, bf16[256,256]{1,0:T(8,128)(2,1)S(1)}, u32[]{:S(2)}, u32[]{:S(2)}) %collective-permute-start.1) | collective-permute-done | bytes 131104 | tf_op jit(solution)/shard_map/ppermute | solution.py:167
  33.1 1.4 collective-permute-done
  34.5 0.1 fusion.1
  34.6 8.1 %collective-permute-start.3 = (bf16[256,256]{1,0:T(8,128)(2,1)S(1)}, bf16[256,256]{1,0:T(8,128)(2,1)S(1)}, u32[]{:S(2)}, u32[]{:S(2)}) collective-permute-start(bf16[256,256]{1,0:T(8,128)(2,1)S(1)} %fusion.1), channel_id=1, source_target_pairs={{0,4},{1,5},{2,6},{3,7},{4,0},{5,1},{6,2},{7,3},{8,12},{9,13},{10,... | collective-permute-start | bytes 393224 | tf_op jit(solution)/shard_map/ppermute | solution.py:167
  42.7 2.4 %collective-permute-done.3 = bf16[256,256]{1,0:T(8,128)(2,1)S(1)} collective-permute-done((bf16[256,256]{1,0:T(8,128)(2,1)S(1)}, bf16[256,256]{1,0:T(8,128)(2,1)S(1)}, u32[]{:S(2)}, u32[]{:S(2)}) %collective-permute-start.3) | collective-permute-done | bytes 131104 | tf_op jit(solution)/shard_map/ppermute | solution.py:167
  45.1 0.1 add_convert_fusion.proj0
  45.2 8.1 %collective-permute-start.4 = (bf16[256,256]{1,0:T(8,128)(2,1)S(1)}, bf16[256,256]{1,0:T(8,128)(2,1)S(1)}, u32[]{:S(2)}, u32[]{:S(2)}) collective-permute-start(bf16[256,256]{1,0:T(8,128)(2,1)S(1)} %add_convert_fusion.proj0), channel_id=1, source_target_pairs={{0,1},{1,0},{2,3},{3,2},{4,5},{5,4},{6,7},{7,6},{8,9},{9,8},{10,11... | collective-permute-start | bytes 393224 | tf_op jit(solution)/shard_map/ppermute | solution.py:167
  53.3 2.4 %collective-permute-start.5 = (bf16[256,256]{1,0:T(8,128)(2,1)S(1)}, bf16[256,256]{1,0:T(8,128)(2,1)S(1)}, u32[]{:S(2)}, u32[]{:S(2)}) collective-permute-start(bf16[256,256]{1,0:T(8,128)(2,1)S(1)} %add_convert_fusion.proj0), channel_id=1, source_target_pairs={{0,2},{1,3},{2,0},{3,1},{4,6},{5,7},{6,4},{7,5},{8,10},{9,11},{10,... | collective-permute-start | bytes 393224 | tf_op jit(solution)/shard_map/ppermute | solution.py:167
  55.7 3.5 %collective-permute-start.6 = (bf16[256,256]{1,0:T(8,128)(2,1)S(1)}, bf16[256,256]{1,0:T(8,128)(2,1)S(1)}, u32[]{:S(2)}, u32[]{:S(2)}) collective-permute-start(bf16[256,256]{1,0:T(8,128)(2,1)S(1)} %add_convert_fusion.proj0), channel_id=1, source_target_pairs={{0,3},{1,2},{2,1},{3,0},{4,7},{5,6},{6,5},{7,4},{8,11},{9,10},{10,... | collective-permute-start | bytes 393224 | tf_op jit(solution)/shard_map/ppermute | solution.py:167
  59.2 0.0 collective-permute-done.4.proj1
  59.2 5.2 %collective-permute-done.5.proj2 = bf16[256,256]{1,0:T(8,128)(2,1)S(1)} collective-permute-done((bf16[256,256]{1,0:T(8,128)(2,1)S(1)}, bf16[256,256]{1,0:T(8,128)(2,1)S(1)}, u32[]{:S(2)}, u32[]{:S(2)}) %collective-permute-start.5) | collective-permute-done | bytes 131104 | tf_op jit(solution)/shard_map/ppermute | solution.py:167
  64.4 0.0 collective-permute-done.6.proj3
  64.4 2.9 %all-to-all-done = bf16[64,16,1024]{2,1,0:T(8,128)(2,1)} async-done(((bf16[64,16,1024]{2,1,0:T(8,128)(2,1)}), bf16[64,16,1024]{2,1,0:T(8,128)(2,1)}, u32[]{:S(2)}, u32[]{:S(2)}) %all-to-all-start) | async-done | bytes 2097184 | tf_op jit(solution)/shard_map/all_to_all | solution.py:21
  67.3 2.9 %shard_map.61 = bf16[8,256,128]{2,1,0:T(8,128)(2,1)S(1)} custom-call(s32[1]{0:T(128)} %bitcast.2.quarter_ref, bf16[1024,1024]{1,0:T(8,128)(2,1)} %bitcast.6.rows_ref, bf16[256,256]{1,0:T(8,128)(2,1)S(1)} %add_convert_fusion.proj0, bf16[256,256]{1,0:T(8,128)(2,1)S(1)} %collective-permute-done.4.proj1, bf16[256,256]{1,0:T(8,128)(2,1)S(1)} %collective-permute-done.5.proj2, ...), custom_call_target="tpu_custom_call" | custom-call | flops 1073741824 | bytes 3145732 | tf_op jit(solution)/shard_map/pallas_call | solution.py:36
  70.2 26.3 %all_to_all.30.parts_ref = bf16[8,256,128]{2,1,0:T(8,128)(2,1)S(1)} all-to-all(bf16[8,256,128]{2,1,0:T(8,128)(2,1)S(1)} %shard_map.61), channel_id=1, replica_groups=mesh['x'=4,'y'=8,'c'=2,'z'=8] {'z'}, dimensions={0} | all-to-all | bytes 1048576 | tf_op jit(solution)/shard_map/all_to_all | solution.py:21
  96.5 0.9 shard_map.62
  97.5 3.5 %all-to-all-start.2 = ((bf16[8,128,256]{2,1,0:T(8,128)(2,1)}), bf16[8,128,256]{2,1,0:T(8,128)(2,1)S(1)}, u32[]{:S(2)}, u32[]{:S(2)}) async-start(bf16[8,128,256]{2,1,0:T(8,128)(2,1)} %shard_map.62), calls=%async_computation.2 | async-start | bytes 1048576 | tf_op jit(solution)/shard_map/all_to_all | solution.py:21
  101.0 15.8 %all-to-all-done.2 = bf16[8,128,256]{2,1,0:T(8,128)(2,1)S(1)} async-done(((bf16[8,128,256]{2,1,0:T(8,128)(2,1)}), bf16[8,128,256]{2,1,0:T(8,128)(2,1)S(1)}, u32[]{:S(2)}, u32[]{:S(2)}) %all-to-all-start.2) | async-done | bytes 524320 | tf_op jit(solution)/shard_map/all_to_all | solution.py:21
  116.8 0.6 shard_map.63
  117.4 4.3 %all-gather = bf16[1792,128]{1,0:T(8,128)(2,1)S(1)} all-gather(bf16[896,128]{1,0:T(8,128)(2,1)S(1)} %get-tuple-element.9), channel_id=2, replica_groups=mesh['x'=4,'y'=8,'c'=2,'z'=8] {'c'}, dimensions={0}, use_global_device_ids=true | all-gather | bytes 688128 | tf_op jit(solution)/shard_map/all_gather | solution.py:228
  121.7 0.1 fusion
  121.9 15.6 %all_to_all.31 = bf16[32,28,128]{2,1,0:T(8,128)(2,1)S(1)} all-to-all(bf16[32,28,128]{2,1,0:T(8,128)(2,1)S(1)} %reshape.29), channel_id=1, replica_groups=mesh['x'=4,'y'=8,'c'=2,'z'=8] {'x','y'}, dimensions={0} | all-to-all | bytes 458752 | tf_op jit(solution)/shard_map/all_to_all | solution.py:21
  137.5 0.1 reduce_sum.12
  137.6 16.2 %all_to_all.32 = bf16[32,28,128]{2,1,0:T(8,128)(2,1)S(1)} all-to-all(bf16[32,28,128]{2,1,0:T(8,128)(2,1)S(1)} %broadcast_in_dim.17), channel_id=1, replica_groups=mesh['x'=4,'y'=8,'c'=2,'z'=8] {'x','y'}, dimensions={0} | all-to-all | bytes 458752 | tf_op jit(solution)/shard_map/all_to_all | solution.py:21
  153.8 5.4 %all_gather.11.basis_ref = bf16[896,256]{1,0:T(8,128)(2,1)S(1)} all-gather(bf16[896,128]{1,0:T(8,128)(2,1)S(1)} %reshape.30), channel_id=1, replica_groups=mesh['x'=4,'y'=8,'c'=2,'z'=8] {'c'}, dimensions={1}, use_global_device_ids=true | all-gather | bytes 688128 | tf_op jit(solution)/shard_map/all_gather | solution.py:232
  159.2 1.6 shard_map.64
  160.7 3.5 %all-to-all-start.5 = ((bf16[8,128,256]{2,1,0:T(8,128)(2,1)}), bf16[8,128,256]{2,1,0:T(8,128)(2,1)S(1)}, u32[]{:S(2)}, u32[]{:S(2)}) async-start(bf16[8,128,256]{2,1,0:T(8,128)(2,1)} %shard_map.64), calls=%async_computation.5 | async-start | bytes 1048576 | tf_op jit(solution)/shard_map/all_to_all | solution.py:21
  164.2 0.6 dynamic-slice_convert_fusion
  164.9 17.3 %all-to-all-done.5.parts_ref = bf16[8,128,256]{2,1,0:T(8,128)(2,1)S(1)} async-done(((bf16[8,128,256]{2,1,0:T(8,128)(2,1)}), bf16[8,128,256]{2,1,0:T(8,128)(2,1)S(1)}, u32[]{:S(2)}, u32[]{:S(2)}) %all-to-all-start.5) | async-done | bytes 524320 | tf_op jit(solution)/shard_map/all_to_all | solution.py:21
  182.2 0.8 shard_map.65
  (4 shorter events, 0.2 us)
Async XLA Ops:
  4.0 12.0 %copy-start = (bf16[1,896,1024]{2,1,0:T(8,128)(2,1)S(1)}, bf16[1,896,1024]{2,1,0:T(8,128)(2,1)}, u32[]{:S(2)}) copy-start(bf16[1,896,1024]{2,1,0:T(8,128)(2,1)} %param.6) | copy-start | bytes 5505028
  4.1 12.0 %copy-start.1 = (bf16[896,256]{1,0:T(8,128)(2,1)S(1)}, bf16[896,256]{1,0:T(8,128)(2,1)}, u32[]{:S(2)}) copy-start(bf16[896,256]{1,0:T(8,128)(2,1)} %probe_ref.1) | copy-start | bytes 1376260
  4.1 63.2 %all-to-all-start = ((bf16[64,16,1024]{2,1,0:T(8,128)(2,1)}), bf16[64,16,1024]{2,1,0:T(8,128)(2,1)}, u32[]{:S(2)}, u32[]{:S(2)}) async-start(bf16[64,16,1024]{2,1,0:T(8,128)(2,1)} %bitcast.23), calls=%async_computation | async-start | bytes 4194304 | tf_op jit(solution)/shard_map/all_to_all | solution.py:21
  16.9 11.7 %collective-permute-start.2 = (bf16[256,256]{1,0:T(8,128)(2,1)S(1)}, bf16[256,256]{1,0:T(8,128)(2,1)S(1)}, u32[]{:S(2)}, u32[]{:S(2)}) collective-permute-start(bf16[256,256]{1,0:T(8,128)(2,1)S(1)} %get-tuple-element.11), channel_id=1, source_target_pairs={{0,1},{1,0},{2,3},{3,2},{4,5},{5,4},{6,7},{7,6},{8,9},{9,8},{10,11... | collective-permute-start | bytes 393224 | tf_op jit(solution)/shard_map/ppermute | solution.py:167
  20.9 12.3 %collective-permute-start.1 = (bf16[256,256]{1,0:T(8,128)(2,1)S(1)}, bf16[256,256]{1,0:T(8,128)(2,1)S(1)}, u32[]{:S(2)}, u32[]{:S(2)}) collective-permute-start(bf16[256,256]{1,0:T(8,128)(2,1)S(1)} %get-tuple-element.12), channel_id=1, source_target_pairs={{0,2},{1,3},{2,0},{3,1},{4,6},{5,7},{6,4},{7,5},{8,10},{9,11},{10,... | collective-permute-start | bytes 393224 | tf_op jit(solution)/shard_map/ppermute | solution.py:167
  26.7 7.8 %collective-permute-start = (bf16[256,256]{1,0:T(8,128)(2,1)S(1)}, bf16[256,256]{1,0:T(8,128)(2,1)S(1)}, u32[]{:S(2)}, u32[]{:S(2)}) collective-permute-start(bf16[256,256]{1,0:T(8,128)(2,1)S(1)} %get-tuple-element.10), channel_id=1, source_target_pairs={{0,3},{1,2},{2,1},{3,0},{4,7},{5,6},{6,5},{7,4},{8,11},{9,10},{10,... | collective-permute-start | bytes 393224 | tf_op jit(solution)/shard_map/ppermute | solution.py:167
  34.6 10.5 %collective-permute-start.3 = (bf16[256,256]{1,0:T(8,128)(2,1)S(1)}, bf16[256,256]{1,0:T(8,128)(2,1)S(1)}, u32[]{:S(2)}, u32[]{:S(2)}) collective-permute-start(bf16[256,256]{1,0:T(8,128)(2,1)S(1)} %fusion.1), channel_id=1, source_target_pairs={{0,4},{1,5},{2,6},{3,7},{4,0},{5,1},{6,2},{7,3},{8,12},{9,13},{10,... | collective-permute-start | bytes 393224 | tf_op jit(solution)/shard_map/ppermute | solution.py:167
  45.2 14.0 %collective-permute-start.4 = (bf16[256,256]{1,0:T(8,128)(2,1)S(1)}, bf16[256,256]{1,0:T(8,128)(2,1)S(1)}, u32[]{:S(2)}, u32[]{:S(2)}) collective-permute-start(bf16[256,256]{1,0:T(8,128)(2,1)S(1)} %add_convert_fusion.proj0), channel_id=1, source_target_pairs={{0,1},{1,0},{2,3},{3,2},{4,5},{5,4},{6,7},{7,6},{8,9},{9,8},{10,11... | collective-permute-start | bytes 393224 | tf_op jit(solution)/shard_map/ppermute | solution.py:167
  53.3 11.1 %collective-permute-start.5 = (bf16[256,256]{1,0:T(8,128)(2,1)S(1)}, bf16[256,256]{1,0:T(8,128)(2,1)S(1)}, u32[]{:S(2)}, u32[]{:S(2)}) collective-permute-start(bf16[256,256]{1,0:T(8,128)(2,1)S(1)} %add_convert_fusion.proj0), channel_id=1, source_target_pairs={{0,2},{1,3},{2,0},{3,1},{4,6},{5,7},{6,4},{7,5},{8,10},{9,11},{10,... | collective-permute-start | bytes 393224 | tf_op jit(solution)/shard_map/ppermute | solution.py:167
  55.7 8.7 %collective-permute-start.6 = (bf16[256,256]{1,0:T(8,128)(2,1)S(1)}, bf16[256,256]{1,0:T(8,128)(2,1)S(1)}, u32[]{:S(2)}, u32[]{:S(2)}) collective-permute-start(bf16[256,256]{1,0:T(8,128)(2,1)S(1)} %add_convert_fusion.proj0), channel_id=1, source_target_pairs={{0,3},{1,2},{2,1},{3,0},{4,7},{5,6},{6,5},{7,4},{8,11},{9,10},{10,... | collective-permute-start | bytes 393224 | tf_op jit(solution)/shard_map/ppermute | solution.py:167
  97.5 19.3 %all-to-all-start.2 = ((bf16[8,128,256]{2,1,0:T(8,128)(2,1)}), bf16[8,128,256]{2,1,0:T(8,128)(2,1)S(1)}, u32[]{:S(2)}, u32[]{:S(2)}) async-start(bf16[8,128,256]{2,1,0:T(8,128)(2,1)} %shard_map.62), calls=%async_computation.2 | async-start | bytes 1048576 | tf_op jit(solution)/shard_map/all_to_all | solution.py:21
  160.7 21.4 %all-to-all-start.5 = ((bf16[8,128,256]{2,1,0:T(8,128)(2,1)}), bf16[8,128,256]{2,1,0:T(8,128)(2,1)S(1)}, u32[]{:S(2)}, u32[]{:S(2)}) async-start(bf16[8,128,256]{2,1,0:T(8,128)(2,1)} %shard_map.64), calls=%async_computation.5 | async-start | bytes 1048576 | tf_op jit(solution)/shard_map/all_to_all | solution.py:21

commit v4 on v3

--- a/solution.py
+++ b/solution.py
@@ -120,32 +120,61 @@
 
 
 def share_kernel(scale, parts_ref, out_ref):
+    cores, devices, _, half = out_ref.shape
     total = jnp.sum(parts_ref[...].astype(F32), axis=0) * scale
     value = total.astype(BF16).T
-    for i in range(out_ref.shape[0]):
-        out_ref[i] = value
-
-
-def image_kernel(core_ref, weight_ref, gram_ref, kept_ref, given_ref):
-    half = kept_ref.shape[1]
-    image = jnp.dot(weight_ref[...], gram_ref[...], preferred_element_type=F32)
-    left, right = image[:, :half], image[:, half:]
-    first = core_ref[0] == 0
-    kept_ref[...] = jnp.where(first, left, right)
-    given_ref[...] = jnp.where(first, right, left).astype(BF16)
-
-
-def coef_kernel(weight_ref, basis_ref, out_ref):
-    size = out_ref.shape[1]
-    basis = basis_ref[...]
-    for i in range(0, weight_ref.shape[1], 2 * size):
-        part = contract(weight_ref[:, i : i + 2 * size], basis, 0, 0).astype(BF16)
-        out_ref[i // size] = part[:size]
-        out_ref[i // size + 1] = part[size:]
+    for core in range(cores):
+        for device in range(devices):
+            out_ref[core, device] = value[:, core * half : (core + 1) * half]
+
+
+def image_kernel(core_ref, own_ref, other_hbm, gram_ref, out_ref, other_ref, sems):
+    core = core_ref[0]
+    block = own_ref.shape[0] // sems.shape[0]
+    parts = [pl.ds(i * block, block) for i in range(sems.shape[0])]
+    fetches = [
+        pltpu.make_async_copy(other_hbm.at[part, :], other_ref.at[part, :], sems.at[i]) for i, part in enumerate(parts)
+    ]
+    for fetch in fetches:
+        fetch.start()
+    own, other = gram_ref[core], gram_ref[1 - core]
+    for part, fetch in zip(parts, fetches):
+        image = jnp.dot(own_ref[part, :], own, preferred_element_type=F32)
+        fetch.wait()
+        image += jnp.dot(other_ref[part, :], other, preferred_element_type=F32)
+        out_ref[part, :] = image.astype(BF16)
+
+
+def coef_kernel(core_ref, own_ref, other_hbm, basis_ref, out_hbm, other_ref, out_ref, in_sems, out_sems):
+    core = core_ref[0]
+    size = out_ref.shape[3]
+    block = own_ref.shape[1] // in_sems.shape[0]
+    parts = [pl.ds(i * block, block) for i in range(in_sems.shape[0])]
+    fetches = [
+        pltpu.make_async_copy(other_hbm.at[:, part], other_ref.at[:, part], in_sems.at[i])
+        for i, part in enumerate(parts)
+    ]
+    for fetch in fetches:
+        fetch.start()
+    turned = basis_ref[...].T
+    sends = []
+    for turn, (which, weight_ref) in enumerate(((core, own_ref), (1 - core, other_ref))):
+        for i, part in enumerate(parts):
+            if turn == 1:
+                fetches[i].wait()
+            value = jnp.dot(turned, weight_ref[:, part], preferred_element_type=F32).astype(BF16)
+            for j in range(block // size):
+                out_ref[turn, i * (block // size) + j] = value[:, j * size : (j + 1) * size]
+        sends.append(pltpu.make_async_copy(out_ref.at[turn], out_hbm.at[which], out_sems.at[turn]))
+        sends[-1].start()
+    for send in sends:
+        send.wait()
 
 
 def total_kernel(parts_ref, out_ref):
-    out_ref[...] = jnp.sum(parts_ref[...].astype(F32), axis=0).T
+    size = parts_ref.shape[2]
+    for core in range(parts_ref.shape[0]):
+        out_ref[core * size : (core + 1) * size, :] = jnp.sum(parts_ref[core].astype(F32), axis=0)
 
 
 def body(hidden_rows, routes, down_weight, probe):
@@ -200,6 +229,7 @@
     proj = kept + sum(across(given[step - 1], "z", nz, step).astype(F32) for step in (3, 2, 1))
     proj = (proj + across(proj.astype(BF16), "z", nz, 4).astype(F32)).astype(BF16)
     quarters = [across(proj, "z", nz, step) for step in (3, 2, 1)]
+    neighbour = across(weight, "c", nc, 1)
 
     gram_part = call(
         gram_kernel,
@@ -212,30 +242,46 @@
     )
     copies = call(
         functools.partial(share_kernel, 1.0 / row_mean),
-        [shape((nz, block, panel), BF16)],
+        [shape((nc, nz, block, half), BF16)],
         nz * block * panel,
         [swap(gram_part, "z")],
     )
-    gram = swap(copies, "z").reshape(width, panel)
-
-    kept, given = call(
+    gram = swap(copies.reshape(nc * nz, block, half), ("c", "z")).reshape(nc, width, half)
+
+    image = call(
         image_kernel,
-        [shape((depth, half), F32), shape((depth, half), BF16)],
+        [shape((depth, half), BF16)],
         2 * depth * width * panel,
-        [core[None], weight, gram],
-        [SMEM, VMEM, VMEM],
-    )
-    chip_sum = kept + lax.dynamic_index_in_dim(lax.all_gather(given, "c"), 1 - core, 0, False).astype(F32)
-    pieces = swap(chip_sum.astype(BF16).reshape(chips, depth // chips, half), ("x", "y"))
-    own = jnp.sum(pieces.astype(F32), axis=0).astype(BF16)
-    basis_half = share(own, ("x", "y"), chips)
-    basis = lax.all_gather(basis_half, "c", axis=1, tiled=True)
+        [core[None], weight, neighbour, gram],
+        [SMEM, VMEM, HBM, VMEM],
+        None,
+        [pltpu.VMEM((depth, width), BF16), pltpu.SemaphoreType.DMA((4,))],
+    )
+    pieces = swap(image.reshape(chips, depth // chips, half), ("x", "y"))
+    own = jnp.sum(pieces.astype(F32), axis=0)
+    basis = share(own.astype(BF16), ("x", "y"), chips)
 
     rows_own = depth // experts
-    place = (lax.axis_index("x") * ny + lax.axis_index("y")) * nc + core
-    basis_rows = lax.dynamic_slice_in_dim(basis, place * rows_own, rows_own, 0).astype(F32)
-    coef_part = call(coef_kernel, [shape((nz, block, panel), BF16)], 2 * depth * width * panel, [weight, basis])
-    coefficients = call(total_kernel, [shape((panel, block), F32)], nz * block * panel, [swap(coef_part, "z")])
+    mine = lax.dynamic_slice_in_dim(own, core * rows_own, rows_own, 0)
+    other = across(lax.dynamic_slice_in_dim(own, (1 - core) * rows_own, rows_own, 0), "c", nc, 1)
+    basis_rows = jnp.where(core == 0, jnp.concatenate([mine, other], 1), jnp.concatenate([other, mine], 1))
+
+    coef_part = call(
+        coef_kernel,
+        [shape((nc, nz, half, block), BF16)],
+        2 * depth * width * panel,
+        [core[None], weight, neighbour, basis],
+        [SMEM, VMEM, HBM, VMEM],
+        [HBM],
+        [
+            pltpu.VMEM((depth, width), BF16),
+            pltpu.VMEM((nc, nz, half, block), BF16),
+            pltpu.SemaphoreType.DMA((4,)),
+            pltpu.SemaphoreType.DMA((nc,)),
+        ],
+    )
+    arrived = swap(coef_part.reshape(nc * nz, half, block), ("c", "z")).reshape(nc, nz, half, block)
+    coefficients = call(total_kernel, [shape((panel, block), F32)], nz * block * panel, [arrived])
     return basis_rows, coefficients[None]
 
 

time: 184 us -> 180 us (0.978)
  blocking collectives: 67.8 us -> 29.9 us
  starting transfers between devices: 52.7 us -> 68.3 us
  waiting for transfers between devices: 49.5 us -> 63.8 us
  Pallas kernels: 11 us -> 15.5 us
    all_to_all x3 -> x2, blocking collectives: 58.1 us -> 29.9 us  [swap(): return lax.all_to_all(value, axes, split_axis=0, concat_axis=0, tiled=False)]
    all_to_all x3 -> x4, starting transfers between devices: 18.9 us -> 35.1 us  [swap(): return lax.all_to_all(value, axes, split_axis=0, concat_axis=0, tiled=False)]
    all_to_all x3 -> x4, waiting for transfers between devices: 36 us -> 46.5 us  [swap(): return lax.all_to_all(value, axes, split_axis=0, concat_axis=0, tiled=False)]
    all_gather x2 -> x0, blocking collectives: 9.66 us -> none  [the longest x1 5.35 us: body(): basis = lax.all_gather(basis_half, 'c', axis=1, tiled=True)]
    pallas_call x7, Pallas kernels: 11 us -> 15.5 us  [call(): pl.pallas_call(kernel, out_shape=outs, in_specs=in_specs or [VMEM] * len(...]
    ppermute x7 -> x9, waiting for transfers between devices: 13.6 us -> 17.3 us  [across(): return lax.ppermute(value, axis, [(i, i ^ step) for i in range(size)])]
    ppermute x7 -> x9, starting transfers between devices: 33.8 us -> 33.2 us  [across(): return lax.ppermute(value, axis, [(i, i ^ step) for i in range(size)])]
  transfers between devices with their start and end apart: 10 -> 13, of which waited for: 7 -> 10; matrix products, arithmetic and copies ran while one was open for 0% -> 0% of each run, Pallas kernels for 0% -> 1%
where the time goes in v4:
time: 180 us; the launch traced here: 179 us
  starting transfers between devices  68.3 us (38%)
  waiting for transfers between devices  63.8 us (35%)
  blocking collectives  29.9 us (17%)
  Pallas kernels  15.5 us (9%)
    all_to_all x4, waiting for transfers between devices, swap(): return lax.all_to_all(value, axes, split_axis=0, concat_axis=0, tiled=False)  46.5 us
    all_to_all x4, starting transfers between devices, swap(): return lax.all_to_all(value, axes, split_axis=0, concat_axis=0, tiled=False)  35.1 us
    ppermute x9, starting transfers between devices, across(): return lax.ppermute(value, axis, [(i, i ^ step) for i in range(size)])  33.2 us
    all_to_all x2, blocking collectives, swap(): return lax.all_to_all(value, axes, split_axis=0, concat_axis=0, tiled=False)  29.9 us
    ppermute x9, waiting for transfers between devices, across(): return lax.ppermute(value, axis, [(i, i ^ step) for i in range(size)])  17.3 us
    pallas_call x7, Pallas kernels, call(): pl.pallas_call(kernel, out_shape=outs, in_specs=in_specs or [VMEM] * len(...  15.5 us
  transfers between devices with their start and end apart: 13, of which 10 were waited for; matrix products, arithmetic and copies ran while one was open for 0% of the time, Pallas kernels for 1%

profile of v4, /device:TPU:1, one launch (start us, length us, event | category | flops | bytes accessed | tf_op | source)
XLA Modules:
  0.0 179.5 jit_solution(5951406044689941155)
XLA Ops:
  0.6 3.4 %shard_map.59 = bf16[1024,1024]{1,0:T(8,128)(2,1)} custom-call(s32[8,64]{1,0:T(8,128)} %bitcast.27, bf16[512,1024]{1,0:T(8,128)(2,1)} %bitcast.26), custom_call_target="tpu_custom_call" | custom-call | flops 1073741824 | bytes 3147776 | tf_op jit(solution)/shard_map/pallas_call | solution.py:36
  4.0 0.0 copy-start
  4.1 0.0 copy-start.1
  4.1 12.0 %all-to-all-start = ((bf16[64,16,1024]{2,1,0:T(8,128)(2,1)}), bf16[64,16,1024]{2,1,0:T(8,128)(2,1)}, u32[]{:S(2)}, u32[]{:S(2)}) async-start(bf16[64,16,1024]{2,1,0:T(8,128)(2,1)} %bitcast.24), calls=%async_computation | async-start | bytes 4194304 | tf_op jit(solution)/shard_map/all_to_all | solution.py:21
  16.1 0.0 copy-done
  16.1 0.0 copy-done.1
  16.1 0.8 shard_map.60
  16.9 7.6 %collective-permute-start.1 = (bf16[256,256]{1,0:T(8,128)(2,1)S(1)}, bf16[256,256]{1,0:T(8,128)(2,1)S(1)}, u32[]{:S(2)}, u32[]{:S(2)}) collective-permute-start(bf16[256,256]{1,0:T(8,128)(2,1)S(1)} %get-tuple-element.6), channel_id=1, source_target_pairs={{0,3},{1,2},{2,1},{3,0},{4,7},{5,6},{6,5},{7,4},{8,11},{9,10},{10,... | collective-permute-start | bytes 393224 | tf_op jit(solution)/shard_map/ppermute | solution.py:196
  24.5 1.9 %collective-permute-start.2 = (bf16[256,256]{1,0:T(8,128)(2,1)S(1)}, bf16[256,256]{1,0:T(8,128)(2,1)S(1)}, u32[]{:S(2)}, u32[]{:S(2)}) collective-permute-start(bf16[256,256]{1,0:T(8,128)(2,1)S(1)} %get-tuple-element.8), channel_id=1, source_target_pairs={{0,2},{1,3},{2,0},{3,1},{4,6},{5,7},{6,4},{7,5},{8,10},{9,11},{10,... | collective-permute-start | bytes 393224 | tf_op jit(solution)/shard_map/ppermute | solution.py:196
  26.4 2.2 %collective-permute-start.3 = (bf16[256,256]{1,0:T(8,128)(2,1)S(1)}, bf16[256,256]{1,0:T(8,128)(2,1)S(1)}, u32[]{:S(2)}, u32[]{:S(2)}) collective-permute-start(bf16[256,256]{1,0:T(8,128)(2,1)S(1)} %get-tuple-element.7), channel_id=1, source_target_pairs={{0,1},{1,0},{2,3},{3,2},{4,5},{5,4},{6,7},{7,6},{8,9},{9,8},{10,11... | collective-permute-start | bytes 393224 | tf_op jit(solution)/shard_map/ppermute | solution.py:196
  28.6 0.0 collective-permute-done.1
  28.6 6.0 %collective-permute-done.2 = bf16[256,256]{1,0:T(8,128)(2,1)S(1)} collective-permute-done((bf16[256,256]{1,0:T(8,128)(2,1)S(1)}, bf16[256,256]{1,0:T(8,128)(2,1)S(1)}, u32[]{:S(2)}, u32[]{:S(2)}) %collective-permute-start.2) | collective-permute-done | bytes 131104 | tf_op jit(solution)/shard_map/ppermute | solution.py:196
  34.6 1.1 collective-permute-done.3
  35.8 0.1 fusion
  35.8 7.6 %collective-permute-start.4 = (bf16[256,256]{1,0:T(8,128)(2,1)S(1)}, bf16[256,256]{1,0:T(8,128)(2,1)S(1)}, u32[]{:S(2)}, u32[]{:S(2)}) collective-permute-start(bf16[256,256]{1,0:T(8,128)(2,1)S(1)} %fusion), channel_id=1, source_target_pairs={{0,4},{1,5},{2,6},{3,7},{4,0},{5,1},{6,2},{7,3},{8,12},{9,13},{10,... | collective-permute-start | bytes 393224 | tf_op jit(solution)/shard_map/ppermute | solution.py:196
  43.5 2.7 %collective-permute-done.4 = bf16[256,256]{1,0:T(8,128)(2,1)S(1)} collective-permute-done((bf16[256,256]{1,0:T(8,128)(2,1)S(1)}, bf16[256,256]{1,0:T(8,128)(2,1)S(1)}, u32[]{:S(2)}, u32[]{:S(2)}) %collective-permute-start.4) | collective-permute-done | bytes 131104 | tf_op jit(solution)/shard_map/ppermute | solution.py:196
  46.2 0.1 add_convert_fusion.proj0
  46.3 1.9 %collective-permute-start.5 = (bf16[256,256]{1,0:T(8,128)(2,1)S(1)}, bf16[256,256]{1,0:T(8,128)(2,1)S(1)}, u32[]{:S(2)}, u32[]{:S(2)}) collective-permute-start(bf16[256,256]{1,0:T(8,128)(2,1)S(1)} %add_convert_fusion.proj0), channel_id=1, source_target_pairs={{0,1},{1,0},{2,3},{3,2},{4,5},{5,4},{6,7},{7,6},{8,9},{9,8},{10,11... | collective-permute-start | bytes 393224 | tf_op jit(solution)/shard_map/ppermute | solution.py:196
  48.2 4.4 %collective-permute-start.6 = (bf16[256,256]{1,0:T(8,128)(2,1)S(1)}, bf16[256,256]{1,0:T(8,128)(2,1)S(1)}, u32[]{:S(2)}, u32[]{:S(2)}) collective-permute-start(bf16[256,256]{1,0:T(8,128)(2,1)S(1)} %add_convert_fusion.proj0), channel_id=1, source_target_pairs={{0,2},{1,3},{2,0},{3,1},{4,6},{5,7},{6,4},{7,5},{8,10},{9,11},{10,... | collective-permute-start | bytes 393224 | tf_op jit(solution)/shard_map/ppermute | solution.py:196
  52.7 2.9 %collective-permute-start.7 = (bf16[256,256]{1,0:T(8,128)(2,1)S(1)}, bf16[256,256]{1,0:T(8,128)(2,1)S(1)}, u32[]{:S(2)}, u32[]{:S(2)}) collective-permute-start(bf16[256,256]{1,0:T(8,128)(2,1)S(1)} %add_convert_fusion.proj0), channel_id=1, source_target_pairs={{0,3},{1,2},{2,1},{3,0},{4,7},{5,6},{6,5},{7,4},{8,11},{9,10},{10,... | collective-permute-start | bytes 393224 | tf_op jit(solution)/shard_map/ppermute | solution.py:196
  55.6 0.0 collective-permute-done.5.proj1
  55.6 1.2 collective-permute-done.6.proj2
  56.8 5.2 %collective-permute-done.7.proj3 = bf16[256,256]{1,0:T(8,128)(2,1)S(1)} collective-permute-done((bf16[256,256]{1,0:T(8,128)(2,1)S(1)}, bf16[256,256]{1,0:T(8,128)(2,1)S(1)}, u32[]{:S(2)}, u32[]{:S(2)}) %collective-permute-start.7) | collective-permute-done | bytes 131104 | tf_op jit(solution)/shard_map/ppermute | solution.py:196
  62.0 5.3 %all-to-all-done = bf16[64,16,1024]{2,1,0:T(8,128)(2,1)} async-done(((bf16[64,16,1024]{2,1,0:T(8,128)(2,1)}), bf16[64,16,1024]{2,1,0:T(8,128)(2,1)}, u32[]{:S(2)}, u32[]{:S(2)}) %all-to-all-start) | async-done | bytes 2097184 | tf_op jit(solution)/shard_map/all_to_all | solution.py:21
  67.3 3.7 %shard_map.61 = bf16[8,256,128]{2,1,0:T(8,128)(2,1)} custom-call(s32[1]{0:T(128)} %bitcast.2.quarter_ref, bf16[1024,1024]{1,0:T(8,128)(2,1)} %bitcast.6.rows_ref, bf16[256,256]{1,0:T(8,128)(2,1)S(1)} %add_convert_fusion.proj0, bf16[256,256]{1,0:T(8,128)(2,1)S(1)} %collective-permute-done.5.proj1, bf16[256,256]{1,0:T(8,128)(2,1)S(1)} %collective-permute-done.6.proj2, ...), custom_call_target="tpu_custom_call" | custom-call | flops 1073741824 | bytes 3145732 | tf_op jit(solution)/shard_map/pallas_call | solution.py:36
  71.0 9.9 %all-to-all-start.1 = ((bf16[8,256,128]{2,1,0:T(8,128)(2,1)}), bf16[8,256,128]{2,1,0:T(8,128)(2,1)S(1)}, u32[]{:S(2)}, u32[]{:S(2)}) async-start(bf16[8,256,128]{2,1,0:T(8,128)(2,1)} %shard_map.61), calls=%async_computation.1 | async-start | bytes 1048576 | tf_op jit(solution)/shard_map/all_to_all | solution.py:21
  80.9 2.6 %collective-permute-start = (bf16[896,1024]{1,0:T(8,128)(2,1)S(1)}, bf16[896,1024]{1,0:T(8,128)(2,1)}, u32[]{:S(2)}, u32[]{:S(2)}) collective-permute-start(bf16[896,1024]{1,0:T(8,128)(2,1)S(1)} %bitcast.19), channel_id=1, source_target_pairs={{0,8},{8,0},{1,9},{9,1},{2,10},{10,2},{3,11},{11,3},{4,12},{12,4},... | collective-permute-start | bytes 5505032 | tf_op jit(solution)/shard_map/ppermute | solution.py:196
  83.5 15.4 %all-to-all-done.1.parts_ref = bf16[8,256,128]{2,1,0:T(8,128)(2,1)S(1)} async-done(((bf16[8,256,128]{2,1,0:T(8,128)(2,1)}), bf16[8,256,128]{2,1,0:T(8,128)(2,1)S(1)}, u32[]{:S(2)}, u32[]{:S(2)}) %all-to-all-start.1) | async-done | bytes 524320 | tf_op jit(solution)/shard_map/all_to_all | solution.py:21
  98.9 1.0 shard_map.62
  99.9 3.9 %all-to-all-start.2 = ((bf16[16,128,128]{2,1,0:T(8,128)(2,1)}), bf16[16,128,128]{2,1,0:T(8,128)(2,1)S(1)}, u32[]{:S(2)}, u32[]{:S(2)}) async-start(bf16[16,128,128]{2,1,0:T(8,128)(2,1)} %bitcast.10), calls=%async_computation.2 | async-start | bytes 1048576 | tf_op jit(solution)/shard_map/all_to_all | solution.py:21
  103.8 0.0 collective-permute-done.other_hbm
  103.8 14.8 %all-to-all-done.2 = bf16[16,128,128]{2,1,0:T(8,128)(2,1)S(1)} async-done(((bf16[16,128,128]{2,1,0:T(8,128)(2,1)}), bf16[16,128,128]{2,1,0:T(8,128)(2,1)S(1)}, u32[]{:S(2)}, u32[]{:S(2)}) %all-to-all-start.2) | async-done | bytes 524320 | tf_op jit(solution)/shard_map/all_to_all | solution.py:21
  118.6 2.7 %shard_map.63 = bf16[896,128]{1,0:T(8,128)(2,1)S(1)} custom-call(s32[1]{0:T(128)} %bitcast.core_ref, bf16[896,1024]{1,0:T(8,128)(2,1)S(1)} %bitcast.20, bf16[896,1024]{1,0:T(8,128)(2,1)} %collective-permute-done.other_hbm, bf16[2,1024,128]{2,1,0:T(8,128)(2,1)S(1)} %bitcast.22), custom_call_target="tpu_custom_call" | custom-call | flops 469762048 | bytes 4423684 | tf_op jit(solution)/shard_map/pallas_call | solution.py:36
  121.3 14.4 %all_to_all.30 = bf16[32,28,128]{2,1,0:T(8,128)(2,1)S(1)} all-to-all(bf16[32,28,128]{2,1,0:T(8,128)(2,1)S(1)} %reshape.39), channel_id=1, replica_groups=mesh['x'=4,'y'=8,'c'=2,'z'=8] {'x','y'}, dimensions={0} | all-to-all | bytes 458752 | tf_op jit(solution)/shard_map/all_to_all | solution.py:21
  135.7 0.1 convert_reduce_fusion
  135.8 15.5 %all_to_all.31 = bf16[32,28,128]{2,1,0:T(8,128)(2,1)S(1)} all-to-all(bf16[32,28,128]{2,1,0:T(8,128)(2,1)S(1)} %broadcast_in_dim.18), channel_id=1, replica_groups=mesh['x'=4,'y'=8,'c'=2,'z'=8] {'x','y'}, dimensions={0} | all-to-all | bytes 458752 | tf_op jit(solution)/shard_map/all_to_all | solution.py:21
  151.4 3.2 %shard_map.64 = bf16[2,8,128,128]{3,2,1,0:T(8,128)(2,1)} custom-call(s32[1]{0:T(128)} %bitcast.core_ref, bf16[896,1024]{1,0:T(8,128)(2,1)S(1)} %bitcast.21, bf16[896,1024]{1,0:T(8,128)(2,1)} %collective-permute-done.other_hbm, bf16[896,128]{1,0:T(8,128)(2,1)S(1)} %reshape.40.basis_ref), custom_call_target="tpu_custom_call" | custom-call | flops 469762048 | bytes 4423684 | tf_op jit(solution)/shard_map/pallas_call | solution.py:36
  154.6 9.3 %all-to-all-start.5 = ((bf16[16,128,128]{2,1,0:T(8,128)(2,1)}), bf16[16,128,128]{2,1,0:T(8,128)(2,1)S(1)}, u32[]{:S(2)}, u32[]{:S(2)}) async-start(bf16[16,128,128]{2,1,0:T(8,128)(2,1)} %bitcast.12), calls=%async_computation.5 | async-start | bytes 1048576 | tf_op jit(solution)/shard_map/all_to_all | solution.py:21
  164.0 2.0 %collective-permute-start.8 = (f32[14,128]{1,0:T(8,128)S(1)}, f32[14,128]{1,0:T(8,128)S(1)}, u32[]{:S(2)}, u32[]{:S(2)}) collective-permute-start(f32[14,128]{1,0:T(8,128)S(1)} %get-tuple-element.10), channel_id=1, source_target_pairs={{0,8},{8,0},{1,9},{9,1},{2,10},{10,2},{3,11},{11,3},{4,12},{12,4},... | collective-permute-start | bytes 21512 | tf_op jit(solution)/shard_map/ppermute | solution.py:196
  166.0 1.0 collective-permute-done.8
  167.0 0.6 maximum_select_fusion
  167.7 11.1 %all-to-all-done.5 = bf16[16,128,128]{2,1,0:T(8,128)(2,1)S(1)} async-done(((bf16[16,128,128]{2,1,0:T(8,128)(2,1)}), bf16[16,128,128]{2,1,0:T(8,128)(2,1)S(1)}, u32[]{:S(2)}, u32[]{:S(2)}) %all-to-all-start.5) | async-done | bytes 524320 | tf_op jit(solution)/shard_map/all_to_all | solution.py:21
  178.7 0.7 shard_map.65
  (6 shorter events, 0.2 us)
Async XLA Ops:
  4.0 12.0 %copy-start = (bf16[1,896,1024]{2,1,0:T(8,128)(2,1)S(1)}, bf16[1,896,1024]{2,1,0:T(8,128)(2,1)}, u32[]{:S(2)}) copy-start(bf16[1,896,1024]{2,1,0:T(8,128)(2,1)} %param.6) | copy-start | bytes 5505028
  4.1 12.0 %copy-start.1 = (bf16[896,256]{1,0:T(8,128)(2,1)S(1)}, bf16[896,256]{1,0:T(8,128)(2,1)}, u32[]{:S(2)}) copy-start(bf16[896,256]{1,0:T(8,128)(2,1)} %probe_ref.1) | copy-start | bytes 1376260
  4.1 63.2 %all-to-all-start = ((bf16[64,16,1024]{2,1,0:T(8,128)(2,1)}), bf16[64,16,1024]{2,1,0:T(8,128)(2,1)}, u32[]{:S(2)}, u32[]{:S(2)}) async-start(bf16[64,16,1024]{2,1,0:T(8,128)(2,1)} %bitcast.24), calls=%async_computation | async-start | bytes 4194304 | tf_op jit(solution)/shard_map/all_to_all | solution.py:21
  16.9 11.7 %collective-permute-start.1 = (bf16[256,256]{1,0:T(8,128)(2,1)S(1)}, bf16[256,256]{1,0:T(8,128)(2,1)S(1)}, u32[]{:S(2)}, u32[]{:S(2)}) collective-permute-start(bf16[256,256]{1,0:T(8,128)(2,1)S(1)} %get-tuple-element.6), channel_id=1, source_target_pairs={{0,3},{1,2},{2,1},{3,0},{4,7},{5,6},{6,5},{7,4},{8,11},{9,10},{10,... | collective-permute-start | bytes 393224 | tf_op jit(solution)/shard_map/ppermute | solution.py:196
  24.5 10.1 %collective-permute-start.2 = (bf16[256,256]{1,0:T(8,128)(2,1)S(1)}, bf16[256,256]{1,0:T(8,128)(2,1)S(1)}, u32[]{:S(2)}, u32[]{:S(2)}) collective-permute-start(bf16[256,256]{1,0:T(8,128)(2,1)S(1)} %get-tuple-element.8), channel_id=1, source_target_pairs={{0,2},{1,3},{2,0},{3,1},{4,6},{5,7},{6,4},{7,5},{8,10},{9,11},{10,... | collective-permute-start | bytes 393224 | tf_op jit(solution)/shard_map/ppermute | solution.py:196
  26.4 9.3 %collective-permute-start.3 = (bf16[256,256]{1,0:T(8,128)(2,1)S(1)}, bf16[256,256]{1,0:T(8,128)(2,1)S(1)}, u32[]{:S(2)}, u32[]{:S(2)}) collective-permute-start(bf16[256,256]{1,0:T(8,128)(2,1)S(1)} %get-tuple-element.7), channel_id=1, source_target_pairs={{0,1},{1,0},{2,3},{3,2},{4,5},{5,4},{6,7},{7,6},{8,9},{9,8},{10,11... | collective-permute-start | bytes 393224 | tf_op jit(solution)/shard_map/ppermute | solution.py:196
  35.8 10.4 %collective-permute-start.4 = (bf16[256,256]{1,0:T(8,128)(2,1)S(1)}, bf16[256,256]{1,0:T(8,128)(2,1)S(1)}, u32[]{:S(2)}, u32[]{:S(2)}) collective-permute-start(bf16[256,256]{1,0:T(8,128)(2,1)S(1)} %fusion), channel_id=1, source_target_pairs={{0,4},{1,5},{2,6},{3,7},{4,0},{5,1},{6,2},{7,3},{8,12},{9,13},{10,... | collective-permute-start | bytes 393224 | tf_op jit(solution)/shard_map/ppermute | solution.py:196
  46.3 9.3 %collective-permute-start.5 = (bf16[256,256]{1,0:T(8,128)(2,1)S(1)}, bf16[256,256]{1,0:T(8,128)(2,1)S(1)}, u32[]{:S(2)}, u32[]{:S(2)}) collective-permute-start(bf16[256,256]{1,0:T(8,128)(2,1)S(1)} %add_convert_fusion.proj0), channel_id=1, source_target_pairs={{0,1},{1,0},{2,3},{3,2},{4,5},{5,4},{6,7},{7,6},{8,9},{9,8},{10,11... | collective-permute-start | bytes 393224 | tf_op jit(solution)/shard_map/ppermute | solution.py:196
  48.2 8.6 %collective-permute-start.6 = (bf16[256,256]{1,0:T(8,128)(2,1)S(1)}, bf16[256,256]{1,0:T(8,128)(2,1)S(1)}, u32[]{:S(2)}, u32[]{:S(2)}) collective-permute-start(bf16[256,256]{1,0:T(8,128)(2,1)S(1)} %add_convert_fusion.proj0), channel_id=1, source_target_pairs={{0,2},{1,3},{2,0},{3,1},{4,6},{5,7},{6,4},{7,5},{8,10},{9,11},{10,... | collective-permute-start | bytes 393224 | tf_op jit(solution)/shard_map/ppermute | solution.py:196
  52.7 9.3 %collective-permute-start.7 = (bf16[256,256]{1,0:T(8,128)(2,1)S(1)}, bf16[256,256]{1,0:T(8,128)(2,1)S(1)}, u32[]{:S(2)}, u32[]{:S(2)}) collective-permute-start(bf16[256,256]{1,0:T(8,128)(2,1)S(1)} %add_convert_fusion.proj0), channel_id=1, source_target_pairs={{0,3},{1,2},{2,1},{3,0},{4,7},{5,6},{6,5},{7,4},{8,11},{9,10},{10,... | collective-permute-start | bytes 393224 | tf_op jit(solution)/shard_map/ppermute | solution.py:196
  71.0 27.9 %all-to-all-start.1 = ((bf16[8,256,128]{2,1,0:T(8,128)(2,1)}), bf16[8,256,128]{2,1,0:T(8,128)(2,1)S(1)}, u32[]{:S(2)}, u32[]{:S(2)}) async-start(bf16[8,256,128]{2,1,0:T(8,128)(2,1)} %shard_map.61), calls=%async_computation.1 | async-start | bytes 1048576 | tf_op jit(solution)/shard_map/all_to_all | solution.py:21
  80.9 22.8 %collective-permute-start = (bf16[896,1024]{1,0:T(8,128)(2,1)S(1)}, bf16[896,1024]{1,0:T(8,128)(2,1)}, u32[]{:S(2)}, u32[]{:S(2)}) collective-permute-start(bf16[896,1024]{1,0:T(8,128)(2,1)S(1)} %bitcast.19), channel_id=1, source_target_pairs={{0,8},{8,0},{1,9},{9,1},{2,10},{10,2},{3,11},{11,3},{4,12},{12,4},... | collective-permute-start | bytes 5505032 | tf_op jit(solution)/shard_map/ppermute | solution.py:196
  99.9 18.7 %all-to-all-start.2 = ((bf16[16,128,128]{2,1,0:T(8,128)(2,1)}), bf16[16,128,128]{2,1,0:T(8,128)(2,1)S(1)}, u32[]{:S(2)}, u32[]{:S(2)}) async-start(bf16[16,128,128]{2,1,0:T(8,128)(2,1)} %bitcast.10), calls=%async_computation.2 | async-start | bytes 1048576 | tf_op jit(solution)/shard_map/all_to_all | solution.py:21
  154.6 24.1 %all-to-all-start.5 = ((bf16[16,128,128]{2,1,0:T(8,128)(2,1)}), bf16[16,128,128]{2,1,0:T(8,128)(2,1)S(1)}, u32[]{:S(2)}, u32[]{:S(2)}) async-start(bf16[16,128,128]{2,1,0:T(8,128)(2,1)} %bitcast.12), calls=%async_computation.5 | async-start | bytes 1048576 | tf_op jit(solution)/shard_map/all_to_all | solution.py:21
  164.0 3.1 %collective-permute-start.8 = (f32[14,128]{1,0:T(8,128)S(1)}, f32[14,128]{1,0:T(8,128)S(1)}, u32[]{:S(2)}, u32[]{:S(2)}) collective-permute-start(f32[14,128]{1,0:T(8,128)S(1)} %get-tuple-element.10), channel_id=1, source_target_pairs={{0,8},{8,0},{1,9},{9,1},{2,10},{10,2},{3,11},{11,3},{4,12},{12,4},... | collective-permute-start | bytes 21512 | tf_op jit(solution)/shard_map/ppermute | solution.py:196

commit v5 on v4

--- a/solution.py
+++ b/solution.py
@@ -99,7 +99,7 @@
             given_ref[step - 1] = part.astype(BF16)
 
 
-def gram_kernel(quarter_ref, rows_ref, proj0, proj1, proj2, proj3, out_ref, proj_ref):
+def gram_kernel(quarter_ref, rows_ref, proj3, proj2, proj1, proj0, out_ref, proj_ref):
     quarter = quarter_ref[0]
     block = 256
     count, width = rows_ref.shape
@@ -226,16 +226,18 @@
         [quarter, weight, probe],
         [SMEM, VMEM, VMEM],
     )
-    proj = kept + sum(across(given[step - 1], "z", nz, step).astype(F32) for step in (3, 2, 1))
+    proj = kept + sum(across(given[step - 1], "z", nz, step).astype(F32) for step in (1, 2, 3))
     proj = (proj + across(proj.astype(BF16), "z", nz, 4).astype(F32)).astype(BF16)
-    quarters = [across(proj, "z", nz, step) for step in (3, 2, 1)]
+    quarters = [across(proj, "z", nz, step) for step in (1, 2, 3)]
     neighbour = across(weight, "c", nc, 1)
+
+    rows, neighbour = lax.optimization_barrier((rows, neighbour))
 
     gram_part = call(
         gram_kernel,
         [shape((nz, panel, block), BF16)],
         4 * slots * width * panel,
-        [quarter, rows, proj] + quarters[::-1],
+        [quarter, rows] + quarters[::-1] + [proj],
         [SMEM] + [VMEM] * 5,
         None,
         [pltpu.VMEM((width, panel), BF16)],

time: 180 us -> 179 us (level)
  blocking collectives: 29.9 us -> 56.2 us
  waiting for transfers between devices: 63.8 us -> 45.7 us
  starting transfers between devices: 68.3 us -> 60 us
    all_to_all x2 -> x3, blocking collectives: 29.9 us -> 56.2 us  [swap(): return lax.all_to_all(value, axes, split_axis=0, concat_axis=0, tiled=False)]
    all_to_all x4 -> x3, waiting for transfers between devices: 46.5 us -> 34.3 us  [swap(): return lax.all_to_all(value, axes, split_axis=0, concat_axis=0, tiled=False)]
    all_to_all x4 -> x3, starting transfers between devices: 35.1 us -> 26.6 us  [swap(): return lax.all_to_all(value, axes, split_axis=0, concat_axis=0, tiled=False)]
    ppermute x9, waiting for transfers between devices: 17.3 us -> 11.3 us  [across(): return lax.ppermute(value, axis, [(i, i ^ step) for i in range(size)])]
  transfers between devices with their start and end apart: 13 -> 12, of which waited for: 10 -> 7; matrix products, arithmetic and copies ran while one was open for 0% -> 0% of each run, Pallas kernels for 1% -> 0%
where the time goes in v5:
time: 179 us; the launch traced here: 178 us
  starting transfers between devices  60 us (34%)
  blocking collectives  56.2 us (31%)
  waiting for transfers between devices  45.7 us (26%)
  Pallas kernels  14.7 us (8%)
    all_to_all x3, blocking collectives, swap(): return lax.all_to_all(value, axes, split_axis=0, concat_axis=0, tiled=False)  56.2 us
    all_to_all x3, waiting for transfers between devices, swap(): return lax.all_to_all(value, axes, split_axis=0, concat_axis=0, tiled=False)  34.3 us
    ppermute x9, starting transfers between devices, across(): return lax.ppermute(value, axis, [(i, i ^ step) for i in range(size)])  33.4 us
    all_to_all x3, starting transfers between devices, swap(): return lax.all_to_all(value, axes, split_axis=0, concat_axis=0, tiled=False)  26.6 us
    pallas_call x7, Pallas kernels, call(): pl.pallas_call(kernel, out_shape=outs, in_specs=in_specs or [VMEM] * len(...  14.7 us
    ppermute x9, waiting for transfers between devices, across(): return lax.ppermute(value, axis, [(i, i ^ step) for i in range(size)])  11.3 us
  transfers between devices with their start and end apart: 12, of which 7 were waited for; matrix products, arithmetic and copies ran while one was open for 0% of the time, Pallas kernels for 0%

profile of v5, /device:TPU:1, one launch (start us, length us, event | category | flops | bytes accessed | tf_op | source)
XLA Modules:
  0.0 178.4 jit_solution(8646305068726999019)
XLA Ops:
  0.6 3.4 %shard_map.59 = bf16[1024,1024]{1,0:T(8,128)(2,1)} custom-call(s32[8,64]{1,0:T(8,128)} %bitcast.27, bf16[512,1024]{1,0:T(8,128)(2,1)} %bitcast.26), custom_call_target="tpu_custom_call" | custom-call | flops 1073741824 | bytes 3147776 | tf_op jit(solution)/shard_map/pallas_call | solution.py:36
  4.1 0.0 copy-start
  4.1 0.0 copy-start.1
  4.1 12.0 %all-to-all-start = ((bf16[64,16,1024]{2,1,0:T(8,128)(2,1)}), bf16[64,16,1024]{2,1,0:T(8,128)(2,1)}, u32[]{:S(2)}, u32[]{:S(2)}) async-start(bf16[64,16,1024]{2,1,0:T(8,128)(2,1)} %bitcast.24), calls=%async_computation | async-start | bytes 4194304 | tf_op jit(solution)/shard_map/all_to_all | solution.py:21
  16.0 0.0 copy-done
  16.1 2.5 %collective-permute-start = (bf16[896,1024]{1,0:T(8,128)(2,1)S(1)}, bf16[896,1024]{1,0:T(8,128)(2,1)}, u32[]{:S(2)}, u32[]{:S(2)}) collective-permute-start(bf16[896,1024]{1,0:T(8,128)(2,1)S(1)} %bitcast.18), channel_id=1, source_target_pairs={{0,8},{8,0},{1,9},{9,1},{2,10},{10,2},{3,11},{11,3},{4,12},{12,4},... | collective-permute-start | bytes 5505032 | tf_op jit(solution)/shard_map/ppermute | solution.py:196
  18.6 0.0 copy-done.1
  18.6 0.8 shard_map.60
  19.4 7.5 %collective-permute-start.3 = (bf16[256,256]{1,0:T(8,128)(2,1)S(1)}, bf16[256,256]{1,0:T(8,128)(2,1)S(1)}, u32[]{:S(2)}, u32[]{:S(2)}) collective-permute-start(bf16[256,256]{1,0:T(8,128)(2,1)S(1)} %get-tuple-element.11), channel_id=1, source_target_pairs={{0,3},{1,2},{2,1},{3,0},{4,7},{5,6},{6,5},{7,4},{8,11},{9,10},{10,... | collective-permute-start | bytes 393224 | tf_op jit(solution)/shard_map/ppermute | solution.py:196
  27.0 1.9 %collective-permute-start.2 = (bf16[256,256]{1,0:T(8,128)(2,1)S(1)}, bf16[256,256]{1,0:T(8,128)(2,1)S(1)}, u32[]{:S(2)}, u32[]{:S(2)}) collective-permute-start(bf16[256,256]{1,0:T(8,128)(2,1)S(1)} %get-tuple-element.12), channel_id=1, source_target_pairs={{0,2},{1,3},{2,0},{3,1},{4,6},{5,7},{6,4},{7,5},{8,10},{9,11},{10,... | collective-permute-start | bytes 393224 | tf_op jit(solution)/shard_map/ppermute | solution.py:196
  28.9 2.2 %collective-permute-start.1 = (bf16[256,256]{1,0:T(8,128)(2,1)S(1)}, bf16[256,256]{1,0:T(8,128)(2,1)S(1)}, u32[]{:S(2)}, u32[]{:S(2)}) collective-permute-start(bf16[256,256]{1,0:T(8,128)(2,1)S(1)} %get-tuple-element.10), channel_id=1, source_target_pairs={{0,1},{1,0},{2,3},{3,2},{4,5},{5,4},{6,7},{7,6},{8,9},{9,8},{10,11... | collective-permute-start | bytes 393224 | tf_op jit(solution)/shard_map/ppermute | solution.py:196
  31.1 0.0 collective-permute-done.3
  31.1 6.5 %collective-permute-done.2 = bf16[256,256]{1,0:T(8,128)(2,1)S(1)} collective-permute-done((bf16[256,256]{1,0:T(8,128)(2,1)S(1)}, bf16[256,256]{1,0:T(8,128)(2,1)S(1)}, u32[]{:S(2)}, u32[]{:S(2)}) %collective-permute-start.2) | collective-permute-done | bytes 131104 | tf_op jit(solution)/shard_map/ppermute | solution.py:196
  37.5 0.9 collective-permute-done.1
  38.5 0.1 fusion
  38.6 8.0 %collective-permute-start.4 = (bf16[256,256]{1,0:T(8,128)(2,1)S(1)}, bf16[256,256]{1,0:T(8,128)(2,1)S(1)}, u32[]{:S(2)}, u32[]{:S(2)}) collective-permute-start(bf16[256,256]{1,0:T(8,128)(2,1)S(1)} %fusion), channel_id=1, source_target_pairs={{0,4},{1,5},{2,6},{3,7},{4,0},{5,1},{6,2},{7,3},{8,12},{9,13},{10,... | collective-permute-start | bytes 393224 | tf_op jit(solution)/shard_map/ppermute | solution.py:196
  46.5 2.9 %collective-permute-done.4 = bf16[256,256]{1,0:T(8,128)(2,1)S(1)} collective-permute-done((bf16[256,256]{1,0:T(8,128)(2,1)S(1)}, bf16[256,256]{1,0:T(8,128)(2,1)S(1)}, u32[]{:S(2)}, u32[]{:S(2)}) %collective-permute-start.4) | collective-permute-done | bytes 131104 | tf_op jit(solution)/shard_map/ppermute | solution.py:196
  49.4 0.1 add_convert_fusion.proj0
  49.5 4.1 %collective-permute-start.5 = (bf16[256,256]{1,0:T(8,128)(2,1)S(1)}, bf16[256,256]{1,0:T(8,128)(2,1)S(1)}, u32[]{:S(2)}, u32[]{:S(2)}) collective-permute-start(bf16[256,256]{1,0:T(8,128)(2,1)S(1)} %add_convert_fusion.proj0), channel_id=1, source_target_pairs={{0,3},{1,2},{2,1},{3,0},{4,7},{5,6},{6,5},{7,4},{8,11},{9,10},{10,... | collective-permute-start | bytes 393224 | tf_op jit(solution)/shard_map/ppermute | solution.py:196
  53.6 1.9 %collective-permute-start.6 = (bf16[256,256]{1,0:T(8,128)(2,1)S(1)}, bf16[256,256]{1,0:T(8,128)(2,1)S(1)}, u32[]{:S(2)}, u32[]{:S(2)}) collective-permute-start(bf16[256,256]{1,0:T(8,128)(2,1)S(1)} %add_convert_fusion.proj0), channel_id=1, source_target_pairs={{0,2},{1,3},{2,0},{3,1},{4,6},{5,7},{6,4},{7,5},{8,10},{9,11},{10,... | collective-permute-start | bytes 393224 | tf_op jit(solution)/shard_map/ppermute | solution.py:196
  55.5 3.3 %collective-permute-start.7 = (bf16[256,256]{1,0:T(8,128)(2,1)S(1)}, bf16[256,256]{1,0:T(8,128)(2,1)S(1)}, u32[]{:S(2)}, u32[]{:S(2)}) collective-permute-start(bf16[256,256]{1,0:T(8,128)(2,1)S(1)} %add_convert_fusion.proj0), channel_id=1, source_target_pairs={{0,1},{1,0},{2,3},{3,2},{4,5},{5,4},{6,7},{7,6},{8,9},{9,8},{10,11... | collective-permute-start | bytes 393224 | tf_op jit(solution)/shard_map/ppermute | solution.py:196
  58.8 0.0 collective-permute-done.other_hbm
  58.8 8.5 %all-to-all-done = bf16[64,16,1024]{2,1,0:T(8,128)(2,1)} async-done(((bf16[64,16,1024]{2,1,0:T(8,128)(2,1)}), bf16[64,16,1024]{2,1,0:T(8,128)(2,1)}, u32[]{:S(2)}, u32[]{:S(2)}) %all-to-all-start) | async-done | bytes 2097184 | tf_op jit(solution)/shard_map/all_to_all | solution.py:21
  67.3 0.0 collective-permute-done.5.proj3
  67.3 0.0 collective-permute-done.6.proj2
  67.3 0.0 collective-permute-done.7.proj1
  67.3 2.9 %shard_map.61 = bf16[8,256,128]{2,1,0:T(8,128)(2,1)S(1)} custom-call(s32[1]{0:T(128)} %bitcast.6.quarter_ref, bf16[1024,1024]{1,0:T(8,128)(2,1)} %bitcast.5.rows_ref, bf16[256,256]{1,0:T(8,128)(2,1)S(1)} %collective-permute-done.5.proj3, bf16[256,256]{1,0:T(8,128)(2,1)S(1)} %collective-permute-done.6.proj2, ...), custom_call_target="tpu_custom_call" | custom-call | flops 1073741824 | bytes 3145732 | tf_op jit(solution)/shard_map/pallas_call | solution.py:36
  70.2 26.3 %all_to_all.30.parts_ref = bf16[8,256,128]{2,1,0:T(8,128)(2,1)S(1)} all-to-all(bf16[8,256,128]{2,1,0:T(8,128)(2,1)S(1)} %shard_map.61), channel_id=1, replica_groups=mesh['x'=4,'y'=8,'c'=2,'z'=8] {'z'}, dimensions={0} | all-to-all | bytes 1048576 | tf_op jit(solution)/shard_map/all_to_all | solution.py:21
  96.5 1.0 shard_map.62
  97.5 5.3 %all-to-all-start.2 = ((bf16[16,128,128]{2,1,0:T(8,128)(2,1)}), bf16[16,128,128]{2,1,0:T(8,128)(2,1)S(1)}, u32[]{:S(2)}, u32[]{:S(2)}) async-start(bf16[16,128,128]{2,1,0:T(8,128)(2,1)} %bitcast.10), calls=%async_computation.2 | async-start | bytes 1048576 | tf_op jit(solution)/shard_map/all_to_all | solution.py:21
  102.8 14.8 %all-to-all-done.2 = bf16[16,128,128]{2,1,0:T(8,128)(2,1)S(1)} async-done(((bf16[16,128,128]{2,1,0:T(8,128)(2,1)}), bf16[16,128,128]{2,1,0:T(8,128)(2,1)S(1)}, u32[]{:S(2)}, u32[]{:S(2)}) %all-to-all-start.2) | async-done | bytes 524320 | tf_op jit(solution)/shard_map/all_to_all | solution.py:21
  117.6 2.7 %shard_map.63 = bf16[896,128]{1,0:T(8,128)(2,1)S(1)} custom-call(s32[1]{0:T(128)} %bitcast.core_ref, bf16[896,1024]{1,0:T(8,128)(2,1)S(1)} %bitcast.20, bf16[896,1024]{1,0:T(8,128)(2,1)} %collective-permute-done.other_hbm, bf16[2,1024,128]{2,1,0:T(8,128)(2,1)S(1)} %bitcast.22), custom_call_target="tpu_custom_call" | custom-call | flops 469762048 | bytes 4423684 | tf_op jit(solution)/shard_map/pallas_call | solution.py:36
  120.3 14.3 %all_to_all.31 = bf16[32,28,128]{2,1,0:T(8,128)(2,1)S(1)} all-to-all(bf16[32,28,128]{2,1,0:T(8,128)(2,1)S(1)} %reshape.39), channel_id=1, replica_groups=mesh['x'=4,'y'=8,'c'=2,'z'=8] {'x','y'}, dimensions={0} | all-to-all | bytes 458752 | tf_op jit(solution)/shard_map/all_to_all | solution.py:21
  134.7 0.1 convert_reduce_fusion
  134.8 15.5 %all_to_all.32 = bf16[32,28,128]{2,1,0:T(8,128)(2,1)S(1)} all-to-all(bf16[32,28,128]{2,1,0:T(8,128)(2,1)S(1)} %broadcast_in_dim.18), channel_id=1, replica_groups=mesh['x'=4,'y'=8,'c'=2,'z'=8] {'x','y'}, dimensions={0} | all-to-all | bytes 458752 | tf_op jit(solution)/shard_map/all_to_all | solution.py:21
  150.4 3.2 %shard_map.64 = bf16[2,8,128,128]{3,2,1,0:T(8,128)(2,1)} custom-call(s32[1]{0:T(128)} %bitcast.core_ref, bf16[896,1024]{1,0:T(8,128)(2,1)S(1)} %bitcast.21, bf16[896,1024]{1,0:T(8,128)(2,1)} %collective-permute-done.other_hbm, bf16[896,128]{1,0:T(8,128)(2,1)S(1)} %reshape.40.basis_ref), custom_call_target="tpu_custom_call" | custom-call | flops 469762048 | bytes 4423684 | tf_op jit(solution)/shard_map/pallas_call | solution.py:36
  153.6 9.3 %all-to-all-start.5 = ((bf16[16,128,128]{2,1,0:T(8,128)(2,1)}), bf16[16,128,128]{2,1,0:T(8,128)(2,1)S(1)}, u32[]{:S(2)}, u32[]{:S(2)}) async-start(bf16[16,128,128]{2,1,0:T(8,128)(2,1)} %bitcast.12), calls=%async_computation.5 | async-start | bytes 1048576 | tf_op jit(solution)/shard_map/all_to_all | solution.py:21
  162.9 2.0 %collective-permute-start.8 = (f32[14,128]{1,0:T(8,128)S(1)}, f32[14,128]{1,0:T(8,128)S(1)}, u32[]{:S(2)}, u32[]{:S(2)}) collective-permute-start(f32[14,128]{1,0:T(8,128)S(1)} %get-tuple-element.14), channel_id=1, source_target_pairs={{0,8},{8,0},{1,9},{9,1},{2,10},{10,2},{3,11},{11,3},{4,12},{12,4},... | collective-permute-start | bytes 21512 | tf_op jit(solution)/shard_map/ppermute | solution.py:196
  164.9 1.0 collective-permute-done.8
  166.0 0.6 maximum_select_fusion
  166.6 11.1 %all-to-all-done.5 = bf16[16,128,128]{2,1,0:T(8,128)(2,1)S(1)} async-done(((bf16[16,128,128]{2,1,0:T(8,128)(2,1)}), bf16[16,128,128]{2,1,0:T(8,128)(2,1)S(1)}, u32[]{:S(2)}, u32[]{:S(2)}) %all-to-all-start.5) | async-done | bytes 524320 | tf_op jit(solution)/shard_map/all_to_all | solution.py:21
  177.7 0.7 shard_map.65
  (6 shorter events, 0.2 us)
Async XLA Ops:
  4.1 12.0 %copy-start = (bf16[1,896,1024]{2,1,0:T(8,128)(2,1)S(1)}, bf16[1,896,1024]{2,1,0:T(8,128)(2,1)}, u32[]{:S(2)}) copy-start(bf16[1,896,1024]{2,1,0:T(8,128)(2,1)} %param.6) | copy-start | bytes 5505028
  4.1 14.5 %copy-start.1 = (bf16[896,256]{1,0:T(8,128)(2,1)S(1)}, bf16[896,256]{1,0:T(8,128)(2,1)}, u32[]{:S(2)}) copy-start(bf16[896,256]{1,0:T(8,128)(2,1)} %probe_ref.1) | copy-start | bytes 1376260
  4.1 63.2 %all-to-all-start = ((bf16[64,16,1024]{2,1,0:T(8,128)(2,1)}), bf16[64,16,1024]{2,1,0:T(8,128)(2,1)}, u32[]{:S(2)}, u32[]{:S(2)}) async-start(bf16[64,16,1024]{2,1,0:T(8,128)(2,1)} %bitcast.24), calls=%async_computation | async-start | bytes 4194304 | tf_op jit(solution)/shard_map/all_to_all | solution.py:21
  16.1 42.8 %collective-permute-start = (bf16[896,1024]{1,0:T(8,128)(2,1)S(1)}, bf16[896,1024]{1,0:T(8,128)(2,1)}, u32[]{:S(2)}, u32[]{:S(2)}) collective-permute-start(bf16[896,1024]{1,0:T(8,128)(2,1)S(1)} %bitcast.18), channel_id=1, source_target_pairs={{0,8},{8,0},{1,9},{9,1},{2,10},{10,2},{3,11},{11,3},{4,12},{12,4},... | collective-permute-start | bytes 5505032 | tf_op jit(solution)/shard_map/ppermute | solution.py:196
  19.4 11.7 %collective-permute-start.3 = (bf16[256,256]{1,0:T(8,128)(2,1)S(1)}, bf16[256,256]{1,0:T(8,128)(2,1)S(1)}, u32[]{:S(2)}, u32[]{:S(2)}) collective-permute-start(bf16[256,256]{1,0:T(8,128)(2,1)S(1)} %get-tuple-element.11), channel_id=1, source_target_pairs={{0,3},{1,2},{2,1},{3,0},{4,7},{5,6},{6,5},{7,4},{8,11},{9,10},{10,... | collective-permute-start | bytes 393224 | tf_op jit(solution)/shard_map/ppermute | solution.py:196
  27.0 10.6 %collective-permute-start.2 = (bf16[256,256]{1,0:T(8,128)(2,1)S(1)}, bf16[256,256]{1,0:T(8,128)(2,1)S(1)}, u32[]{:S(2)}, u32[]{:S(2)}) collective-permute-start(bf16[256,256]{1,0:T(8,128)(2,1)S(1)} %get-tuple-element.12), channel_id=1, source_target_pairs={{0,2},{1,3},{2,0},{3,1},{4,6},{5,7},{6,4},{7,5},{8,10},{9,11},{10,... | collective-permute-start | bytes 393224 | tf_op jit(solution)/shard_map/ppermute | solution.py:196
  28.9 9.6 %collective-permute-start.1 = (bf16[256,256]{1,0:T(8,128)(2,1)S(1)}, bf16[256,256]{1,0:T(8,128)(2,1)S(1)}, u32[]{:S(2)}, u32[]{:S(2)}) collective-permute-start(bf16[256,256]{1,0:T(8,128)(2,1)S(1)} %get-tuple-element.10), channel_id=1, source_target_pairs={{0,1},{1,0},{2,3},{3,2},{4,5},{5,4},{6,7},{7,6},{8,9},{9,8},{10,11... | collective-permute-start | bytes 393224 | tf_op jit(solution)/shard_map/ppermute | solution.py:196
  38.6 10.9 %collective-permute-start.4 = (bf16[256,256]{1,0:T(8,128)(2,1)S(1)}, bf16[256,256]{1,0:T(8,128)(2,1)S(1)}, u32[]{:S(2)}, u32[]{:S(2)}) collective-permute-start(bf16[256,256]{1,0:T(8,128)(2,1)S(1)} %fusion), channel_id=1, source_target_pairs={{0,4},{1,5},{2,6},{3,7},{4,0},{5,1},{6,2},{7,3},{8,12},{9,13},{10,... | collective-permute-start | bytes 393224 | tf_op jit(solution)/shard_map/ppermute | solution.py:196
  49.5 17.8 %collective-permute-start.5 = (bf16[256,256]{1,0:T(8,128)(2,1)S(1)}, bf16[256,256]{1,0:T(8,128)(2,1)S(1)}, u32[]{:S(2)}, u32[]{:S(2)}) collective-permute-start(bf16[256,256]{1,0:T(8,128)(2,1)S(1)} %add_convert_fusion.proj0), channel_id=1, source_target_pairs={{0,3},{1,2},{2,1},{3,0},{4,7},{5,6},{6,5},{7,4},{8,11},{9,10},{10,... | collective-permute-start | bytes 393224 | tf_op jit(solution)/shard_map/ppermute | solution.py:196
  53.6 13.7 %collective-permute-start.6 = (bf16[256,256]{1,0:T(8,128)(2,1)S(1)}, bf16[256,256]{1,0:T(8,128)(2,1)S(1)}, u32[]{:S(2)}, u32[]{:S(2)}) collective-permute-start(bf16[256,256]{1,0:T(8,128)(2,1)S(1)} %add_convert_fusion.proj0), channel_id=1, source_target_pairs={{0,2},{1,3},{2,0},{3,1},{4,6},{5,7},{6,4},{7,5},{8,10},{9,11},{10,... | collective-permute-start | bytes 393224 | tf_op jit(solution)/shard_map/ppermute | solution.py:196
  55.5 11.8 %collective-permute-start.7 = (bf16[256,256]{1,0:T(8,128)(2,1)S(1)}, bf16[256,256]{1,0:T(8,128)(2,1)S(1)}, u32[]{:S(2)}, u32[]{:S(2)}) collective-permute-start(bf16[256,256]{1,0:T(8,128)(2,1)S(1)} %add_convert_fusion.proj0), channel_id=1, source_target_pairs={{0,1},{1,0},{2,3},{3,2},{4,5},{5,4},{6,7},{7,6},{8,9},{9,8},{10,11... | collective-permute-start | bytes 393224 | tf_op jit(solution)/shard_map/ppermute | solution.py:196
  97.5 20.1 %all-to-all-start.2 = ((bf16[16,128,128]{2,1,0:T(8,128)(2,1)}), bf16[16,128,128]{2,1,0:T(8,128)(2,1)S(1)}, u32[]{:S(2)}, u32[]{:S(2)}) async-start(bf16[16,128,128]{2,1,0:T(8,128)(2,1)} %bitcast.10), calls=%async_computation.2 | async-start | bytes 1048576 | tf_op jit(solution)/shard_map/all_to_all | solution.py:21
  153.6 24.1 %all-to-all-start.5 = ((bf16[16,128,128]{2,1,0:T(8,128)(2,1)}), bf16[16,128,128]{2,1,0:T(8,128)(2,1)S(1)}, u32[]{:S(2)}, u32[]{:S(2)}) async-start(bf16[16,128,128]{2,1,0:T(8,128)(2,1)} %bitcast.12), calls=%async_computation.5 | async-start | bytes 1048576 | tf_op jit(solution)/shard_map/all_to_all | solution.py:21
  162.9 3.1 %collective-permute-start.8 = (f32[14,128]{1,0:T(8,128)S(1)}, f32[14,128]{1,0:T(8,128)S(1)}, u32[]{:S(2)}, u32[]{:S(2)}) collective-permute-start(f32[14,128]{1,0:T(8,128)S(1)} %get-tuple-element.14), channel_id=1, source_target_pairs={{0,8},{8,0},{1,9},{9,1},{2,10},{10,2},{3,11},{11,3},{4,12},{12,4},... | collective-permute-start | bytes 21512 | tf_op jit(solution)/shard_map/ppermute | solution.py:196

commit v6 on v5

--- a/solution.py
+++ b/solution.py
@@ -62,14 +62,13 @@
 
     spread = flag(iota((top, count), 0) == iota((top, count), 1) % top)
     token = flag(iota((tokens, count), 0) == iota((tokens, count), 1) // top)
-    earlier = flag(iota((tokens, tokens), 0) < iota((tokens, tokens), 1))
+    earlier = flag(iota((count, count), 0) < iota((count, count), 1))
     names.wait()
     spelled = contract(routes_ref[...].astype(F32).astype(BF16), spread, 0, 0)
     expert = jnp.sum(spelled * token.astype(F32), axis=0, keepdims=True).astype(jnp.int32)
     named = flag(iota((experts, count), 0) == expert)
-    by_token = contract(named, token, 1, 1).astype(BF16)
-    before = jnp.dot(by_token, earlier, preferred_element_type=F32).astype(BF16)
-    position = jnp.sum(jnp.dot(before, token, preferred_element_type=F32) * named.astype(F32), axis=0, keepdims=True)
+    before = jnp.dot(named, earlier, preferred_element_type=F32)
+    position = jnp.sum(before * named.astype(F32), axis=0, keepdims=True)
     slot = expert * capacity + position.astype(jnp.int32)
 
     block = 256
@@ -231,7 +230,7 @@
     quarters = [across(proj, "z", nz, step) for step in (1, 2, 3)]
     neighbour = across(weight, "c", nc, 1)
 
-    rows, neighbour = lax.optimization_barrier((rows, neighbour))
+    rows, neighbour, core = lax.optimization_barrier((rows, neighbour, core))
 
     gram_part = call(
         gram_kernel,

time: 179 us -> 177 us (0.989)
  blocking collectives: 56.2 us -> 75.3 us
  waiting for transfers between devices: 45.7 us -> 30.9 us
  starting transfers between devices: 60 us -> 54.7 us
    all_to_all x3 -> x4, blocking collectives: 56.2 us -> 75.3 us  [swap(): return lax.all_to_all(value, axes, split_axis=0, concat_axis=0, tiled=False)]
    all_to_all x3 -> x2, waiting for transfers between devices: 34.3 us -> 19.6 us  [swap(): return lax.all_to_all(value, axes, split_axis=0, concat_axis=0, tiled=False)]
    all_to_all x3 -> x2, starting transfers between devices: 26.6 us -> 21.3 us  [swap(): return lax.all_to_all(value, axes, split_axis=0, concat_axis=0, tiled=False)]
  transfers between devices with their start and end apart: 12 -> 11, of which waited for: 7 -> 6; matrix products, arithmetic and copies ran while one was open for 0% -> 0% of each run, Pallas kernels for 0% -> 0%
where the time goes in v6:
time: 177 us
  blocking collectives  75.3 us (43%)
  starting transfers between devices  54.7 us (31%)
  waiting for transfers between devices  30.9 us (17%)
  Pallas kernels  13.8 us (8%)
    all_to_all x4, blocking collectives, swap(): return lax.all_to_all(value, axes, split_axis=0, concat_axis=0, tiled=False)  75.3 us
    ppermute x9, starting transfers between devices, across(): return lax.ppermute(value, axis, [(i, i ^ step) for i in range(size)])  33.4 us
    all_to_all x2, starting transfers between devices, swap(): return lax.all_to_all(value, axes, split_axis=0, concat_axis=0, tiled=False)  21.3 us
    all_to_all x2, waiting for transfers between devices, swap(): return lax.all_to_all(value, axes, split_axis=0, concat_axis=0, tiled=False)  19.6 us
    pallas_call x7, Pallas kernels, call(): pl.pallas_call(kernel, out_shape=outs, in_specs=in_specs or [VMEM] * len(...  13.8 us
    ppermute x9, waiting for transfers between devices, across(): return lax.ppermute(value, axis, [(i, i ^ step) for i in range(size)])  11.3 us
  transfers between devices with their start and end apart: 11, of which 6 were waited for; matrix products, arithmetic and copies ran while one was open for 0% of the time, Pallas kernels for 0%

profile of v6, /device:TPU:1, one launch (start us, length us, event | category | flops | bytes accessed | tf_op | source)
XLA Modules:
  0.0 176.6 jit_solution(11486735238973415594)
XLA Ops:
  0.6 3.4 %shard_map.59 = bf16[1024,1024]{1,0:T(8,128)(2,1)} custom-call(s32[8,64]{1,0:T(8,128)} %bitcast.28, bf16[512,1024]{1,0:T(8,128)(2,1)} %bitcast.27), custom_call_target="tpu_custom_call" | custom-call | flops 1073741824 | bytes 3147776 | tf_op jit(solution)/shard_map/pallas_call | solution.py:36
  4.0 0.0 copy-start
  4.0 0.0 copy-start.1
  4.0 12.0 %all-to-all-start = ((bf16[64,16,1024]{2,1,0:T(8,128)(2,1)}), bf16[64,16,1024]{2,1,0:T(8,128)(2,1)}, u32[]{:S(2)}, u32[]{:S(2)}) async-start(bf16[64,16,1024]{2,1,0:T(8,128)(2,1)} %bitcast.25), calls=%async_computation | async-start | bytes 4194304 | tf_op jit(solution)/shard_map/all_to_all | solution.py:21
  16.0 0.0 copy-done
  16.0 2.5 %collective-permute-start = (bf16[896,1024]{1,0:T(8,128)(2,1)S(1)}, bf16[896,1024]{1,0:T(8,128)(2,1)}, u32[]{:S(2)}, u32[]{:S(2)}) collective-permute-start(bf16[896,1024]{1,0:T(8,128)(2,1)S(1)} %bitcast.18), channel_id=1, source_target_pairs={{0,8},{8,0},{1,9},{9,1},{2,10},{10,2},{3,11},{11,3},{4,12},{12,4},... | collective-permute-start | bytes 5505032 | tf_op jit(solution)/shard_map/ppermute | solution.py:195
  18.5 0.0 copy-done.1
  18.6 0.8 shard_map.60
  19.4 7.5 %collective-permute-start.3 = (bf16[256,256]{1,0:T(8,128)(2,1)S(1)}, bf16[256,256]{1,0:T(8,128)(2,1)S(1)}, u32[]{:S(2)}, u32[]{:S(2)}) collective-permute-start(bf16[256,256]{1,0:T(8,128)(2,1)S(1)} %get-tuple-element.13), channel_id=1, source_target_pairs={{0,3},{1,2},{2,1},{3,0},{4,7},{5,6},{6,5},{7,4},{8,11},{9,10},{10,... | collective-permute-start | bytes 393224 | tf_op jit(solution)/shard_map/ppermute | solution.py:195
  26.9 1.9 %collective-permute-start.2 = (bf16[256,256]{1,0:T(8,128)(2,1)S(1)}, bf16[256,256]{1,0:T(8,128)(2,1)S(1)}, u32[]{:S(2)}, u32[]{:S(2)}) collective-permute-start(bf16[256,256]{1,0:T(8,128)(2,1)S(1)} %get-tuple-element.14), channel_id=1, source_target_pairs={{0,2},{1,3},{2,0},{3,1},{4,6},{5,7},{6,4},{7,5},{8,10},{9,11},{10,... | collective-permute-start | bytes 393224 | tf_op jit(solution)/shard_map/ppermute | solution.py:195
  28.8 2.2 %collective-permute-start.1 = (bf16[256,256]{1,0:T(8,128)(2,1)S(1)}, bf16[256,256]{1,0:T(8,128)(2,1)S(1)}, u32[]{:S(2)}, u32[]{:S(2)}) collective-permute-start(bf16[256,256]{1,0:T(8,128)(2,1)S(1)} %get-tuple-element.12), channel_id=1, source_target_pairs={{0,1},{1,0},{2,3},{3,2},{4,5},{5,4},{6,7},{7,6},{8,9},{9,8},{10,11... | collective-permute-start | bytes 393224 | tf_op jit(solution)/shard_map/ppermute | solution.py:195
  31.0 0.0 collective-permute-done.3
  31.0 6.5 %collective-permute-done.2 = bf16[256,256]{1,0:T(8,128)(2,1)S(1)} collective-permute-done((bf16[256,256]{1,0:T(8,128)(2,1)S(1)}, bf16[256,256]{1,0:T(8,128)(2,1)S(1)}, u32[]{:S(2)}, u32[]{:S(2)}) %collective-permute-start.2) | collective-permute-done | bytes 131104 | tf_op jit(solution)/shard_map/ppermute | solution.py:195
  37.5 0.9 collective-permute-done.1
  38.4 0.1 fusion
  38.5 8.0 %collective-permute-start.4 = (bf16[256,256]{1,0:T(8,128)(2,1)S(1)}, bf16[256,256]{1,0:T(8,128)(2,1)S(1)}, u32[]{:S(2)}, u32[]{:S(2)}) collective-permute-start(bf16[256,256]{1,0:T(8,128)(2,1)S(1)} %fusion), channel_id=1, source_target_pairs={{0,4},{1,5},{2,6},{3,7},{4,0},{5,1},{6,2},{7,3},{8,12},{9,13},{10,... | collective-permute-start | bytes 393224 | tf_op jit(solution)/shard_map/ppermute | solution.py:195
  46.5 2.9 %collective-permute-done.4 = bf16[256,256]{1,0:T(8,128)(2,1)S(1)} collective-permute-done((bf16[256,256]{1,0:T(8,128)(2,1)S(1)}, bf16[256,256]{1,0:T(8,128)(2,1)S(1)}, u32[]{:S(2)}, u32[]{:S(2)}) %collective-permute-start.4) | collective-permute-done | bytes 131104 | tf_op jit(solution)/shard_map/ppermute | solution.py:195
  49.4 0.1 add_convert_fusion.proj0
  49.5 4.1 %collective-permute-start.5 = (bf16[256,256]{1,0:T(8,128)(2,1)S(1)}, bf16[256,256]{1,0:T(8,128)(2,1)S(1)}, u32[]{:S(2)}, u32[]{:S(2)}) collective-permute-start(bf16[256,256]{1,0:T(8,128)(2,1)S(1)} %add_convert_fusion.proj0), channel_id=1, source_target_pairs={{0,3},{1,2},{2,1},{3,0},{4,7},{5,6},{6,5},{7,4},{8,11},{9,10},{10,... | collective-permute-start | bytes 393224 | tf_op jit(solution)/shard_map/ppermute | solution.py:195
  53.6 1.9 %collective-permute-start.6 = (bf16[256,256]{1,0:T(8,128)(2,1)S(1)}, bf16[256,256]{1,0:T(8,128)(2,1)S(1)}, u32[]{:S(2)}, u32[]{:S(2)}) collective-permute-start(bf16[256,256]{1,0:T(8,128)(2,1)S(1)} %add_convert_fusion.proj0), channel_id=1, source_target_pairs={{0,2},{1,3},{2,0},{3,1},{4,6},{5,7},{6,4},{7,5},{8,10},{9,11},{10,... | collective-permute-start | bytes 393224 | tf_op jit(solution)/shard_map/ppermute | solution.py:195
  55.5 3.2 %collective-permute-start.7 = (bf16[256,256]{1,0:T(8,128)(2,1)S(1)}, bf16[256,256]{1,0:T(8,128)(2,1)S(1)}, u32[]{:S(2)}, u32[]{:S(2)}) collective-permute-start(bf16[256,256]{1,0:T(8,128)(2,1)S(1)} %add_convert_fusion.proj0), channel_id=1, source_target_pairs={{0,1},{1,0},{2,3},{3,2},{4,5},{5,4},{6,7},{7,6},{8,9},{9,8},{10,11... | collective-permute-start | bytes 393224 | tf_op jit(solution)/shard_map/ppermute | solution.py:195
  58.8 0.0 collective-permute-done.other_hbm
  58.8 8.5 %all-to-all-done = bf16[64,16,1024]{2,1,0:T(8,128)(2,1)} async-done(((bf16[64,16,1024]{2,1,0:T(8,128)(2,1)}), bf16[64,16,1024]{2,1,0:T(8,128)(2,1)}, u32[]{:S(2)}, u32[]{:S(2)}) %all-to-all-start) | async-done | bytes 2097184 | tf_op jit(solution)/shard_map/all_to_all | solution.py:21
  67.2 0.0 collective-permute-done.5.proj3
  67.2 0.0 collective-permute-done.6.proj2
  67.2 0.0 collective-permute-done.7.proj1
  67.2 2.9 %shard_map.61 = bf16[8,256,128]{2,1,0:T(8,128)(2,1)S(1)} custom-call(s32[1]{0:T(128)} %bitcast.6.quarter_ref, bf16[1024,1024]{1,0:T(8,128)(2,1)} %bitcast.3.rows_ref, bf16[256,256]{1,0:T(8,128)(2,1)S(1)} %collective-permute-done.5.proj3, bf16[256,256]{1,0:T(8,128)(2,1)S(1)} %collective-permute-done.6.proj2, ...), custom_call_target="tpu_custom_call" | custom-call | flops 1073741824 | bytes 3145732 | tf_op jit(solution)/shard_map/pallas_call | solution.py:36
  70.2 26.3 %all_to_all.30.parts_ref = bf16[8,256,128]{2,1,0:T(8,128)(2,1)S(1)} all-to-all(bf16[8,256,128]{2,1,0:T(8,128)(2,1)S(1)} %shard_map.61), channel_id=1, replica_groups=mesh['x'=4,'y'=8,'c'=2,'z'=8] {'z'}, dimensions={0} | all-to-all | bytes 1048576 | tf_op jit(solution)/shard_map/all_to_all | solution.py:21
  96.5 0.2 shard_map.62
  96.6 19.2 %all_to_all.31 = bf16[16,128,128]{2,1,0:T(8,128)(2,1)S(1)} all-to-all(bf16[16,128,128]{2,1,0:T(8,128)(2,1)S(1)} %bitcast.24), channel_id=1, replica_groups=mesh['x'=4,'y'=8,'c'=2,'z'=8] {'c','z'}, dimensions={0} | all-to-all | bytes 1048576 | tf_op jit(solution)/shard_map/all_to_all | solution.py:21
  115.8 2.7 %shard_map.63 = bf16[896,128]{1,0:T(8,128)(2,1)S(1)} custom-call(s32[1]{0:T(128)} %bitcast.5.core_ref, bf16[896,1024]{1,0:T(8,128)(2,1)S(1)} %bitcast.20, bf16[896,1024]{1,0:T(8,128)(2,1)} %collective-permute-done.other_hbm, bf16[2,1024,128]{2,1,0:T(8,128)(2,1)S(1)} %bitcast.22), custom_call_target="tpu_custom_call" | custom-call | flops 469762048 | bytes 4423684 | tf_op jit(solution)/shard_map/pallas_call | solution.py:36
  118.5 14.3 %all_to_all.32 = bf16[32,28,128]{2,1,0:T(8,128)(2,1)S(1)} all-to-all(bf16[32,28,128]{2,1,0:T(8,128)(2,1)S(1)} %reshape.39), channel_id=1, replica_groups=mesh['x'=4,'y'=8,'c'=2,'z'=8] {'x','y'}, dimensions={0} | all-to-all | bytes 458752 | tf_op jit(solution)/shard_map/all_to_all | solution.py:21
  132.9 0.1 convert_reduce_fusion
  133.0 15.5 %all_to_all.33 = bf16[32,28,128]{2,1,0:T(8,128)(2,1)S(1)} all-to-all(bf16[32,28,128]{2,1,0:T(8,128)(2,1)S(1)} %broadcast_in_dim.18), channel_id=1, replica_groups=mesh['x'=4,'y'=8,'c'=2,'z'=8] {'x','y'}, dimensions={0} | all-to-all | bytes 458752 | tf_op jit(solution)/shard_map/all_to_all | solution.py:21
  148.6 3.2 %shard_map.64 = bf16[2,8,128,128]{3,2,1,0:T(8,128)(2,1)} custom-call(s32[1]{0:T(128)} %bitcast.5.core_ref, bf16[896,1024]{1,0:T(8,128)(2,1)S(1)} %bitcast.21, bf16[896,1024]{1,0:T(8,128)(2,1)} %collective-permute-done.other_hbm, bf16[896,128]{1,0:T(8,128)(2,1)S(1)} %reshape.40.basis_ref), custom_call_target="tpu_custom_call" | custom-call | flops 469762048 | bytes 4423684 | tf_op jit(solution)/shard_map/pallas_call | solution.py:36
  151.8 9.3 %all-to-all-start.5 = ((bf16[16,128,128]{2,1,0:T(8,128)(2,1)}), bf16[16,128,128]{2,1,0:T(8,128)(2,1)S(1)}, u32[]{:S(2)}, u32[]{:S(2)}) async-start(bf16[16,128,128]{2,1,0:T(8,128)(2,1)} %bitcast.12), calls=%async_computation.5 | async-start | bytes 1048576 | tf_op jit(solution)/shard_map/all_to_all | solution.py:21
  161.1 2.0 %collective-permute-start.8 = (f32[14,128]{1,0:T(8,128)S(1)}, f32[14,128]{1,0:T(8,128)S(1)}, u32[]{:S(2)}, u32[]{:S(2)}) collective-permute-start(f32[14,128]{1,0:T(8,128)S(1)} %get-tuple-element.16), channel_id=1, source_target_pairs={{0,8},{8,0},{1,9},{9,1},{2,10},{10,2},{3,11},{11,3},{4,12},{12,4},... | collective-permute-start | bytes 21512 | tf_op jit(solution)/shard_map/ppermute | solution.py:195
  163.2 1.0 collective-permute-done.8
  164.2 0.6 maximum_select_fusion
  164.8 11.1 %all-to-all-done.5 = bf16[16,128,128]{2,1,0:T(8,128)(2,1)S(1)} async-done(((bf16[16,128,128]{2,1,0:T(8,128)(2,1)}), bf16[16,128,128]{2,1,0:T(8,128)(2,1)S(1)}, u32[]{:S(2)}, u32[]{:S(2)}) %all-to-all-start.5) | async-done | bytes 524320 | tf_op jit(solution)/shard_map/all_to_all | solution.py:21
  175.9 0.7 shard_map.65
  (6 shorter events, 0.2 us)
Async XLA Ops:
  4.0 12.0 %copy-start = (bf16[1,896,1024]{2,1,0:T(8,128)(2,1)S(1)}, bf16[1,896,1024]{2,1,0:T(8,128)(2,1)}, u32[]{:S(2)}) copy-start(bf16[1,896,1024]{2,1,0:T(8,128)(2,1)} %param.6) | copy-start | bytes 5505028
  4.0 14.5 %copy-start.1 = (bf16[896,256]{1,0:T(8,128)(2,1)S(1)}, bf16[896,256]{1,0:T(8,128)(2,1)}, u32[]{:S(2)}) copy-start(bf16[896,256]{1,0:T(8,128)(2,1)} %probe_ref.1) | copy-start | bytes 1376260
  4.0 63.2 %all-to-all-start = ((bf16[64,16,1024]{2,1,0:T(8,128)(2,1)}), bf16[64,16,1024]{2,1,0:T(8,128)(2,1)}, u32[]{:S(2)}, u32[]{:S(2)}) async-start(bf16[64,16,1024]{2,1,0:T(8,128)(2,1)} %bitcast.25), calls=%async_computation | async-start | bytes 4194304 | tf_op jit(solution)/shard_map/all_to_all | solution.py:21
  16.0 42.8 %collective-permute-start = (bf16[896,1024]{1,0:T(8,128)(2,1)S(1)}, bf16[896,1024]{1,0:T(8,128)(2,1)}, u32[]{:S(2)}, u32[]{:S(2)}) collective-permute-start(bf16[896,1024]{1,0:T(8,128)(2,1)S(1)} %bitcast.18), channel_id=1, source_target_pairs={{0,8},{8,0},{1,9},{9,1},{2,10},{10,2},{3,11},{11,3},{4,12},{12,4},... | collective-permute-start | bytes 5505032 | tf_op jit(solution)/shard_map/ppermute | solution.py:195
  19.4 11.7 %collective-permute-start.3 = (bf16[256,256]{1,0:T(8,128)(2,1)S(1)}, bf16[256,256]{1,0:T(8,128)(2,1)S(1)}, u32[]{:S(2)}, u32[]{:S(2)}) collective-permute-start(bf16[256,256]{1,0:T(8,128)(2,1)S(1)} %get-tuple-element.13), channel_id=1, source_target_pairs={{0,3},{1,2},{2,1},{3,0},{4,7},{5,6},{6,5},{7,4},{8,11},{9,10},{10,... | collective-permute-start | bytes 393224 | tf_op jit(solution)/shard_map/ppermute | solution.py:195
  26.9 10.6 %collective-permute-start.2 = (bf16[256,256]{1,0:T(8,128)(2,1)S(1)}, bf16[256,256]{1,0:T(8,128)(2,1)S(1)}, u32[]{:S(2)}, u32[]{:S(2)}) collective-permute-start(bf16[256,256]{1,0:T(8,128)(2,1)S(1)} %get-tuple-element.14), channel_id=1, source_target_pairs={{0,2},{1,3},{2,0},{3,1},{4,6},{5,7},{6,4},{7,5},{8,10},{9,11},{10,... | collective-permute-start | bytes 393224 | tf_op jit(solution)/shard_map/ppermute | solution.py:195
  28.8 9.6 %collective-permute-start.1 = (bf16[256,256]{1,0:T(8,128)(2,1)S(1)}, bf16[256,256]{1,0:T(8,128)(2,1)S(1)}, u32[]{:S(2)}, u32[]{:S(2)}) collective-permute-start(bf16[256,256]{1,0:T(8,128)(2,1)S(1)} %get-tuple-element.12), channel_id=1, source_target_pairs={{0,1},{1,0},{2,3},{3,2},{4,5},{5,4},{6,7},{7,6},{8,9},{9,8},{10,11... | collective-permute-start | bytes 393224 | tf_op jit(solution)/shard_map/ppermute | solution.py:195
  38.5 10.9 %collective-permute-start.4 = (bf16[256,256]{1,0:T(8,128)(2,1)S(1)}, bf16[256,256]{1,0:T(8,128)(2,1)S(1)}, u32[]{:S(2)}, u32[]{:S(2)}) collective-permute-start(bf16[256,256]{1,0:T(8,128)(2,1)S(1)} %fusion), channel_id=1, source_target_pairs={{0,4},{1,5},{2,6},{3,7},{4,0},{5,1},{6,2},{7,3},{8,12},{9,13},{10,... | collective-permute-start | bytes 393224 | tf_op jit(solution)/shard_map/ppermute | solution.py:195
  49.5 17.8 %collective-permute-start.5 = (bf16[256,256]{1,0:T(8,128)(2,1)S(1)}, bf16[256,256]{1,0:T(8,128)(2,1)S(1)}, u32[]{:S(2)}, u32[]{:S(2)}) collective-permute-start(bf16[256,256]{1,0:T(8,128)(2,1)S(1)} %add_convert_fusion.proj0), channel_id=1, source_target_pairs={{0,3},{1,2},{2,1},{3,0},{4,7},{5,6},{6,5},{7,4},{8,11},{9,10},{10,... | collective-permute-start | bytes 393224 | tf_op jit(solution)/shard_map/ppermute | solution.py:195
  53.6 13.7 %collective-permute-start.6 = (bf16[256,256]{1,0:T(8,128)(2,1)S(1)}, bf16[256,256]{1,0:T(8,128)(2,1)S(1)}, u32[]{:S(2)}, u32[]{:S(2)}) collective-permute-start(bf16[256,256]{1,0:T(8,128)(2,1)S(1)} %add_convert_fusion.proj0), channel_id=1, source_target_pairs={{0,2},{1,3},{2,0},{3,1},{4,6},{5,7},{6,4},{7,5},{8,10},{9,11},{10,... | collective-permute-start | bytes 393224 | tf_op jit(solution)/shard_map/ppermute | solution.py:195
  55.5 11.8 %collective-permute-start.7 = (bf16[256,256]{1,0:T(8,128)(2,1)S(1)}, bf16[256,256]{1,0:T(8,128)(2,1)S(1)}, u32[]{:S(2)}, u32[]{:S(2)}) collective-permute-start(bf16[256,256]{1,0:T(8,128)(2,1)S(1)} %add_convert_fusion.proj0), channel_id=1, source_target_pairs={{0,1},{1,0},{2,3},{3,2},{4,5},{5,4},{6,7},{7,6},{8,9},{9,8},{10,11... | collective-permute-start | bytes 393224 | tf_op jit(solution)/shard_map/ppermute | solution.py:195
  151.8 24.1 %all-to-all-start.5 = ((bf16[16,128,128]{2,1,0:T(8,128)(2,1)}), bf16[16,128,128]{2,1,0:T(8,128)(2,1)S(1)}, u32[]{:S(2)}, u32[]{:S(2)}) async-start(bf16[16,128,128]{2,1,0:T(8,128)(2,1)} %bitcast.12), calls=%async_computation.5 | async-start | bytes 1048576 | tf_op jit(solution)/shard_map/all_to_all | solution.py:21
  161.1 3.1 %collective-permute-start.8 = (f32[14,128]{1,0:T(8,128)S(1)}, f32[14,128]{1,0:T(8,128)S(1)}, u32[]{:S(2)}, u32[]{:S(2)}) collective-permute-start(f32[14,128]{1,0:T(8,128)S(1)} %get-tuple-element.16), channel_id=1, source_target_pairs={{0,8},{8,0},{1,9},{9,1},{2,10},{10,2},{3,11},{11,3},{4,12},{12,4},... | collective-permute-start | bytes 21512 | tf_op jit(solution)/shard_map/ppermute | solution.py:195

commit v7 on v6

--- a/solution.py
+++ b/solution.py
@@ -102,7 +102,8 @@
     quarter = quarter_ref[0]
     block = 256
     count, width = rows_ref.shape
-    size = out_ref.shape[2]
+    size = out_ref.shape[3]
+    half = out_ref.shape[2]
     depth = proj0.shape[0]
     for step, part in enumerate((proj0, proj1, proj2, proj3)):
         proj_ref[pl.ds(pl.multiple_of((quarter ^ step) * depth, depth), depth), :] = part[...]
@@ -115,16 +116,16 @@
     for i in range(0, width, block):
         part = jnp.dot(turned, rows_ref[:, i : i + block], preferred_element_type=F32).astype(BF16)
         for j in range(0, block, size):
-            out_ref[(i + j) // size] = part[:, j : j + size]
+            for core in range(out_ref.shape[0]):
+                out_ref[core, (i + j) // size] = part[core * half : (core + 1) * half, j : j + size]
 
 
 def share_kernel(scale, parts_ref, out_ref):
-    cores, devices, _, half = out_ref.shape
-    total = jnp.sum(parts_ref[...].astype(F32), axis=0) * scale
-    value = total.astype(BF16).T
-    for core in range(cores):
-        for device in range(devices):
-            out_ref[core, device] = value[:, core * half : (core + 1) * half]
+    for expert in range(parts_ref.shape[0]):
+        total = jnp.sum(parts_ref[expert].astype(F32), axis=0) * scale
+        value = total.astype(BF16).T
+        for device in range(out_ref.shape[0]):
+            out_ref[device, expert] = value
 
 
 def image_kernel(core_ref, own_ref, other_hbm, gram_ref, out_ref, other_ref, sems):
@@ -136,7 +137,7 @@
     ]
     for fetch in fetches:
         fetch.start()
-    own, other = gram_ref[core], gram_ref[1 - core]
+    own, other = (gram_ref[:, i].reshape(-1, gram_ref.shape[3]) for i in (core, 1 - core))
     for part, fetch in zip(parts, fetches):
         image = jnp.dot(own_ref[part, :], own, preferred_element_type=F32)
         fetch.wait()
@@ -234,20 +235,21 @@
 
     gram_part = call(
         gram_kernel,
-        [shape((nz, panel, block), BF16)],
+        [shape((nc, nz, half, block), BF16)],
         4 * slots * width * panel,
         [quarter, rows] + quarters[::-1] + [proj],
         [SMEM] + [VMEM] * 5,
         None,
         [pltpu.VMEM((width, panel), BF16)],
     )
+    arrived = swap(gram_part.reshape(nc * nz, half, block), ("c", "z")).reshape(nc, nz, half, block)
     copies = call(
         functools.partial(share_kernel, 1.0 / row_mean),
-        [shape((nc, nz, block, half), BF16)],
+        [shape((nz, nc, block, half), BF16)],
         nz * block * panel,
-        [swap(gram_part, "z")],
-    )
-    gram = swap(copies.reshape(nc * nz, block, half), ("c", "z")).reshape(nc, width, half)
+        [arrived],
+    )
+    gram = swap(copies, "z")
 
     image = call(
         image_kernel,

time: 177 us -> 176 us (level)
  no operation moved by 1% of the time
where the time goes in v7:
time: 176 us; the launch traced here: 175 us
  blocking collectives  75 us (43%)
  starting transfers between devices  53.7 us (31%)
  waiting for transfers between devices  30.8 us (18%)
  Pallas kernels  13.8 us (8%)
    all_to_all x4, blocking collectives, swap(): return lax.all_to_all(value, axes, split_axis=0, concat_axis=0, tiled=False)  75 us
    ppermute x9, starting transfers between devices, across(): return lax.ppermute(value, axis, [(i, i ^ step) for i in range(size)])  33.5 us
    all_to_all x2, starting transfers between devices, swap(): return lax.all_to_all(value, axes, split_axis=0, concat_axis=0, tiled=False)  20.2 us
    all_to_all x2, waiting for transfers between devices, swap(): return lax.all_to_all(value, axes, split_axis=0, concat_axis=0, tiled=False)  19.6 us
    pallas_call x7, Pallas kernels, call(): pl.pallas_call(kernel, out_shape=outs, in_specs=in_specs or [VMEM] * len(...  13.8 us
    ppermute x9, waiting for transfers between devices, across(): return lax.ppermute(value, axis, [(i, i ^ step) for i in range(size)])  11.3 us
  transfers between devices with their start and end apart: 11, of which 6 were waited for; matrix products, arithmetic and copies ran while one was open for 0% of the time, Pallas kernels for 0%

profile of v7, /device:TPU:1, one launch (start us, length us, event | category | flops | bytes accessed | tf_op | source)
XLA Modules:
  0.0 175.1 jit_solution(17097567562303214722)
XLA Ops:
  0.6 3.4 %shard_map.59 = bf16[1024,1024]{1,0:T(8,128)(2,1)} custom-call(s32[8,64]{1,0:T(8,128)} %bitcast.28, bf16[512,1024]{1,0:T(8,128)(2,1)} %bitcast.27), custom_call_target="tpu_custom_call" | custom-call | flops 1073741824 | bytes 3147776 | tf_op jit(solution)/shard_map/pallas_call | solution.py:36
  4.0 0.0 copy-start
  4.0 0.0 copy-start.1
  4.0 12.0 %all-to-all-start = ((bf16[64,16,1024]{2,1,0:T(8,128)(2,1)}), bf16[64,16,1024]{2,1,0:T(8,128)(2,1)}, u32[]{:S(2)}, u32[]{:S(2)}) async-start(bf16[64,16,1024]{2,1,0:T(8,128)(2,1)} %bitcast.25), calls=%async_computation | async-start | bytes 4194304 | tf_op jit(solution)/shard_map/all_to_all | solution.py:21
  16.0 0.0 copy-done
  16.0 2.5 %collective-permute-start = (bf16[896,1024]{1,0:T(8,128)(2,1)S(1)}, bf16[896,1024]{1,0:T(8,128)(2,1)}, u32[]{:S(2)}, u32[]{:S(2)}) collective-permute-start(bf16[896,1024]{1,0:T(8,128)(2,1)S(1)} %bitcast.18), channel_id=1, source_target_pairs={{0,8},{8,0},{1,9},{9,1},{2,10},{10,2},{3,11},{11,3},{4,12},{12,4},... | collective-permute-start | bytes 5505032 | tf_op jit(solution)/shard_map/ppermute | solution.py:196
  18.5 0.0 copy-done.1
  18.6 0.8 shard_map.60
  19.4 7.5 %collective-permute-start.3 = (bf16[256,256]{1,0:T(8,128)(2,1)S(1)}, bf16[256,256]{1,0:T(8,128)(2,1)S(1)}, u32[]{:S(2)}, u32[]{:S(2)}) collective-permute-start(bf16[256,256]{1,0:T(8,128)(2,1)S(1)} %get-tuple-element.13), channel_id=1, source_target_pairs={{0,3},{1,2},{2,1},{3,0},{4,7},{5,6},{6,5},{7,4},{8,11},{9,10},{10,... | collective-permute-start | bytes 393224 | tf_op jit(solution)/shard_map/ppermute | solution.py:196
  26.9 1.9 %collective-permute-start.2 = (bf16[256,256]{1,0:T(8,128)(2,1)S(1)}, bf16[256,256]{1,0:T(8,128)(2,1)S(1)}, u32[]{:S(2)}, u32[]{:S(2)}) collective-permute-start(bf16[256,256]{1,0:T(8,128)(2,1)S(1)} %get-tuple-element.14), channel_id=1, source_target_pairs={{0,2},{1,3},{2,0},{3,1},{4,6},{5,7},{6,4},{7,5},{8,10},{9,11},{10,... | collective-permute-start | bytes 393224 | tf_op jit(solution)/shard_map/ppermute | solution.py:196
  28.8 2.2 %collective-permute-start.1 = (bf16[256,256]{1,0:T(8,128)(2,1)S(1)}, bf16[256,256]{1,0:T(8,128)(2,1)S(1)}, u32[]{:S(2)}, u32[]{:S(2)}) collective-permute-start(bf16[256,256]{1,0:T(8,128)(2,1)S(1)} %get-tuple-element.12), channel_id=1, source_target_pairs={{0,1},{1,0},{2,3},{3,2},{4,5},{5,4},{6,7},{7,6},{8,9},{9,8},{10,11... | collective-permute-start | bytes 393224 | tf_op jit(solution)/shard_map/ppermute | solution.py:196
  31.0 0.0 collective-permute-done.3
  31.0 6.5 %collective-permute-done.2 = bf16[256,256]{1,0:T(8,128)(2,1)S(1)} collective-permute-done((bf16[256,256]{1,0:T(8,128)(2,1)S(1)}, bf16[256,256]{1,0:T(8,128)(2,1)S(1)}, u32[]{:S(2)}, u32[]{:S(2)}) %collective-permute-start.2) | collective-permute-done | bytes 131104 | tf_op jit(solution)/shard_map/ppermute | solution.py:196
  37.5 0.9 collective-permute-done.1
  38.4 0.1 fusion
  38.5 8.0 %collective-permute-start.4 = (bf16[256,256]{1,0:T(8,128)(2,1)S(1)}, bf16[256,256]{1,0:T(8,128)(2,1)S(1)}, u32[]{:S(2)}, u32[]{:S(2)}) collective-permute-start(bf16[256,256]{1,0:T(8,128)(2,1)S(1)} %fusion), channel_id=1, source_target_pairs={{0,4},{1,5},{2,6},{3,7},{4,0},{5,1},{6,2},{7,3},{8,12},{9,13},{10,... | collective-permute-start | bytes 393224 | tf_op jit(solution)/shard_map/ppermute | solution.py:196
  46.5 2.9 %collective-permute-done.4 = bf16[256,256]{1,0:T(8,128)(2,1)S(1)} collective-permute-done((bf16[256,256]{1,0:T(8,128)(2,1)S(1)}, bf16[256,256]{1,0:T(8,128)(2,1)S(1)}, u32[]{:S(2)}, u32[]{:S(2)}) %collective-permute-start.4) | collective-permute-done | bytes 131104 | tf_op jit(solution)/shard_map/ppermute | solution.py:196
  49.4 0.1 add_convert_fusion.proj0
  49.5 4.1 %collective-permute-start.5 = (bf16[256,256]{1,0:T(8,128)(2,1)S(1)}, bf16[256,256]{1,0:T(8,128)(2,1)S(1)}, u32[]{:S(2)}, u32[]{:S(2)}) collective-permute-start(bf16[256,256]{1,0:T(8,128)(2,1)S(1)} %add_convert_fusion.proj0), channel_id=1, source_target_pairs={{0,3},{1,2},{2,1},{3,0},{4,7},{5,6},{6,5},{7,4},{8,11},{9,10},{10,... | collective-permute-start | bytes 393224 | tf_op jit(solution)/shard_map/ppermute | solution.py:196
  53.6 1.9 %collective-permute-start.6 = (bf16[256,256]{1,0:T(8,128)(2,1)S(1)}, bf16[256,256]{1,0:T(8,128)(2,1)S(1)}, u32[]{:S(2)}, u32[]{:S(2)}) collective-permute-start(bf16[256,256]{1,0:T(8,128)(2,1)S(1)} %add_convert_fusion.proj0), channel_id=1, source_target_pairs={{0,2},{1,3},{2,0},{3,1},{4,6},{5,7},{6,4},{7,5},{8,10},{9,11},{10,... | collective-permute-start | bytes 393224 | tf_op jit(solution)/shard_map/ppermute | solution.py:196
  55.5 3.2 %collective-permute-start.7 = (bf16[256,256]{1,0:T(8,128)(2,1)S(1)}, bf16[256,256]{1,0:T(8,128)(2,1)S(1)}, u32[]{:S(2)}, u32[]{:S(2)}) collective-permute-start(bf16[256,256]{1,0:T(8,128)(2,1)S(1)} %add_convert_fusion.proj0), channel_id=1, source_target_pairs={{0,1},{1,0},{2,3},{3,2},{4,5},{5,4},{6,7},{7,6},{8,9},{9,8},{10,11... | collective-permute-start | bytes 393224 | tf_op jit(solution)/shard_map/ppermute | solution.py:196
  58.8 0.0 collective-permute-done.other_hbm
  58.8 8.5 %all-to-all-done = bf16[64,16,1024]{2,1,0:T(8,128)(2,1)} async-done(((bf16[64,16,1024]{2,1,0:T(8,128)(2,1)}), bf16[64,16,1024]{2,1,0:T(8,128)(2,1)}, u32[]{:S(2)}, u32[]{:S(2)}) %all-to-all-start) | async-done | bytes 2097184 | tf_op jit(solution)/shard_map/all_to_all | solution.py:21
  67.2 0.0 collective-permute-done.5.proj3
  67.2 0.0 collective-permute-done.6.proj2
  67.2 0.0 collective-permute-done.7.proj1
  67.2 2.9 %shard_map.61 = bf16[2,8,128,128]{3,2,1,0:T(8,128)(2,1)S(1)} custom-call(s32[1]{0:T(128)} %bitcast.6.quarter_ref, bf16[1024,1024]{1,0:T(8,128)(2,1)} %bitcast.3.rows_ref, bf16[256,256]{1,0:T(8,128)(2,1)S(1)} %collective-permute-done.5.proj3, bf16[256,256]{1,0:T(8,128)(2,1)S(1)} %collective-permute-done.6.proj2, ...), custom_call_target="tpu_custom_call" | custom-call | flops 1073741824 | bytes 3145732 | tf_op jit(solution)/shard_map/pallas_call | solution.py:36
  70.2 25.2 %all_to_all.30 = bf16[16,128,128]{2,1,0:T(8,128)(2,1)S(1)} all-to-all(bf16[16,128,128]{2,1,0:T(8,128)(2,1)S(1)} %bitcast.24), channel_id=1, replica_groups=mesh['x'=4,'y'=8,'c'=2,'z'=8] {'c','z'}, dimensions={0} | all-to-all | bytes 1048576 | tf_op jit(solution)/shard_map/all_to_all | solution.py:21
  95.4 0.2 shard_map.62
  95.6 20.8 %all_to_all.31.gram_ref = bf16[8,2,128,128]{3,2,1,0:T(8,128)(2,1)S(1)} all-to-all(bf16[8,2,128,128]{3,2,1,0:T(8,128)(2,1)S(1)} %shard_map.62), channel_id=1, replica_groups=mesh['x'=4,'y'=8,'c'=2,'z'=8] {'z'}, dimensions={0} | all-to-all | bytes 1048576 | tf_op jit(solution)/shard_map/all_to_all | solution.py:21
  116.3 2.7 %shard_map.63 = bf16[896,128]{1,0:T(8,128)(2,1)S(1)} custom-call(s32[1]{0:T(128)} %bitcast.5.core_ref, bf16[896,1024]{1,0:T(8,128)(2,1)S(1)} %bitcast.20, bf16[896,1024]{1,0:T(8,128)(2,1)} %collective-permute-done.other_hbm, bf16[8,2,128,128]{3,2,1,0:T(8,128)(2,1)S(1)} %all_to_all.31.gram_ref), custom_call_target="tpu_custom_call" | custom-call | flops 469762048 | bytes 4423684 | tf_op jit(solution)/shard_map/pallas_call | solution.py:36
  119.1 14.8 %all_to_all.32 = bf16[32,28,128]{2,1,0:T(8,128)(2,1)S(1)} all-to-all(bf16[32,28,128]{2,1,0:T(8,128)(2,1)S(1)} %reshape.39), channel_id=1, replica_groups=mesh['x'=4,'y'=8,'c'=2,'z'=8] {'x','y'}, dimensions={0} | all-to-all | bytes 458752 | tf_op jit(solution)/shard_map/all_to_all | solution.py:21
  133.9 0.1 convert_reduce_fusion
  134.0 14.2 %all_to_all.33 = bf16[32,28,128]{2,1,0:T(8,128)(2,1)S(1)} all-to-all(bf16[32,28,128]{2,1,0:T(8,128)(2,1)S(1)} %broadcast_in_dim.18), channel_id=1, replica_groups=mesh['x'=4,'y'=8,'c'=2,'z'=8] {'x','y'}, dimensions={0} | all-to-all | bytes 458752 | tf_op jit(solution)/shard_map/all_to_all | solution.py:21
  148.2 3.2 %shard_map.64 = bf16[2,8,128,128]{3,2,1,0:T(8,128)(2,1)} custom-call(s32[1]{0:T(128)} %bitcast.5.core_ref, bf16[896,1024]{1,0:T(8,128)(2,1)S(1)} %bitcast.21, bf16[896,1024]{1,0:T(8,128)(2,1)} %collective-permute-done.other_hbm, bf16[896,128]{1,0:T(8,128)(2,1)S(1)} %reshape.40.basis_ref), custom_call_target="tpu_custom_call" | custom-call | flops 469762048 | bytes 4423684 | tf_op jit(solution)/shard_map/pallas_call | solution.py:36
  151.4 8.2 %all-to-all-start.5 = ((bf16[16,128,128]{2,1,0:T(8,128)(2,1)}), bf16[16,128,128]{2,1,0:T(8,128)(2,1)S(1)}, u32[]{:S(2)}, u32[]{:S(2)}) async-start(bf16[16,128,128]{2,1,0:T(8,128)(2,1)} %bitcast.12), calls=%async_computation.5 | async-start | bytes 1048576 | tf_op jit(solution)/shard_map/all_to_all | solution.py:21
  159.7 2.1 %collective-permute-start.8 = (f32[14,128]{1,0:T(8,128)S(1)}, f32[14,128]{1,0:T(8,128)S(1)}, u32[]{:S(2)}, u32[]{:S(2)}) collective-permute-start(f32[14,128]{1,0:T(8,128)S(1)} %get-tuple-element.16), channel_id=1, source_target_pairs={{0,8},{8,0},{1,9},{9,1},{2,10},{10,2},{3,11},{11,3},{4,12},{12,4},... | collective-permute-start | bytes 21512 | tf_op jit(solution)/shard_map/ppermute | solution.py:196
  161.8 1.0 collective-permute-done.8
  162.7 0.6 maximum_select_fusion
  163.3 11.1 %all-to-all-done.5 = bf16[16,128,128]{2,1,0:T(8,128)(2,1)S(1)} async-done(((bf16[16,128,128]{2,1,0:T(8,128)(2,1)}), bf16[16,128,128]{2,1,0:T(8,128)(2,1)S(1)}, u32[]{:S(2)}, u32[]{:S(2)}) %all-to-all-start.5) | async-done | bytes 524320 | tf_op jit(solution)/shard_map/all_to_all | solution.py:21
  174.4 0.7 shard_map.65
  (6 shorter events, 0.2 us)
Async XLA Ops:
  4.0 12.0 %copy-start = (bf16[1,896,1024]{2,1,0:T(8,128)(2,1)S(1)}, bf16[1,896,1024]{2,1,0:T(8,128)(2,1)}, u32[]{:S(2)}) copy-start(bf16[1,896,1024]{2,1,0:T(8,128)(2,1)} %param.6) | copy-start | bytes 5505028
  4.0 14.5 %copy-start.1 = (bf16[896,256]{1,0:T(8,128)(2,1)S(1)}, bf16[896,256]{1,0:T(8,128)(2,1)}, u32[]{:S(2)}) copy-start(bf16[896,256]{1,0:T(8,128)(2,1)} %probe_ref.1) | copy-start | bytes 1376260
  4.0 63.2 %all-to-all-start = ((bf16[64,16,1024]{2,1,0:T(8,128)(2,1)}), bf16[64,16,1024]{2,1,0:T(8,128)(2,1)}, u32[]{:S(2)}, u32[]{:S(2)}) async-start(bf16[64,16,1024]{2,1,0:T(8,128)(2,1)} %bitcast.25), calls=%async_computation | async-start | bytes 4194304 | tf_op jit(solution)/shard_map/all_to_all | solution.py:21
  16.0 42.8 %collective-permute-start = (bf16[896,1024]{1,0:T(8,128)(2,1)S(1)}, bf16[896,1024]{1,0:T(8,128)(2,1)}, u32[]{:S(2)}, u32[]{:S(2)}) collective-permute-start(bf16[896,1024]{1,0:T(8,128)(2,1)S(1)} %bitcast.18), channel_id=1, source_target_pairs={{0,8},{8,0},{1,9},{9,1},{2,10},{10,2},{3,11},{11,3},{4,12},{12,4},... | collective-permute-start | bytes 5505032 | tf_op jit(solution)/shard_map/ppermute | solution.py:196
  19.4 11.7 %collective-permute-start.3 = (bf16[256,256]{1,0:T(8,128)(2,1)S(1)}, bf16[256,256]{1,0:T(8,128)(2,1)S(1)}, u32[]{:S(2)}, u32[]{:S(2)}) collective-permute-start(bf16[256,256]{1,0:T(8,128)(2,1)S(1)} %get-tuple-element.13), channel_id=1, source_target_pairs={{0,3},{1,2},{2,1},{3,0},{4,7},{5,6},{6,5},{7,4},{8,11},{9,10},{10,... | collective-permute-start | bytes 393224 | tf_op jit(solution)/shard_map/ppermute | solution.py:196
  26.9 10.6 %collective-permute-start.2 = (bf16[256,256]{1,0:T(8,128)(2,1)S(1)}, bf16[256,256]{1,0:T(8,128)(2,1)S(1)}, u32[]{:S(2)}, u32[]{:S(2)}) collective-permute-start(bf16[256,256]{1,0:T(8,128)(2,1)S(1)} %get-tuple-element.14), channel_id=1, source_target_pairs={{0,2},{1,3},{2,0},{3,1},{4,6},{5,7},{6,4},{7,5},{8,10},{9,11},{10,... | collective-permute-start | bytes 393224 | tf_op jit(solution)/shard_map/ppermute | solution.py:196
  28.8 9.6 %collective-permute-start.1 = (bf16[256,256]{1,0:T(8,128)(2,1)S(1)}, bf16[256,256]{1,0:T(8,128)(2,1)S(1)}, u32[]{:S(2)}, u32[]{:S(2)}) collective-permute-start(bf16[256,256]{1,0:T(8,128)(2,1)S(1)} %get-tuple-element.12), channel_id=1, source_target_pairs={{0,1},{1,0},{2,3},{3,2},{4,5},{5,4},{6,7},{7,6},{8,9},{9,8},{10,11... | collective-permute-start | bytes 393224 | tf_op jit(solution)/shard_map/ppermute | solution.py:196
  38.5 10.9 %collective-permute-start.4 = (bf16[256,256]{1,0:T(8,128)(2,1)S(1)}, bf16[256,256]{1,0:T(8,128)(2,1)S(1)}, u32[]{:S(2)}, u32[]{:S(2)}) collective-permute-start(bf16[256,256]{1,0:T(8,128)(2,1)S(1)} %fusion), channel_id=1, source_target_pairs={{0,4},{1,5},{2,6},{3,7},{4,0},{5,1},{6,2},{7,3},{8,12},{9,13},{10,... | collective-permute-start | bytes 393224 | tf_op jit(solution)/shard_map/ppermute | solution.py:196
  49.5 17.8 %collective-permute-start.5 = (bf16[256,256]{1,0:T(8,128)(2,1)S(1)}, bf16[256,256]{1,0:T(8,128)(2,1)S(1)}, u32[]{:S(2)}, u32[]{:S(2)}) collective-permute-start(bf16[256,256]{1,0:T(8,128)(2,1)S(1)} %add_convert_fusion.proj0), channel_id=1, source_target_pairs={{0,3},{1,2},{2,1},{3,0},{4,7},{5,6},{6,5},{7,4},{8,11},{9,10},{10,... | collective-permute-start | bytes 393224 | tf_op jit(solution)/shard_map/ppermute | solution.py:196
  53.6 13.7 %collective-permute-start.6 = (bf16[256,256]{1,0:T(8,128)(2,1)S(1)}, bf16[256,256]{1,0:T(8,128)(2,1)S(1)}, u32[]{:S(2)}, u32[]{:S(2)}) collective-permute-start(bf16[256,256]{1,0:T(8,128)(2,1)S(1)} %add_convert_fusion.proj0), channel_id=1, source_target_pairs={{0,2},{1,3},{2,0},{3,1},{4,6},{5,7},{6,4},{7,5},{8,10},{9,11},{10,... | collective-permute-start | bytes 393224 | tf_op jit(solution)/shard_map/ppermute | solution.py:196
  55.5 11.8 %collective-permute-start.7 = (bf16[256,256]{1,0:T(8,128)(2,1)S(1)}, bf16[256,256]{1,0:T(8,128)(2,1)S(1)}, u32[]{:S(2)}, u32[]{:S(2)}) collective-permute-start(bf16[256,256]{1,0:T(8,128)(2,1)S(1)} %add_convert_fusion.proj0), channel_id=1, source_target_pairs={{0,1},{1,0},{2,3},{3,2},{4,5},{5,4},{6,7},{7,6},{8,9},{9,8},{10,11... | collective-permute-start | bytes 393224 | tf_op jit(solution)/shard_map/ppermute | solution.py:196
  151.4 23.0 %all-to-all-start.5 = ((bf16[16,128,128]{2,1,0:T(8,128)(2,1)}), bf16[16,128,128]{2,1,0:T(8,128)(2,1)S(1)}, u32[]{:S(2)}, u32[]{:S(2)}) async-start(bf16[16,128,128]{2,1,0:T(8,128)(2,1)} %bitcast.12), calls=%async_computation.5 | async-start | bytes 1048576 | tf_op jit(solution)/shard_map/all_to_all | solution.py:21
  159.7 3.1 %collective-permute-start.8 = (f32[14,128]{1,0:T(8,128)S(1)}, f32[14,128]{1,0:T(8,128)S(1)}, u32[]{:S(2)}, u32[]{:S(2)}) collective-permute-start(f32[14,128]{1,0:T(8,128)S(1)} %get-tuple-element.16), channel_id=1, source_target_pairs={{0,8},{8,0},{1,9},{9,1},{2,10},{10,2},{3,11},{11,3},{4,12},{12,4},... | collective-permute-start | bytes 21512 | tf_op jit(solution)/shard_map/ppermute | solution.py:196

commit v8 on v7

--- a/solution.py
+++ b/solution.py
@@ -19,11 +19,6 @@
 
 def swap(value, axes):
     return lax.all_to_all(value, axes, split_axis=0, concat_axis=0, tiled=False)
-
-
-def share(value, axes, count):
-    copies = jnp.broadcast_to(value[None], (count,) + value.shape)
-    return swap(copies, axes).reshape(-1, value.shape[1])
 
 
 VMEM = pl.BlockSpec(memory_space=pltpu.VMEM)
@@ -145,30 +140,33 @@
         out_ref[part, :] = image.astype(BF16)
 
 
-def coef_kernel(core_ref, own_ref, other_hbm, basis_ref, out_hbm, other_ref, out_ref, in_sems, out_sems):
+def coef_kernel(core_ref, own_ref, other_hbm, basis_ref, out_ref, other_ref, sems):
     core = core_ref[0]
     size = out_ref.shape[3]
-    block = own_ref.shape[1] // in_sems.shape[0]
-    parts = [pl.ds(i * block, block) for i in range(in_sems.shape[0])]
+    block = own_ref.shape[1] // sems.shape[0]
+    parts = [pl.ds(i * block, block) for i in range(sems.shape[0])]
     fetches = [
-        pltpu.make_async_copy(other_hbm.at[:, part], other_ref.at[:, part], in_sems.at[i])
+        pltpu.make_async_copy(other_hbm.at[:, part], other_ref.at[:, part], sems.at[i])
         for i, part in enumerate(parts)
     ]
     for fetch in fetches:
         fetch.start()
     turned = basis_ref[...].T
-    sends = []
     for turn, (which, weight_ref) in enumerate(((core, own_ref), (1 - core, other_ref))):
         for i, part in enumerate(parts):
             if turn == 1:
                 fetches[i].wait()
             value = jnp.dot(turned, weight_ref[:, part], preferred_element_type=F32).astype(BF16)
             for j in range(block // size):
-                out_ref[turn, i * (block // size) + j] = value[:, j * size : (j + 1) * size]
-        sends.append(pltpu.make_async_copy(out_ref.at[turn], out_hbm.at[which], out_sems.at[turn]))
-        sends[-1].start()
-    for send in sends:
-        send.wait()
+                out_ref[which, i * (block // size) + j] = value[:, j * size : (j + 1) * size]
+
+
+def spread_kernel(pieces_ref, own_ref, copies_ref):
+    own = jnp.sum(pieces_ref[...].astype(F32), axis=0)
+    own_ref[...] = own
+    value = own.astype(BF16)
+    for i in range(copies_ref.shape[0]):
+        copies_ref[i] = value
 
 
 def total_kernel(parts_ref, out_ref):
@@ -261,13 +259,20 @@
         [pltpu.VMEM((depth, width), BF16), pltpu.SemaphoreType.DMA((4,))],
     )
     pieces = swap(image.reshape(chips, depth // chips, half), ("x", "y"))
-    own = jnp.sum(pieces.astype(F32), axis=0)
-    basis = share(own.astype(BF16), ("x", "y"), chips)
+    own, copies = call(
+        spread_kernel,
+        [shape((depth // chips, half), F32), shape(pieces.shape, BF16)],
+        depth * half,
+        [pieces],
+    )
+    basis = swap(copies, ("x", "y")).reshape(depth, half)
 
     rows_own = depth // experts
     mine = lax.dynamic_slice_in_dim(own, core * rows_own, rows_own, 0)
     other = across(lax.dynamic_slice_in_dim(own, (1 - core) * rows_own, rows_own, 0), "c", nc, 1)
     basis_rows = jnp.where(core == 0, jnp.concatenate([mine, other], 1), jnp.concatenate([other, mine], 1))
+
+    basis, basis_rows = lax.optimization_barrier((basis, basis_rows))
 
     coef_part = call(
         coef_kernel,
@@ -275,13 +280,8 @@
         2 * depth * width * panel,
         [core[None], weight, neighbour, basis],
         [SMEM, VMEM, HBM, VMEM],
-        [HBM],
-        [
-            pltpu.VMEM((depth, width), BF16),
-            pltpu.VMEM((nc, nz, half, block), BF16),
-            pltpu.SemaphoreType.DMA((4,)),
-            pltpu.SemaphoreType.DMA((nc,)),
-        ],
+        None,
+        [pltpu.VMEM((depth, width), BF16), pltpu.SemaphoreType.DMA((4,))],
     )
     arrived = swap(coef_part.reshape(nc * nz, half, block), ("c", "z")).reshape(nc, nz, half, block)
     coefficients = call(total_kernel, [shape((panel, block), F32)], nz * block * panel, [arrived])

time: 176 us -> 175 us (level)
  waiting for transfers between devices: 30.8 us -> 22.4 us
  blocking collectives: 75 us -> 83 us
    all_to_all x2, waiting for transfers between devices: 19.6 us -> 11.3 us  [swap(): return lax.all_to_all(value, axes, split_axis=0, concat_axis=0, tiled=False)]
    all_to_all x4, blocking collectives: 75 us -> 83 us  [swap(): return lax.all_to_all(value, axes, split_axis=0, concat_axis=0, tiled=False)]
    all_to_all x2, starting transfers between devices: 20.2 us -> 16.6 us  [swap(): return lax.all_to_all(value, axes, split_axis=0, concat_axis=0, tiled=False)]
    ppermute x9, starting transfers between devices: 33.5 us -> 36.9 us  [across(): return lax.ppermute(value, axis, [(i, i ^ step) for i in range(size)])]
    pallas_call x7 -> x8, Pallas kernels: 13.8 us -> 13.6 us  [call(): pl.pallas_call(kernel, out_shape=outs, in_specs=in_specs or [VMEM] * len(...]
where the time goes in v8:
time: 175 us; the launch traced here: 174 us
  blocking collectives  83 us (47%)
  starting transfers between devices  53.5 us (31%)
  waiting for transfers between devices  22.4 us (13%)
  Pallas kernels  13.6 us (8%)
    all_to_all x4, blocking collectives, swap(): return lax.all_to_all(value, axes, split_axis=0, concat_axis=0, tiled=False)  83 us
    ppermute x9, starting transfers between devices, across(): return lax.ppermute(value, axis, [(i, i ^ step) for i in range(size)])  36.9 us
    all_to_all x2, starting transfers between devices, swap(): return lax.all_to_all(value, axes, split_axis=0, concat_axis=0, tiled=False)  16.6 us
    pallas_call x8, Pallas kernels, call(): pl.pallas_call(kernel, out_shape=outs, in_specs=in_specs or [VMEM] * len(...  13.6 us
    all_to_all x2, waiting for transfers between devices, swap(): return lax.all_to_all(value, axes, split_axis=0, concat_axis=0, tiled=False)  11.3 us
    ppermute x9, waiting for transfers between devices, across(): return lax.ppermute(value, axis, [(i, i ^ step) for i in range(size)])  11.1 us
  transfers between devices with their start and end apart: 11, of which 6 were waited for; matrix products, arithmetic and copies ran while one was open for 0% of the time, Pallas kernels for 0%

profile of v8, /device:TPU:1, one launch (start us, length us, event | category | flops | bytes accessed | tf_op | source)
XLA Modules:
  0.0 174.3 jit_solution(6467794763300195733)
XLA Ops:
  0.6 3.4 %shard_map.59 = bf16[1024,1024]{1,0:T(8,128)(2,1)} custom-call(s32[8,64]{1,0:T(8,128)} %bitcast.29, bf16[512,1024]{1,0:T(8,128)(2,1)} %bitcast.28), custom_call_target="tpu_custom_call" | custom-call | flops 1073741824 | bytes 3147776 | tf_op jit(solution)/shard_map/pallas_call | solution.py:31
  4.0 0.0 copy-start
  4.0 0.0 copy-start.1
  4.0 12.0 %all-to-all-start = ((bf16[64,16,1024]{2,1,0:T(8,128)(2,1)}), bf16[64,16,1024]{2,1,0:T(8,128)(2,1)}, u32[]{:S(2)}, u32[]{:S(2)}) async-start(bf16[64,16,1024]{2,1,0:T(8,128)(2,1)} %bitcast.26), calls=%async_computation | async-start | bytes 4194304 | tf_op jit(solution)/shard_map/all_to_all | solution.py:21
  16.0 0.0 copy-done
  16.0 2.6 %collective-permute-start = (bf16[896,1024]{1,0:T(8,128)(2,1)S(1)}, bf16[896,1024]{1,0:T(8,128)(2,1)}, u32[]{:S(2)}, u32[]{:S(2)}) collective-permute-start(bf16[896,1024]{1,0:T(8,128)(2,1)S(1)} %bitcast.18), channel_id=1, source_target_pairs={{0,8},{8,0},{1,9},{9,1},{2,10},{10,2},{3,11},{11,3},{4,12},{12,4},... | collective-permute-start | bytes 5505032 | tf_op jit(solution)/shard_map/ppermute | solution.py:194
  18.6 0.0 copy-done.1
  18.6 0.8 shard_map.60
  19.4 7.5 %collective-permute-start.3 = (bf16[256,256]{1,0:T(8,128)(2,1)S(1)}, bf16[256,256]{1,0:T(8,128)(2,1)S(1)}, u32[]{:S(2)}, u32[]{:S(2)}) collective-permute-start(bf16[256,256]{1,0:T(8,128)(2,1)S(1)} %get-tuple-element.21), channel_id=1, source_target_pairs={{0,3},{1,2},{2,1},{3,0},{4,7},{5,6},{6,5},{7,4},{8,11},{9,10},{10,... | collective-permute-start | bytes 393224 | tf_op jit(solution)/shard_map/ppermute | solution.py:194
  26.9 1.9 %collective-permute-start.2 = (bf16[256,256]{1,0:T(8,128)(2,1)S(1)}, bf16[256,256]{1,0:T(8,128)(2,1)S(1)}, u32[]{:S(2)}, u32[]{:S(2)}) collective-permute-start(bf16[256,256]{1,0:T(8,128)(2,1)S(1)} %get-tuple-element.22), channel_id=1, source_target_pairs={{0,2},{1,3},{2,0},{3,1},{4,6},{5,7},{6,4},{7,5},{8,10},{9,11},{10,... | collective-permute-start | bytes 393224 | tf_op jit(solution)/shard_map/ppermute | solution.py:194
  28.8 2.2 %collective-permute-start.1 = (bf16[256,256]{1,0:T(8,128)(2,1)S(1)}, bf16[256,256]{1,0:T(8,128)(2,1)S(1)}, u32[]{:S(2)}, u32[]{:S(2)}) collective-permute-start(bf16[256,256]{1,0:T(8,128)(2,1)S(1)} %get-tuple-element.20), channel_id=1, source_target_pairs={{0,1},{1,0},{2,3},{3,2},{4,5},{5,4},{6,7},{7,6},{8,9},{9,8},{10,11... | collective-permute-start | bytes 393224 | tf_op jit(solution)/shard_map/ppermute | solution.py:194
  31.0 0.0 collective-permute-done.3
  31.0 6.5 %collective-permute-done.2 = bf16[256,256]{1,0:T(8,128)(2,1)S(1)} collective-permute-done((bf16[256,256]{1,0:T(8,128)(2,1)S(1)}, bf16[256,256]{1,0:T(8,128)(2,1)S(1)}, u32[]{:S(2)}, u32[]{:S(2)}) %collective-permute-start.2) | collective-permute-done | bytes 131104 | tf_op jit(solution)/shard_map/ppermute | solution.py:194
  37.5 0.9 collective-permute-done.1
  38.4 0.1 fusion
  38.5 8.0 %collective-permute-start.4 = (bf16[256,256]{1,0:T(8,128)(2,1)S(1)}, bf16[256,256]{1,0:T(8,128)(2,1)S(1)}, u32[]{:S(2)}, u32[]{:S(2)}) collective-permute-start(bf16[256,256]{1,0:T(8,128)(2,1)S(1)} %fusion), channel_id=1, source_target_pairs={{0,4},{1,5},{2,6},{3,7},{4,0},{5,1},{6,2},{7,3},{8,12},{9,13},{10,... | collective-permute-start | bytes 393224 | tf_op jit(solution)/shard_map/ppermute | solution.py:194
  46.5 2.9 %collective-permute-done.4 = bf16[256,256]{1,0:T(8,128)(2,1)S(1)} collective-permute-done((bf16[256,256]{1,0:T(8,128)(2,1)S(1)}, bf16[256,256]{1,0:T(8,128)(2,1)S(1)}, u32[]{:S(2)}, u32[]{:S(2)}) %collective-permute-start.4) | collective-permute-done | bytes 131104 | tf_op jit(solution)/shard_map/ppermute | solution.py:194
  49.4 0.1 add_convert_fusion.proj0
  49.4 4.1 %collective-permute-start.5 = (bf16[256,256]{1,0:T(8,128)(2,1)S(1)}, bf16[256,256]{1,0:T(8,128)(2,1)S(1)}, u32[]{:S(2)}, u32[]{:S(2)}) collective-permute-start(bf16[256,256]{1,0:T(8,128)(2,1)S(1)} %add_convert_fusion.proj0), channel_id=1, source_target_pairs={{0,3},{1,2},{2,1},{3,0},{4,7},{5,6},{6,5},{7,4},{8,11},{9,10},{10,... | collective-permute-start | bytes 393224 | tf_op jit(solution)/shard_map/ppermute | solution.py:194
  53.5 1.9 %collective-permute-start.6 = (bf16[256,256]{1,0:T(8,128)(2,1)S(1)}, bf16[256,256]{1,0:T(8,128)(2,1)S(1)}, u32[]{:S(2)}, u32[]{:S(2)}) collective-permute-start(bf16[256,256]{1,0:T(8,128)(2,1)S(1)} %add_convert_fusion.proj0), channel_id=1, source_target_pairs={{0,2},{1,3},{2,0},{3,1},{4,6},{5,7},{6,4},{7,5},{8,10},{9,11},{10,... | collective-permute-start | bytes 393224 | tf_op jit(solution)/shard_map/ppermute | solution.py:194
  55.5 3.2 %collective-permute-start.7 = (bf16[256,256]{1,0:T(8,128)(2,1)S(1)}, bf16[256,256]{1,0:T(8,128)(2,1)S(1)}, u32[]{:S(2)}, u32[]{:S(2)}) collective-permute-start(bf16[256,256]{1,0:T(8,128)(2,1)S(1)} %add_convert_fusion.proj0), channel_id=1, source_target_pairs={{0,1},{1,0},{2,3},{3,2},{4,5},{5,4},{6,7},{7,6},{8,9},{9,8},{10,11... | collective-permute-start | bytes 393224 | tf_op jit(solution)/shard_map/ppermute | solution.py:194
  58.7 0.0 collective-permute-done.other_hbm
  58.7 8.5 %all-to-all-done = bf16[64,16,1024]{2,1,0:T(8,128)(2,1)} async-done(((bf16[64,16,1024]{2,1,0:T(8,128)(2,1)}), bf16[64,16,1024]{2,1,0:T(8,128)(2,1)}, u32[]{:S(2)}, u32[]{:S(2)}) %all-to-all-start) | async-done | bytes 2097184 | tf_op jit(solution)/shard_map/all_to_all | solution.py:21
  67.3 0.0 collective-permute-done.5.proj3
  67.3 0.0 collective-permute-done.6.proj2
  67.3 0.0 collective-permute-done.7.proj1
  67.3 2.9 %shard_map.61 = bf16[2,8,128,128]{3,2,1,0:T(8,128)(2,1)S(1)} custom-call(s32[1]{0:T(128)} %bitcast.6.quarter_ref, bf16[1024,1024]{1,0:T(8,128)(2,1)} %bitcast.3.rows_ref, bf16[256,256]{1,0:T(8,128)(2,1)S(1)} %collective-permute-done.5.proj3, bf16[256,256]{1,0:T(8,128)(2,1)S(1)} %collective-permute-done.6.proj2, ...), custom_call_target="tpu_custom_call" | custom-call | flops 1073741824 | bytes 3145732 | tf_op jit(solution)/shard_map/pallas_call | solution.py:31
  70.2 25.2 %all_to_all.30 = bf16[16,128,128]{2,1,0:T(8,128)(2,1)S(1)} all-to-all(bf16[16,128,128]{2,1,0:T(8,128)(2,1)S(1)} %bitcast.25), channel_id=1, replica_groups=mesh['x'=4,'y'=8,'c'=2,'z'=8] {'c','z'}, dimensions={0} | all-to-all | bytes 1048576 | tf_op jit(solution)/shard_map/all_to_all | solution.py:21
  95.4 0.2 shard_map.62
  95.6 20.8 %all_to_all.31.gram_ref = bf16[8,2,128,128]{3,2,1,0:T(8,128)(2,1)S(1)} all-to-all(bf16[8,2,128,128]{3,2,1,0:T(8,128)(2,1)S(1)} %shard_map.62), channel_id=1, replica_groups=mesh['x'=4,'y'=8,'c'=2,'z'=8] {'z'}, dimensions={0} | all-to-all | bytes 1048576 | tf_op jit(solution)/shard_map/all_to_all | solution.py:21
  116.3 2.7 %shard_map.63 = bf16[896,128]{1,0:T(8,128)(2,1)S(1)} custom-call(s32[1]{0:T(128)} %bitcast.5.core_ref, bf16[896,1024]{1,0:T(8,128)(2,1)S(1)} %bitcast.20, bf16[896,1024]{1,0:T(8,128)(2,1)} %collective-permute-done.other_hbm, bf16[8,2,128,128]{3,2,1,0:T(8,128)(2,1)S(1)} %all_to_all.31.gram_ref), custom_call_target="tpu_custom_call" | custom-call | flops 469762048 | bytes 4423684 | tf_op jit(solution)/shard_map/pallas_call | solution.py:31
  119.0 14.8 %all_to_all.32.pieces_ref = bf16[32,28,128]{2,1,0:T(8,128)(2,1)S(1)} all-to-all(bf16[32,28,128]{2,1,0:T(8,128)(2,1)S(1)} %reshape.36), channel_id=1, replica_groups=mesh['x'=4,'y'=8,'c'=2,'z'=8] {'x','y'}, dimensions={0} | all-to-all | bytes 458752 | tf_op jit(solution)/shard_map/all_to_all | solution.py:21
  133.9 0.8 shard_map.64
  134.6 4.7 %all-to-all-start.4 = ((bf16[32,28,128]{2,1,0:T(8,128)(2,1)}), bf16[32,28,128]{2,1,0:T(8,128)(2,1)S(1)}, u32[]{:S(2)}, u32[]{:S(2)}) async-start(bf16[32,28,128]{2,1,0:T(8,128)(2,1)} %get-tuple-element.16), calls=%async_computation.4 | async-start | bytes 524288 | tf_op jit(solution)/shard_map/all_to_all | solution.py:21
  139.3 5.4 %collective-permute-start.8 = (f32[14,128]{1,0:T(8,128)S(1)}, f32[14,128]{1,0:T(8,128)S(1)}, u32[]{:S(2)}, u32[]{:S(2)}) collective-permute-start(f32[14,128]{1,0:T(8,128)S(1)} %get-tuple-element.24), channel_id=1, source_target_pairs={{0,8},{8,0},{1,9},{9,1},{2,10},{10,2},{3,11},{11,3},{4,12},{12,4},... | collective-permute-start | bytes 21512 | tf_op jit(solution)/shard_map/ppermute | solution.py:194
  144.8 0.8 collective-permute-done.8
  145.6 0.6 maximum_select_fusion
  146.2 2.8 %all-to-all-done.4 = bf16[32,28,128]{2,1,0:T(8,128)(2,1)S(1)} async-done(((bf16[32,28,128]{2,1,0:T(8,128)(2,1)}), bf16[32,28,128]{2,1,0:T(8,128)(2,1)S(1)}, u32[]{:S(2)}, u32[]{:S(2)}) %all-to-all-start.4) | async-done | bytes 229408 | tf_op jit(solution)/shard_map/all_to_all | solution.py:21
  149.1 2.2 %shard_map.65 = bf16[2,8,128,128]{3,2,1,0:T(8,128)(2,1)S(1)} custom-call(s32[1]{0:T(128)} %bitcast.5.core_ref, bf16[896,1024]{1,0:T(8,128)(2,1)S(1)} %bitcast.21, bf16[896,1024]{1,0:T(8,128)(2,1)} %collective-permute-done.other_hbm, bf16[896,128]{1,0:T(8,128)(2,1)S(1)} %reshape.37.basis_ref), custom_call_target="tpu_custom_call" | custom-call | flops 469762048 | bytes 4423684 | tf_op jit(solution)/shard_map/pallas_call | solution.py:31
  151.3 22.2 %all_to_all.33 = bf16[16,128,128]{2,1,0:T(8,128)(2,1)S(1)} all-to-all(bf16[16,128,128]{2,1,0:T(8,128)(2,1)S(1)} %bitcast.22), channel_id=1, replica_groups=mesh['x'=4,'y'=8,'c'=2,'z'=8] {'c','z'}, dimensions={0} | all-to-all | bytes 1048576 | tf_op jit(solution)/shard_map/all_to_all | solution.py:21
  173.5 0.7 shard_map.66
  (4 shorter events, 0.1 us)
Async XLA Ops:
  4.0 12.0 %copy-start = (bf16[1,896,1024]{2,1,0:T(8,128)(2,1)S(1)}, bf16[1,896,1024]{2,1,0:T(8,128)(2,1)}, u32[]{:S(2)}) copy-start(bf16[1,896,1024]{2,1,0:T(8,128)(2,1)} %param.6) | copy-start | bytes 5505028
  4.0 14.6 %copy-start.1 = (bf16[896,256]{1,0:T(8,128)(2,1)S(1)}, bf16[896,256]{1,0:T(8,128)(2,1)}, u32[]{:S(2)}) copy-start(bf16[896,256]{1,0:T(8,128)(2,1)} %probe_ref.1) | copy-start | bytes 1376260
  4.0 63.2 %all-to-all-start = ((bf16[64,16,1024]{2,1,0:T(8,128)(2,1)}), bf16[64,16,1024]{2,1,0:T(8,128)(2,1)}, u32[]{:S(2)}, u32[]{:S(2)}) async-start(bf16[64,16,1024]{2,1,0:T(8,128)(2,1)} %bitcast.26), calls=%async_computation | async-start | bytes 4194304 | tf_op jit(solution)/shard_map/all_to_all | solution.py:21
  16.0 42.7 %collective-permute-start = (bf16[896,1024]{1,0:T(8,128)(2,1)S(1)}, bf16[896,1024]{1,0:T(8,128)(2,1)}, u32[]{:S(2)}, u32[]{:S(2)}) collective-permute-start(bf16[896,1024]{1,0:T(8,128)(2,1)S(1)} %bitcast.18), channel_id=1, source_target_pairs={{0,8},{8,0},{1,9},{9,1},{2,10},{10,2},{3,11},{11,3},{4,12},{12,4},... | collective-permute-start | bytes 5505032 | tf_op jit(solution)/shard_map/ppermute | solution.py:194
  19.4 11.6 %collective-permute-start.3 = (bf16[256,256]{1,0:T(8,128)(2,1)S(1)}, bf16[256,256]{1,0:T(8,128)(2,1)S(1)}, u32[]{:S(2)}, u32[]{:S(2)}) collective-permute-start(bf16[256,256]{1,0:T(8,128)(2,1)S(1)} %get-tuple-element.21), channel_id=1, source_target_pairs={{0,3},{1,2},{2,1},{3,0},{4,7},{5,6},{6,5},{7,4},{8,11},{9,10},{10,... | collective-permute-start | bytes 393224 | tf_op jit(solution)/shard_map/ppermute | solution.py:194
  26.9 10.6 %collective-permute-start.2 = (bf16[256,256]{1,0:T(8,128)(2,1)S(1)}, bf16[256,256]{1,0:T(8,128)(2,1)S(1)}, u32[]{:S(2)}, u32[]{:S(2)}) collective-permute-start(bf16[256,256]{1,0:T(8,128)(2,1)S(1)} %get-tuple-element.22), channel_id=1, source_target_pairs={{0,2},{1,3},{2,0},{3,1},{4,6},{5,7},{6,4},{7,5},{8,10},{9,11},{10,... | collective-permute-start | bytes 393224 | tf_op jit(solution)/shard_map/ppermute | solution.py:194
  28.8 9.6 %collective-permute-start.1 = (bf16[256,256]{1,0:T(8,128)(2,1)S(1)}, bf16[256,256]{1,0:T(8,128)(2,1)S(1)}, u32[]{:S(2)}, u32[]{:S(2)}) collective-permute-start(bf16[256,256]{1,0:T(8,128)(2,1)S(1)} %get-tuple-element.20), channel_id=1, source_target_pairs={{0,1},{1,0},{2,3},{3,2},{4,5},{5,4},{6,7},{7,6},{8,9},{9,8},{10,11... | collective-permute-start | bytes 393224 | tf_op jit(solution)/shard_map/ppermute | solution.py:194
  38.5 10.9 %collective-permute-start.4 = (bf16[256,256]{1,0:T(8,128)(2,1)S(1)}, bf16[256,256]{1,0:T(8,128)(2,1)S(1)}, u32[]{:S(2)}, u32[]{:S(2)}) collective-permute-start(bf16[256,256]{1,0:T(8,128)(2,1)S(1)} %fusion), channel_id=1, source_target_pairs={{0,4},{1,5},{2,6},{3,7},{4,0},{5,1},{6,2},{7,3},{8,12},{9,13},{10,... | collective-permute-start | bytes 393224 | tf_op jit(solution)/shard_map/ppermute | solution.py:194
  49.4 17.8 %collective-permute-start.5 = (bf16[256,256]{1,0:T(8,128)(2,1)S(1)}, bf16[256,256]{1,0:T(8,128)(2,1)S(1)}, u32[]{:S(2)}, u32[]{:S(2)}) collective-permute-start(bf16[256,256]{1,0:T(8,128)(2,1)S(1)} %add_convert_fusion.proj0), channel_id=1, source_target_pairs={{0,3},{1,2},{2,1},{3,0},{4,7},{5,6},{6,5},{7,4},{8,11},{9,10},{10,... | collective-permute-start | bytes 393224 | tf_op jit(solution)/shard_map/ppermute | solution.py:194
  53.5 13.7 %collective-permute-start.6 = (bf16[256,256]{1,0:T(8,128)(2,1)S(1)}, bf16[256,256]{1,0:T(8,128)(2,1)S(1)}, u32[]{:S(2)}, u32[]{:S(2)}) collective-permute-start(bf16[256,256]{1,0:T(8,128)(2,1)S(1)} %add_convert_fusion.proj0), channel_id=1, source_target_pairs={{0,2},{1,3},{2,0},{3,1},{4,6},{5,7},{6,4},{7,5},{8,10},{9,11},{10,... | collective-permute-start | bytes 393224 | tf_op jit(solution)/shard_map/ppermute | solution.py:194
  55.5 11.8 %collective-permute-start.7 = (bf16[256,256]{1,0:T(8,128)(2,1)S(1)}, bf16[256,256]{1,0:T(8,128)(2,1)S(1)}, u32[]{:S(2)}, u32[]{:S(2)}) collective-permute-start(bf16[256,256]{1,0:T(8,128)(2,1)S(1)} %add_convert_fusion.proj0), channel_id=1, source_target_pairs={{0,1},{1,0},{2,3},{3,2},{4,5},{5,4},{6,7},{7,6},{8,9},{9,8},{10,11... | collective-permute-start | bytes 393224 | tf_op jit(solution)/shard_map/ppermute | solution.py:194
  134.6 14.4 %all-to-all-start.4 = ((bf16[32,28,128]{2,1,0:T(8,128)(2,1)}), bf16[32,28,128]{2,1,0:T(8,128)(2,1)S(1)}, u32[]{:S(2)}, u32[]{:S(2)}) async-start(bf16[32,28,128]{2,1,0:T(8,128)(2,1)} %get-tuple-element.16), calls=%async_computation.4 | async-start | bytes 524288 | tf_op jit(solution)/shard_map/all_to_all | solution.py:21
  139.3 6.3 %collective-permute-start.8 = (f32[14,128]{1,0:T(8,128)S(1)}, f32[14,128]{1,0:T(8,128)S(1)}, u32[]{:S(2)}, u32[]{:S(2)}) collective-permute-start(f32[14,128]{1,0:T(8,128)S(1)} %get-tuple-element.24), channel_id=1, source_target_pairs={{0,8},{8,0},{1,9},{9,1},{2,10},{10,2},{3,11},{11,3},{4,12},{12,4},... | collective-permute-start | bytes 21512 | tf_op jit(solution)/shard_map/ppermute | solution.py:194
